TPU v7x, 32 devices: a whole 2x2x4 slice. The times are simulated.
32 devices in a mesh: dp: 2 (over x), row: 4 (over z), col: 4 (over y, core).
Axes of the slice: x: 2, y: 2, z: 4, core: 2. Of those that a mesh axis runs over, the one named last changes fastest.
Arguments:
- block_input: bfloat16 [8192, 2048], P(('dp', 'row'), 'col'), may hold values from -6 to 6
- cotangent: bfloat16 [8192, 2048], P(('dp', 'row'), 'col'), may hold values from -6 to 6
- doc_lengths: int32 [4, 4], P('dp'), may hold values from 1 to 1280, 2048 in all within a row
- layernorm_gain: float32 [2048], P('col'), may hold values from 0.5 to 1.5
- layernorm_bias: float32 [2048], P('col'), may hold values from -2 to 2
- qkv_weight: bfloat16 [3, 2048, 2048], P(None, 'row', 'col'), may hold values from -0.125 to 0.125
- qkv_bias: float32 [3, 2048], P(None, ('row', 'col')), may hold values from -2 to 2
- fc1_weight: bfloat16 [8192, 2048], P('row', 'col'), may hold values from -0.125 to 0.125
- fc1_bias: float32 [8192], P(('row', 'col')), may hold values from -2 to 2
- dense_weight: bfloat16 [2048, 2048], P('col', 'row'), may hold values from -0.375 to 0.375
- fc2_weight: bfloat16 [2048, 8192], P('col', 'row'), may hold values from -0.0625 to 0.0625
- out_bias: float32 [2048], P('col'), may hold values from -2 to 2
Outputs:
- block_output: bfloat16 [8192, 2048], P(('dp', 'row'), 'col')
- input_grad: float32 [8192, 2048], P(('dp', 'row'), 'col')
- ln_gain_grad: float32 [2048], P('col')
- ln_bias_grad: float32 [2048], P('col')
- qkv_weight_grad: float32 [3, 2048, 2048], P(None, 'row', 'col')
- qkv_bias_grad: float32 [3, 2048], P(None, ('row', 'col'))
- fc1_weight_grad: float32 [8192, 2048], P('row', 'col')
- fc1_bias_grad: float32 [8192], P(('row', 'col'))
- dense_weight_grad: float32 [2048, 2048], P('col', 'row')
- fc2_weight_grad: float32 [2048, 8192], P('col', 'row')
- out_bias_grad: float32 [2048], P('col')
Inputs may be any that keep to these rules, and one draw needn't show every extreme that they name: `doc_lengths`: each row gives the 4 document lengths of one sequence in order; they sum to 2048, and the largest of each row is exactly 1280.
All inputs are finite; a program needn't handle non-finite values.
Results may differ from a plain program's by a relative error of at most 0.018.
Values may be sent and summed in bfloat16 or wider, within the bound.
No kernel may reach another device: no remote copies, remote signals or barrier semaphores. Data moves between devices by JAX's collectives and lax.ppermute only.
A program may use at most 256 MiB of HBM per device.

v0:
```python
import math

import jax
import jax.numpy as jnp
from jax import lax
from jax.sharding import PartitionSpec as P

MODEL_WIDTH = 2048
HEAD_DIM = 64
ROT = 32
SEQ = 2048


EPSILON = 1e-05
MASKED = -1e30


def matmul(left, right):
    return jnp.dot(left, right, preferred_element_type=jnp.float32)


def times_transpose(left, right):
    return lax.dot_general(
        left, right, (((1,), (1,)), ((), ())), preferred_element_type=jnp.float32
    )


def contract_rows(left, right):
    return lax.dot_general(
        left, right, (((0,), (0,)), ((), ())), preferred_element_type=jnp.float32
    )


def segment_ids(doc_lengths):
    ends = jnp.cumsum(doc_lengths, axis=1)
    place = jnp.arange(SEQ, dtype=jnp.int32)
    return jnp.sum((place[None, :, None] >= ends[:, None, :]).astype(jnp.int32), axis=2)


def rotary_tables(count):
    place = (jnp.arange(count, dtype=jnp.int32) % SEQ).astype(jnp.float32)
    freqs = jnp.exp(jnp.arange(ROT // 2, dtype=jnp.float32) * (-2.0 * math.log(10000.0) / ROT))
    angle = place[:, None] * freqs[None, :]
    return (jnp.cos(angle)[:, None, :], jnp.sin(angle)[:, None, :])


def rotate(values, cosine, sine):
    half = ROT // 2
    first = values[..., :half]
    second = values[..., half:ROT]
    return jnp.concatenate(
        [first * cosine - second * sine, second * cosine + first * sine, values[..., ROT:]], axis=-1
    )


def to_items(values, heads_here):
    count = values.shape[0] // SEQ
    return (
        values.reshape(count, SEQ, heads_here, HEAD_DIM)
        .transpose(0, 2, 1, 3)
        .reshape(count * heads_here, SEQ, HEAD_DIM)
    )


def from_items(values, heads_here):
    count = values.shape[0] // heads_here
    return (
        values.reshape(count, heads_here, SEQ, HEAD_DIM)
        .transpose(0, 2, 1, 3)
        .reshape(count * SEQ, heads_here * HEAD_DIM)
    )


def allowed_mask(segment):
    place = jnp.arange(SEQ, dtype=jnp.int32)
    return (place[:, None] >= place[None, :]) & (segment[:, None] == segment[None, :])


def attend_forward(item):
    query, keys, values, segment = item
    scores = jnp.where(
        allowed_mask(segment), times_transpose(query, keys) * HEAD_DIM ** (-0.5), MASKED
    )
    peak = jnp.max(scores, axis=1, keepdims=True)
    exponent = jnp.exp(scores - peak)
    total = jnp.sum(exponent, axis=1, keepdims=True)
    probs = (exponent / total).astype(jnp.bfloat16)
    return (matmul(probs, values).astype(jnp.bfloat16), (peak + jnp.log(total))[:, 0])


def attend_backward(item):
    query, keys, values, segment, log_total, d_out = item
    scale = HEAD_DIM ** (-0.5)
    scores = jnp.where(allowed_mask(segment), times_transpose(query, keys) * scale, MASKED)
    probs = jnp.exp(scores - log_total[:, None])
    d_probs = times_transpose(d_out, values)
    delta = jnp.sum(probs * d_probs, axis=1, keepdims=True)
    d_scores = (probs * (d_probs - delta)).astype(jnp.bfloat16)
    d_query = matmul(d_scores, keys) * scale
    d_keys = contract_rows(d_scores, query) * scale
    d_values = contract_rows(probs.astype(jnp.bfloat16), d_out)
    return (d_query, d_keys, d_values)


def gelu_tanh(inner):
    return jax.nn.gelu(inner, approximate=True)


def on_device(
    block_input,
    cotangent,
    doc_lengths,
    layernorm_gain,
    layernorm_bias,
    qkv_weight,
    qkv_bias,
    fc1_weight,
    fc1_bias,
    dense_weight,
    fc2_weight,
    out_bias,
):
    rows_local, cols_local = block_input.shape
    n_col = lax.axis_size("col")
    qkv_local = qkv_weight.shape[1] // n_col
    ff_local = fc1_weight.shape[0] // n_col
    width_in = 3 * qkv_local + ff_local
    heads_here = qkv_local // HEAD_DIM
    input_single = block_input.astype(jnp.float32)
    feature_sum, square_sum = lax.psum(
        (jnp.sum(input_single, axis=1), jnp.sum(input_single * input_single, axis=1)), "col"
    )
    row_average = feature_sum / MODEL_WIDTH
    inverse_deviation = lax.rsqrt(square_sum / MODEL_WIDTH - row_average * row_average + EPSILON)
    centered_input = (input_single - row_average[:, None]) * inverse_deviation[:, None]
    normed_output = (centered_input * layernorm_gain + layernorm_bias).astype(jnp.bfloat16)
    normed_rows = lax.all_gather(normed_output, "row", axis=0, tiled=True)
    group_rows = normed_rows.shape[0]
    qkv_blocks = jnp.transpose(qkv_weight.reshape(3, n_col, qkv_local, cols_local), (1, 0, 2, 3))
    in_weight = jnp.concatenate(
        [
            qkv_blocks.reshape(n_col, 3 * qkv_local, cols_local),
            fc1_weight.reshape(n_col, ff_local, cols_local),
        ],
        axis=1,
    )
    flat_weight = in_weight.reshape(n_col * width_in, cols_local)
    own_sums = jnp.transpose(
        lax.psum_scatter(
            times_transpose(flat_weight, normed_rows), "col", scatter_dimension=0, tiled=True
        )
    )
    own_sums = own_sums + jnp.concatenate([qkv_bias.reshape(-1), fc1_bias])
    cosine, sine = rotary_tables(group_rows)
    query = rotate(
        own_sums[:, :qkv_local].reshape(group_rows, heads_here, HEAD_DIM), cosine, sine
    ).astype(jnp.bfloat16)
    keys = rotate(
        own_sums[:, qkv_local : 2 * qkv_local].reshape(group_rows, heads_here, HEAD_DIM),
        cosine,
        sine,
    ).astype(jnp.bfloat16)
    values = (
        own_sums[:, 2 * qkv_local : 3 * qkv_local]
        .reshape(group_rows, heads_here, HEAD_DIM)
        .astype(jnp.bfloat16)
    )
    fc_pre = own_sums[:, 3 * qkv_local :]
    seg_items = jnp.repeat(segment_ids(doc_lengths), heads_here, axis=0)
    query_items = to_items(query, heads_here)
    keys_items = to_items(keys, heads_here)
    values_items = to_items(values, heads_here)
    attended_items, log_totals = lax.map(
        attend_forward, (query_items, keys_items, values_items, seg_items)
    )
    attended = from_items(attended_items, heads_here)
    activated = gelu_tanh(fc_pre).astype(jnp.bfloat16)
    attended_rows, activated_rows = (
        lax.all_gather(attended, "col", axis=1, tiled=True),
        lax.all_gather(activated, "col", axis=1, tiled=True),
    )
    head_part = attended_rows
    unit_part = activated_rows
    branch = (
        lax.psum_scatter(
            (
                times_transpose(head_part, dense_weight) + times_transpose(unit_part, fc2_weight)
            ).astype(jnp.bfloat16),
            "row",
            scatter_dimension=0,
            tiled=True,
        ).astype(jnp.float32)
        + out_bias
    )
    result = (input_single + branch).astype(jnp.bfloat16)
    branch_gradient = cotangent.astype(jnp.float32)
    piece = lax.all_gather(cotangent, "row", axis=0, tiled=True)
    head_part = attended_rows
    unit_part = activated_rows
    grad_dense = contract_rows(piece, head_part)
    grad_fc2 = contract_rows(piece, unit_part)
    d_attended_part = matmul(piece, dense_weight)
    d_activated_part = matmul(piece, fc2_weight)
    grad_dense, grad_fc2, d_attended_part, d_activated_part = (
        grad_dense,
        grad_fc2,
        d_attended_part,
        d_activated_part,
    )
    d_attended, d_activated = (
        lax.psum_scatter(
            d_attended_part.reshape(group_rows, n_col, qkv_local).astype(jnp.bfloat16),
            "col",
            scatter_dimension=1,
            tiled=True,
        ).astype(jnp.float32),
        lax.psum_scatter(
            d_activated_part.reshape(group_rows, n_col, ff_local).astype(jnp.bfloat16),
            "col",
            scatter_dimension=1,
            tiled=True,
        ).astype(jnp.float32),
    )
    d_attended = d_attended[:, 0].astype(jnp.bfloat16)
    d_activated = d_activated[:, 0]
    gelu_pull = jax.vjp(gelu_tanh, fc_pre)[1]
    d_fc = gelu_pull(d_activated)[0].astype(jnp.bfloat16)
    d_items = to_items(d_attended.reshape(group_rows, heads_here, HEAD_DIM), heads_here)
    d_query_items, d_keys_items, d_values_items = lax.map(
        attend_backward, (query_items, keys_items, values_items, seg_items, log_totals, d_items)
    )
    d_query = rotate(
        from_items(d_query_items, heads_here).reshape(group_rows, heads_here, HEAD_DIM),
        cosine,
        -sine,
    )
    d_keys = rotate(
        from_items(d_keys_items, heads_here).reshape(group_rows, heads_here, HEAD_DIM),
        cosine,
        -sine,
    )
    d_values = from_items(d_values_items, heads_here)
    d_inputs = jnp.concatenate(
        [
            d_query.reshape(group_rows, qkv_local),
            d_keys.reshape(group_rows, qkv_local),
            d_values,
            d_fc.astype(jnp.float32),
        ],
        axis=1,
    ).astype(jnp.bfloat16)
    bias_sums = jnp.sum(d_inputs.astype(jnp.float32), axis=0)
    d_gathered = lax.all_gather(d_inputs, "col", axis=1, tiled=True)
    grad_in = contract_rows(d_gathered, normed_rows).reshape(n_col, width_in, cols_local)
    grad_qkv = jnp.transpose(
        grad_in[:, : 3 * qkv_local].reshape(n_col, 3, qkv_local, cols_local), (1, 0, 2, 3)
    ).reshape(3, n_col * qkv_local, cols_local)
    grad_fc1 = grad_in[:, 3 * qkv_local :].reshape(n_col * ff_local, cols_local)
    normed_gradient = lax.psum_scatter(
        matmul(d_gathered, flat_weight).astype(jnp.bfloat16), "row", scatter_dimension=0, tiled=True
    ).astype(jnp.float32)
    centered_gradient = normed_gradient * layernorm_gain
    centered_gradient_sum, product_sum = lax.psum(
        (jnp.sum(centered_gradient, axis=1), jnp.sum(centered_gradient * centered_input, axis=1)),
        "col",
    )
    input_grad = branch_gradient + inverse_deviation[:, None] * (
        centered_gradient
        - centered_gradient_sum[:, None] / MODEL_WIDTH
        - centered_input * (product_sum[:, None] / MODEL_WIDTH)
    )
    gain_grad, shift_grad, bias_out_grad = lax.psum(
        (
            jnp.sum(normed_gradient * centered_input, axis=0),
            jnp.sum(normed_gradient, axis=0),
            jnp.sum(branch_gradient, axis=0),
        ),
        ("dp", "row"),
    )
    grad_qkv, grad_fc1, grad_dense, grad_fc2, qkv_bias_sum, fc1_bias_sum = (
        lax.psum(grad_qkv.astype(jnp.bfloat16), "dp").astype(jnp.float32),
        lax.psum(grad_fc1.astype(jnp.bfloat16), "dp").astype(jnp.float32),
        lax.psum(grad_dense.astype(jnp.bfloat16), "dp").astype(jnp.float32),
        lax.psum(grad_fc2.astype(jnp.bfloat16), "dp").astype(jnp.float32),
        lax.psum(
            bias_sums[: 3 * qkv_local].reshape(3, qkv_local).astype(jnp.bfloat16), "dp"
        ).astype(jnp.float32),
        lax.psum(bias_sums[3 * qkv_local :].astype(jnp.bfloat16), "dp").astype(jnp.float32),
    )
    return (
        result,
        input_grad,
        gain_grad,
        shift_grad,
        grad_qkv,
        qkv_bias_sum,
        grad_fc1,
        fc1_bias_sum,
        grad_dense,
        grad_fc2,
        bias_out_grad,
    )


def solution(mesh):
    return jax.shard_map(
        on_device,
        mesh=mesh,
        in_specs=(
            P(("dp", "row"), "col"),
            P(("dp", "row"), "col"),
            P("dp", None),
            P("col"),
            P("col"),
            P(None, "row", "col"),
            P(None, ("row", "col")),
            P("row", "col"),
            P(("row", "col")),
            P("col", "row"),
            P("col", "row"),
            P("col"),
        ),
        out_specs=(
            P(("dp", "row"), "col"),
            P(("dp", "row"), "col"),
            P("col"),
            P("col"),
            P(None, "row", "col"),
            P(None, ("row", "col")),
            P("row", "col"),
            P(("row", "col")),
            P("col", "row"),
            P("col", "row"),
            P("col"),
        ),
        check_vma=False,
    )
```

profile of v0, /device:TPU:8, one launch (start us, length us, event | category | flops | bytes accessed | tf_op | source)
XLA Modules:
  0.0 1522.9 jit_solution(4624291286380232513)
XLA Ops:
  24.2 73.6 %all-gather.6.cloned.1.call-done = bf16[4096,512]{1,0:T(8,128)(2,1)} async-done(((bf16[1024,512]{1,0:T(8,128)(2,1)}), bf16[4096,512]{1,0:T(8,128)(2,1)}) %all-gather.6.cloned.1.call-update) | async-done | bytes 4194320 | tf_op jit(solution)/shard_map/all_gather | solution.py:137
  97.8 28.2 %fusion.81 = f32[3584,4096]{1,0:T(8,128)} fusion(bf16[3584,512]{1,0:T(8,128)(2,1)} %bitcast.221, bf16[4096,512]{1,0:T(8,128)(2,1)} %all-gather.6.cloned.1.call-done), kind=kOutput, calls=%fused_computation.145 | convolution fusion | flops 15032385536 | bytes 66584576 | tf_op jit(solution)/shard_map/dot_general | solution.py:23
  126.1 52.6 %all-gather.12.cloned.1.call-done = bf16[4096,512]{1,0:T(8,128)(2,1)} async-done(((bf16[1024,512]{1,0:T(8,128)(2,1)}), bf16[4096,512]{1,0:T(8,128)(2,1)}) %all-gather.12.cloned.1.call-update) | async-done | bytes 4194320 | tf_op jit(solution)/shard_map/all_gather | solution.py:197
  185.9 16.8 %convolution_convert_fusion = bf16[4096,2048]{0,1:T(8,128)(2,1)} fusion(bf16[4096,512]{1,0:T(8,128)(2,1)} %all-gather.12.cloned.1.call-done, bf16[512,2048]{1,0:T(8,128)(2,1)S(1)} %copy-done), kind=kOutput, calls=%fused_computation.57 | convolution fusion | flops 8598323200 | bytes 23068672 | tf_op jit(solution)/shard_map/dot_general | solution.py:19
  205.6 374.7 %reduce-scatter.6.cloned.1.call-done = f32[896,4096]{1,0:T(8,128)} async-done(((f32[3584,4096]{1,0:T(8,128)}), f32[896,4096]{1,0:T(8,128)}) %reduce-scatter.6.cloned.1.call-update) | async-done | bytes 14680080 | tf_op jit(solution)/shard_map/reduce_scatter | solution.py:149
  580.3 14.9 add_bitcast_fusion
  636.4 119.1 %while.26 = (s32[]{:T(128)}, bf16[4,2048,64]{1,2,0:T(8,128)(2,1)S(1)}, f32[4,2048]{1,0:T(4,128)}, s32[4,2048]{1,0:T(4,128)S(1)}, bf16[4,2048,64]{2,1,0:T(8,128)(...) while((s32[]{:T(128)}, ...), condition=%wide.region_10.11_spmd, body=%wide.region_7.10_spmd.sunk | while | flops 1120008192 | bytes 52283500 | solution.py:173
  636.6 13.2 fusion.120
  649.8 10.3 fusion.121
  660.1 9.5 fusion.122
  671.1 9.5 fusion.120
  699.3 9.5 fusion.120
  727.5 9.5 fusion.120
  762.4 11.4 fusion.49
  773.8 193.6 %while.27 = (s32[]{:T(128)}, f32[4,2048,64]{1,2,0:T(8,128)}, f32[4,2048,64]{1,2,0:T(8,128)}, bf16[4,2048,64]{1,2,0:T(8,128)(2,1)}, s32[4,2048]{1,0:T(4,128)S(1)}...) while((s32[]{:T(128)}, f32[4,2048,64]{1,2,0:T(8,128)}, ...), condition=%wide.region_15.16_spmd, body=%wide.region_13.15_spmd.sunk | while | flops 2734946304 | bytes 168899792 | solution.py:229
  774.1 9.4 fusion.131
  784.9 13.2 multiply_reduce_fusion.2
  824.7 9.4 fusion.131
  835.5 13.3 multiply_reduce_fusion.2
  872.2 9.4 fusion.131
  883.0 13.2 multiply_reduce_fusion.2
  919.6 9.4 fusion.131
  930.4 13.2 multiply_reduce_fusion.2
  984.4 17.7 %fusion.60 = bf16[512,2048]{0,1:T(8,128)(2,1)} fusion(bf16[4096,2048]{0,1:T(8,128)(2,1)} %all-gather.10.cloned.1.call-done, bf16[4096,512]{1,0:T(8,128)(2,1)} %all-gather.12.cloned.1.call-done), kind=kOutput, calls=%fused_computation.91 | convolution fusion | flops 8590983168 | bytes 23068672 | tf_op jit(solution)/shard_map/dot_general | solution.py:29
  1002.0 154.4 %all-gather.14.cloned.1.call-done = bf16[4096,3584]{0,1:T(8,128)(2,1)} async-done(((bf16[4096,896]{0,1:T(8,128)(2,1)}), bf16[4096,3584]{0,1:T(8,128)(2,1)}) %all-gather.14.cloned.1.call-update) | async-done | bytes 29360144 | tf_op jit(solution)/shard_map/all_gather | solution.py:253
  1156.4 20.8 %convolution_convert_fusion.1 = bf16[3584,512]{1,0:T(8,128)(2,1)S(1)} fusion(bf16[4096,3584]{0,1:T(8,128)(2,1)} %all-gather.14.cloned.1.call-done, bf16[4096,512]{1,0:T(8,128)(2,1)} %all-gather.6.cloned.1.call-done), kind=kOutput, calls=%fused_computation.76 | convolution fusion | flops 15034220544 | bytes 37224448 | tf_op jit(solution)/shard_map/dot_general | solution.py:29
  1180.2 23.9 %convolution_convert_fusion.2 = bf16[4096,512]{1,0:T(8,128)(2,1)} fusion(bf16[4096,3584]{0,1:T(8,128)(2,1)} %all-gather.14.cloned.1.call-done, bf16[3584,512]{1,0:T(8,128)(2,1)} %bitcast.222), kind=kOutput, calls=%fused_computation.77 | convolution fusion | flops 15034482688 | bytes 37224448 | tf_op jit(solution)/shard_map/dot_general | solution.py:19
  1210.1 14.1 add_convert_fusion
  1230.4 104.2 %all-reduce.7.cloned.1.call-done = (bf16[512,512]{0,1:T(8,128)(2,1)}, bf16[512,2048]{0,1:T(8,128)(2,1)}, bf16[3,512,512]{2,1,0:T(8,128)(2,1)}, bf16[2048,512]{1,0:T(8,128)(2,1)}) async-done(((bf16[512,512]{0,1:T(8,128)(2,1)}, bf16[512,2048]{0,1:T(8,128)(2,1)}, bf16[3,512,512]{2,1,0:T(8,128)(2,1)}, bf16[2048,512]{1,0:T(8,128)(2,1)}), (bf16[512,512]{0,1:T(8,128)(2,1)}, bf16[512,2048]{0,1:T(8,128)(2,1)}, ...) | async-done | bytes 6291472 | tf_op jit(solution)/shard_map/psum | solution.py:283
  1347.5 66.1 %reduce-scatter.14.cloned.1.call-done = bf16[1024,512]{1,0:T(8,128)(2,1)} async-done(((bf16[4096,512]{1,0:T(8,128)(2,1)}), bf16[1024,512]{1,0:T(8,128)(2,1)}) %reduce-scatter.14.cloned.1.call-update) | async-done | bytes 1048592 | tf_op jit(solution)/shard_map/reduce_scatter | solution.py:259
  1423.1 70.2 %reduce-scatter.8.cloned.1.call-done = bf16[1024,512]{1,0:T(8,128)(2,1)} async-done(((bf16[4096,512]{1,0:T(8,128)(2,1)}), bf16[1024,512]{1,0:T(8,128)(2,1)}) %reduce-scatter.8.cloned.1.call-update) | async-done | bytes 1048592 | tf_op jit(solution)/shard_map/reduce_scatter | solution.py:185
  1497.0 19.1 %all-reduce = (f32[512]{0:T(512)}, f32[512]{0:T(512)}, f32[512]{0:T(512)}) all-reduce(f32[512]{0:T(512)S(1)} %get-tuple-element.141, f32[512]{0:T(512)S(1)} %get-tuple-element.144, f32[512]{0:T(512)S(1)} %get-tuple-element.212), channel_id=1, replica_groups=mesh['dp'=2,'row'=4,'col'=4] {'dp','row'}, use_global_device_ids=true, to_apply=%region_23.24 | all-reduce | flops 1536 | bytes 12288 | tf_op jit(solution)/shard_map/psum | solution.py:272
  (209 shorter events, 292.6 us)
Async XLA Ops:
  7.2 178.7 %copy-start = (bf16[512,2048]{1,0:T(8,128)(2,1)S(1)}, bf16[512,2048]{1,0:T(8,128)(2,1)}, u32[]{:S(2)}) copy-start(bf16[512,2048]{1,0:T(8,128)(2,1)} %param.26) | copy-start | bytes 6291460
  7.2 90.6 %all-gather.6.cloned.1.call-start = ((), (), s32[]{:S(2)}) async-start(), calls=%async_computation.5 | async-start | bytes 5242880 | tf_op jit(solution)/shard_map/all_gather | solution.py:137
  19.4 159.4 %all-gather.12.cloned.1.call-start = ((), (), s32[]{:S(2)}) async-start(), calls=%async_computation.10 | async-start | bytes 5242880 | tf_op jit(solution)/shard_map/all_gather | solution.py:197
  20.1 560.2 %reduce-scatter.6.cloned.1.call-start = ((), (), s32[]{:S(2)}) async-start(), calls=%async_computation.6 | async-start | bytes 73400320 | tf_op jit(solution)/shard_map/reduce_scatter | solution.py:149
  126.0 52.7 %copy-start.17 = (bf16[512,512]{1,0:T(8,128)(2,1)S(1)}, bf16[512,512]{1,0:T(8,128)(2,1)}, u32[]{:S(2)}) copy-start(bf16[512,512]{1,0:T(8,128)(2,1)} %param.25) | copy-start | bytes 1572868
  126.1 632.0 %reduce-scatter.10.cloned.1.call-start = ((), (), s32[]{:S(2)}) async-start(), calls=%async_computation.11 | async-start | bytes 5242880 | tf_op jit(solution)/shard_map/reduce_scatter | solution.py:211
  185.3 577.1 %reduce-scatter.12.cloned.1.call-start = ((), (), s32[]{:S(2)}) async-start(), calls=%async_computation.12 | async-start | bytes 20971520 | tf_op jit(solution)/shard_map/reduce_scatter | solution.py:217
  202.7 775.0 %all-gather.8.cloned.1.call-start = ((), (), s32[]{:S(2)}) async-start(), calls=%async_computation.7 | async-start | bytes 5242880 | tf_op jit(solution)/shard_map/all_gather | solution.py:179
  205.6 401.6 %copy-start.9 = (f32[4096,16]{0,1:T(8,128)}, f32[4096,16]{0,1:T(8,128)S(1)}, u32[]{:S(2)}) copy-start(f32[4096,16]{0,1:T(8,128)S(1)} %get-tuple-element.221) | copy-start | bytes 786436
  626.8 6.4 copy-start.5
  626.8 6.4 copy-start.6
  626.8 6.4 copy-start.7
  633.2 3.2 copy-start.16
  757.9 226.4 %all-gather.10.cloned.1.call-start = ((), (), s32[]{:S(2)}) async-start(), calls=%async_computation.8 | async-start | bytes 20971520 | tf_op jit(solution)/shard_map/all_gather | solution.py:180
  773.8 382.6 %all-gather.14.cloned.1.call-start = ((), (), s32[]{:S(2)}) async-start(), calls=%async_computation.13 | async-start | bytes 36700160 | tf_op jit(solution)/shard_map/all_gather | solution.py:253
  774.1 10.8 copy-start.4
  807.5 5.1 copy-start.1
  824.7 10.8 copy-start.4
  857.0 3.9 copy-start.1
  872.2 10.8 copy-start.4
  904.5 3.9 copy-start.1
  919.6 10.8 copy-start.4
  951.9 3.9 copy-start.1
  977.7 356.9 %all-reduce.7.cloned.1.call-start = ((), (), s32[]{:S(2)}) async-start(), calls=%async_computation.15 | async-start | bytes 12582912 | tf_op jit(solution)/shard_map/psum | solution.py:283
  1180.1 233.4 %reduce-scatter.14.cloned.1.call-start = ((), (), s32[]{:S(2)}) async-start(), calls=%async_computation.14 | async-start | bytes 5242880 | tf_op jit(solution)/shard_map/reduce_scatter | solution.py:259
  1204.1 289.2 %reduce-scatter.8.cloned.1.call-start = ((), (), s32[]{:S(2)}) async-start(), calls=%async_computation.9 | async-start | bytes 5242880 | tf_op jit(solution)/shard_map/reduce_scatter | solution.py:185
  1334.6 3.7 copy-start.12
  1340.9 72.7 %copy-start.3 = (bf16[1024,512]{1,0:T(8,128)(2,1)S(1)}, bf16[1024,512]{1,0:T(8,128)(2,1)}, u32[]{:S(2)}) copy-start(bf16[1024,512]{1,0:T(8,128)(2,1)} %param.16) | copy-start | bytes 3145732
  1340.9 72.7 %copy-start.20 = (f32[1024]{0:T(1024)S(1)}, f32[1024]{0:T(1024)}, u32[]{:S(2)}) copy-start(f32[1024]{0:T(1024)} %copy-done.19) | copy-start | bytes 12292
  1340.9 72.7 %copy-start.22 = (f32[1024]{0:T(1024)S(1)}, f32[1024]{0:T(1024)}, u32[]{:S(2)}) copy-start(f32[1024]{0:T(1024)} %copy-done.21) | copy-start | bytes 12292
  1340.9 72.7 %copy-start.23 = (f32[512]{0:T(512)S(1)}, f32[512]{0:T(512)}, u32[]{:S(2)}) copy-start(f32[512]{0:T(512)} %param.19) | copy-start | bytes 6148
  1343.2 150.1 %copy-start.26 = (f32[512]{0:T(512)S(1)}, f32[512]{0:T(512)}, u32[]{:S(2)}) copy-start(f32[512]{0:T(512)} %param.27) | copy-start | bytes 6148
  (13 other events, 17.6 us)
Sparse Core Ops, SparseCore 0:
  19.5 78.3 all-gather.5
  99.4 79.2 all-gather.11
  181.3 398.8 reduce-scatter.5
  583.4 44.5 reduce-scatter.9
  630.4 126.1 reduce-scatter.11
  758.6 34.4 all-gather.7
  795.3 105.9 all-gather.9
  977.8 178.5 all-gather.13
  1180.3 154.3 all-reduce.6
  1336.8 76.7 reduce-scatter.13
  1416.0 77.2 reduce-scatter.7
where the time goes:
time: 1540 us; the launch traced here: 1520 us
  waiting for transfers between devices  897 us (58%)
  matrix products  370 us (24%)
  other arithmetic  134 us (9%)
  local copies, waits for them, and re-layouts  67.8 us (4%)
  blocking collectives  38.2 us (2%)
    reduce_scatter x1, waiting for transfers between devices, on_device(): lax.psum_scatter(times_transpose(flat_weight, normed_rows), 'col', scatte...  375 us
    dot_general x15, matrix products, times_transpose(): lax.dot_general(left, right, (((1,), (1,)), ((), ())), preferred_element_...  180 us
    all_gather x1, waiting for transfers between devices, on_device(): d_gathered = lax.all_gather(d_inputs, 'col', axis=1, tiled=True)  154 us
    psum x1, waiting for transfers between devices, on_device(): lax.psum(grad_dense.astype(jnp.bfloat16), 'dp').astype(jnp.float32)  104 us
    dot_general x11, matrix products, matmul(): return jnp.dot(left, right, preferred_element_type=jnp.float32)  99.2 us
    dot_general x11, matrix products, contract_rows(): lax.dot_general(left, right, (((0,), (0,)), ((), ())), preferred_element_...  90.9 us
    all_gather x1, waiting for transfers between devices, on_device(): normed_rows = lax.all_gather(normed_output, 'row', axis=0, tiled=True)  73.6 us
    reduce_scatter x1, waiting for transfers between devices, on_device(): lax.psum_scatter((times_transpose(head_part, dense_weight) + times_transp...  70.2 us
  transfers between devices with their start and end apart: 11, of which 7 were waited for; matrix products, arithmetic and copies ran while one was open for 35% of the time, Pallas kernels for 0%

commit v1 on v0

v1 whole, which is shorter than its diff:
```python
import functools
import math

import jax
import jax.numpy as jnp
from jax import lax
from jax.experimental import pallas as pl
from jax.experimental.pallas import tpu as pltpu
from jax.sharding import Mesh
from jax.sharding import PartitionSpec as P

MODEL_WIDTH = 2048
HEAD_DIM = 64
ROT = 32
SEQ = 2048
EPSILON = 1e-05
MASKED = -1e30
SCALE = HEAD_DIM ** (-0.5)
VMEM = 60 * 1024 * 1024

BF = jnp.bfloat16
F32 = jnp.float32


def swap(value, axis):
    return lax.ppermute(value, axis, [(0, 1), (1, 0)])


def nt(left, right):
    return lax.dot_general(left, right, (((1,), (1,)), ((), ())), preferred_element_type=F32)


def tn(left, right):
    return lax.dot_general(left, right, (((0,), (0,)), ((), ())), preferred_element_type=F32)


def nn(left, right):
    return lax.dot_general(left, right, (((1,), (0,)), ((), ())), preferred_element_type=F32)


def params():
    return pltpu.CompilerParams(vmem_limit_bytes=VMEM)


def cost(flops, nbytes, transcendentals=0):
    return pl.CostEstimate(
        flops=int(flops), bytes_accessed=int(nbytes), transcendentals=int(transcendentals)
    )


def whole(shape):
    return pl.BlockSpec(shape, lambda *_: (0,) * len(shape))


def pack_kernel(order, sx, qkv, fc1, dense, fc2, near, same, far):
    step = pl.program_id(0)
    x = sx[0]

    def write(put):
        fc2_t = fc2[...].T
        put(0, jnp.where(x == 0, fc2_t[:256], fc2_t[256:]))
        put(256, jnp.where(x == 0, fc2_t[256:], fc2_t[:256]))
        put(512, jnp.where(x == 0, fc1[:256], fc1[256:]))
        put(768, jnp.where(x == 0, fc1[256:], fc1[:256]))
        dense_t = dense[...].T
        for s in range(2):
            base = 1024 + 256 * s
            for part in range(3):
                low, high = qkv[part, :64], qkv[part, 64:]
                first, second = (low, high) if s == 0 else (high, low)
                put(base + 64 * part, jnp.where(x == 0, first, second))
            low, high = dense_t[:64], dense_t[64:]
            first, second = (low, high) if s == 0 else (high, low)
            put(base + 192, jnp.where(x == 0, first, second))

    def into(ref, lead):
        def put(row, value):
            if lead:
                ref[0, row : row + value.shape[0], :] = value
            else:
                ref[row : row + value.shape[0], :] = value

        return put

    @pl.when(step < 2)
    def _():
        write(into(near, True))

    @pl.when(step == 2)
    def _():
        write(into(far, False))

    @pl.when(step == 3)
    def _():
        write(into(same, False))


def pack(order, sx, qkv, fc1, dense, fc2):
    rows = 1536
    return pl.pallas_call(
        pack_kernel,
        grid_spec=pltpu.PrefetchScalarGridSpec(
            num_scalar_prefetch=2,
            grid=(4,),
            in_specs=[
                pl.BlockSpec((3, 128, 512), lambda i, o, x: (0, o[i], 0)),
                pl.BlockSpec((512, 512), lambda i, o, x: (o[i], 0)),
                pl.BlockSpec((512, 128), lambda i, o, x: (0, o[i])),
                pl.BlockSpec((512, 512), lambda i, o, x: (0, o[i])),
            ],
            out_specs=[
                pl.BlockSpec((1, rows, 512), lambda i, o, x: (jnp.minimum(i, 1), 0, 0)),
                pl.BlockSpec((rows, 512), lambda i, o, x: (0, 0)),
                pl.BlockSpec((rows, 512), lambda i, o, x: (0, 0)),
            ],
        ),
        out_shape=[
            jax.ShapeDtypeStruct((2, rows, 512), BF),
            jax.ShapeDtypeStruct((rows, 512), BF),
            jax.ShapeDtypeStruct((rows, 512), BF),
        ],
        compiler_params=params(),
        cost_estimate=cost(0, 4 * rows * 512 * 4),
    )(order, sx, qkv, fc1, dense, fc2)


def unpack_mlp_kernel(order, sx, first, second, fc1_out, fc2_out):
    x = sx[0]
    a, b = first[0].astype(F32), second[0].astype(F32)
    low, high = jnp.where(x == 0, a, b), jnp.where(x == 0, b, a)
    fc1_out[:256, :] = low[256:]
    fc1_out[256:, :] = high[256:]
    fc2_out[:, :256] = low[:256].T
    fc2_out[:, 256:] = high[:256].T


def unpack_mlp(order, sx, first, second):
    piece = pl.BlockSpec((1, 512, 512), lambda i, o, x: (o[i], 0, 0))
    return pl.pallas_call(
        unpack_mlp_kernel,
        grid_spec=pltpu.PrefetchScalarGridSpec(
            num_scalar_prefetch=2,
            grid=(4,),
            in_specs=[piece, piece],
            out_specs=[
                pl.BlockSpec((512, 512), lambda i, o, x: (i, 0)),
                pl.BlockSpec((512, 512), lambda i, o, x: (0, i)),
            ],
        ),
        out_shape=[
            jax.ShapeDtypeStruct((2048, 512), F32),
            jax.ShapeDtypeStruct((512, 2048), F32),
        ],
        compiler_params=params(),
        cost_estimate=cost(0, 12 * 1024 * 1024),
    )(order, sx, first, second)


def unpack_att_kernel(order, sx, first, second, qkv_out, dense_out):
    x = sx[0]
    a, b = first[0].astype(F32), second[0].astype(F32)
    low, high = jnp.where(x == 0, a, b), jnp.where(x == 0, b, a)
    for part in range(3):
        qkv_out[part, :64, :] = low[64 * part : 64 * part + 64]
        qkv_out[part, 64:, :] = high[64 * part : 64 * part + 64]
    dense_out[...] = jnp.concatenate([low[192:], high[192:]], axis=0).T


def unpack_att(order, sx, first, second):
    piece = pl.BlockSpec((1, 256, 512), lambda i, o, x: (o[i], 0, 0))
    return pl.pallas_call(
        unpack_att_kernel,
        grid_spec=pltpu.PrefetchScalarGridSpec(
            num_scalar_prefetch=2,
            grid=(4,),
            in_specs=[piece, piece],
            out_specs=[
                pl.BlockSpec((3, 128, 512), lambda i, o, x: (0, i, 0)),
                pl.BlockSpec((512, 128), lambda i, o, x: (0, i)),
            ],
        ),
        out_shape=[
            jax.ShapeDtypeStruct((3, 512, 512), F32),
            jax.ShapeDtypeStruct((512, 512), F32),
        ],
        compiler_params=params(),
        cost_estimate=cost(0, 6 * 1024 * 1024),
    )(order, sx, first, second)


def norm_kernel(place, xs, scale, normed, stats):
    total = jnp.zeros((256, 1), F32)
    square = jnp.zeros((256, 1), F32)
    for q in range(4):
        value = xs[0, q].astype(F32)
        total += jnp.sum(value, axis=1, keepdims=True)
        square += jnp.sum(value * value, axis=1, keepdims=True)
    average = total / MODEL_WIDTH
    inverse = lax.rsqrt(square / MODEL_WIDTH - average * average + EPSILON)
    for r in range(4):
        value = xs[0, place[r]].astype(F32)
        centered = (value - average) * inverse
        normed[:, 512 * r : 512 * r + 512] = (
            centered * scale[2 * r : 2 * r + 1, :] + scale[2 * r + 1 : 2 * r + 2, :]
        ).astype(BF)
    stats[:, :128] = jnp.broadcast_to(average, (256, 128))
    stats[:, 128:] = jnp.broadcast_to(inverse, (256, 128))


def norm_tokens(place, gathered, scale):
    return pl.pallas_call(
        norm_kernel,
        grid_spec=pltpu.PrefetchScalarGridSpec(
            num_scalar_prefetch=1,
            grid=(8,),
            in_specs=[
                pl.BlockSpec((1, 4, 256, 512), lambda i, o: (i // 4, 0, i % 4, 0)),
                pl.BlockSpec((8, 512), lambda i, o: (0, 0)),
            ],
            out_specs=[
                pl.BlockSpec((256, 2048), lambda i, o: (i, 0)),
                pl.BlockSpec((256, 256), lambda i, o: (i, 0)),
            ],
        ),
        out_shape=[
            jax.ShapeDtypeStruct((SEQ, MODEL_WIDTH), BF),
            jax.ShapeDtypeStruct((SEQ, 256), F32),
        ],
        compiler_params=params(),
        cost_estimate=cost(SEQ * MODEL_WIDTH * 8, SEQ * MODEL_WIDTH * 4 + SEQ * 1024),
    )(place, gathered, scale)


def order_kernel(place, xs, out):
    for r in range(4):
        out[:, 512 * r : 512 * r + 512] = xs[0, place[r]]


def order_tokens(place, gathered):
    return pl.pallas_call(
        order_kernel,
        grid_spec=pltpu.PrefetchScalarGridSpec(
            num_scalar_prefetch=1,
            grid=(8,),
            in_specs=[pl.BlockSpec((1, 4, 256, 512), lambda i, o: (i // 4, 0, i % 4, 0))],
            out_specs=pl.BlockSpec((256, 2048), lambda i, o: (i, 0)),
        ),
        out_shape=jax.ShapeDtypeStruct((SEQ, MODEL_WIDTH), BF),
        compiler_params=params(),
        cost_estimate=cost(0, SEQ * MODEL_WIDTH * 4),
    )(place, gathered)


ROOT = math.sqrt(2.0 / math.pi)
CUBIC = 0.044715
TILE = 512


def store_grad(out, row, value):
    for at, r in enumerate((0, 2, 1, 3)):
        out[at, row : row + value.shape[0], :] = value[:, 512 * r : 512 * r + 512].astype(BF)


def mlp_kernel(n, c, v0, v1, w0, w1, bias, act_out, dfc_out, grad0, grad1, sums, acc):
    step = pl.program_id(0)

    @pl.when(step == 0)
    def _():
        acc[...] = jnp.zeros_like(acc)
        sums[...] = jnp.zeros_like(sums)

    for s, (v, w) in enumerate(((v0, w0), (v1, w1))):
        cols = slice(256 * s, 256 * s + 256)
        pre = nt(n[...], w[...]) + bias[:, cols]
        back = nt(c[...], v[...])
        square = pre * pre
        angle = jnp.tanh(ROOT * pre * (1.0 + CUBIC * square))
        half = 0.5 * (1.0 + angle)
        act = (pre * half).astype(BF)
        slope = half + 0.5 * pre * (1.0 - angle * angle) * (ROOT * (1.0 + 3.0 * CUBIC * square))
        dfc = back * slope
        sums[:, cols] += jnp.sum(dfc, axis=0, keepdims=True)
        dfc = dfc.astype(BF)
        act_out[:, cols] = act
        dfc_out[:, cols] = dfc
        acc[512 * s : 512 * s + 256] += tn(act, c[...])
        acc[512 * s + 256 : 512 * s + 512] += tn(dfc, n[...])

    @pl.when(step == SEQ // TILE - 1)
    def _():
        store_grad(grad0, 0, acc[:512])
        store_grad(grad1, 0, acc[512:])


def mlp(normed, cot, v, w, bias):
    tile = pl.BlockSpec((TILE, MODEL_WIDTH), lambda i: (i, 0))
    weight = whole((256, MODEL_WIDTH))
    units = pl.BlockSpec((TILE, 512), lambda i: (i, 0))
    grad = whole((4, 512, 512))
    return pl.pallas_call(
        mlp_kernel,
        grid=(SEQ // TILE,),
        in_specs=[tile, tile, weight, weight, weight, weight, whole((1, 512))],
        out_specs=[units, units, grad, grad, whole((1, 512))],
        out_shape=[
            jax.ShapeDtypeStruct((SEQ, 512), BF),
            jax.ShapeDtypeStruct((SEQ, 512), BF),
            jax.ShapeDtypeStruct((4, 512, 512), BF),
            jax.ShapeDtypeStruct((4, 512, 512), BF),
            jax.ShapeDtypeStruct((1, 512), F32),
        ],
        scratch_shapes=[pltpu.VMEM((1024, MODEL_WIDTH), F32)],
        compiler_params=params(),
        cost_estimate=cost(8 * SEQ * MODEL_WIDTH * 512, 28 * 1024 * 1024, SEQ * 512),
    )(normed, cot, v[0], v[1], w[0], w[1], bias)


def rotated(value, tables, sign):
    return (
        value * tables[0]
        + pltpu.roll(value, 112, 1) * (sign * tables[1])
        + pltpu.roll(value, 16, 1) * (sign * tables[2])
    )


def heads_kernel(n, c, w0, w1, bias, tables, q_out, k_out, v_out, d_out, joined):
    @pl.when(pl.program_id(0) == 0)
    def _():
        for part in range(4):
            joined[128 * part : 128 * part + 64] = w0[64 * part : 64 * part + 64]
            joined[128 * part + 64 : 128 * part + 128] = w1[64 * part : 64 * part + 64]

    pre = nt(n[...], joined[:384]) + bias[...]
    q_out[...] = (rotated(pre[:, :128], tables, 1.0) * SCALE).astype(BF)
    k_out[...] = rotated(pre[:, 128:256], tables, 1.0).astype(BF)
    v_out[...] = pre[:, 256:].astype(BF)
    d_out[...] = nt(c[...], joined[384:]).astype(BF)


def heads(normed, cot, w, bias, tables):
    tile = pl.BlockSpec((TILE, MODEL_WIDTH), lambda i: (i, 0))
    weight = whole((256, MODEL_WIDTH))
    head = pl.BlockSpec((TILE, 128), lambda i: (i, 0))
    return pl.pallas_call(
        heads_kernel,
        grid=(SEQ // TILE,),
        in_specs=[
            tile,
            tile,
            weight,
            weight,
            whole((1, 384)),
            pl.BlockSpec((3, TILE, 128), lambda i: (0, i, 0)),
        ],
        out_specs=[head] * 4,
        out_shape=[jax.ShapeDtypeStruct((SEQ, 128), BF)] * 4,
        scratch_shapes=[pltpu.VMEM((512, MODEL_WIDTH), BF)],
        compiler_params=params(),
        cost_estimate=cost(2 * SEQ * MODEL_WIDTH * 512, 24 * 1024 * 1024),
    )(normed, cot, w[0], w[1], bias, tables)


BLOCK = 256
BLOCKS = SEQ // BLOCK


def attend_kernel(
    low, q, k, v, d, start, tables, o_out, dq_out, dk_out, dv_out, sums, scores, dk_acc, dv_acc
):
    i = pl.program_id(0)

    @pl.when(i == 0)
    def _():
        dk_acc[...] = jnp.zeros_like(dk_acc)
        dv_acc[...] = jnp.zeros_like(dv_acc)
        sums[...] = jnp.zeros_like(sums)

    lane = lax.broadcasted_iota(jnp.int32, (BLOCK, 128), 1)
    masks = (lane < HEAD_DIM, lane >= HEAD_DIM)
    zero = jnp.zeros((BLOCK, 128), BF)
    queries = [jnp.where(m, q[...], zero) for m in masks]
    grads = [jnp.where(m, d[...], zero) for m in masks]
    col = lax.broadcasted_iota(jnp.int32, (BLOCK, BLOCK), 1)
    row = lax.broadcasted_iota(jnp.int32, (BLOCK, BLOCK), 0) + i * BLOCK
    begin = start[:, :1]

    def at(j):
        return pl.ds(pl.multiple_of(j * BLOCK, BLOCK), BLOCK)

    def score(j, peaks):
        keys = k[at(j), :]
        here = col + j * BLOCK
        allowed = (here >= begin) & (here <= row)
        new = []
        for h in range(2):
            s = jnp.where(allowed, nt(queries[h], keys), MASKED)
            scores[h, j] = s
            new.append(jnp.maximum(peaks[h], jnp.maximum(s[:, :128], s[:, 128:])))
        return tuple(new)

    floor = jnp.full((BLOCK, 128), MASKED, F32)
    peaks = lax.fori_loop(low[i], i + 1, score, (floor, floor))
    peaks = [jnp.max(p, axis=1, keepdims=True) for p in peaks]

    def weigh(j, carry):
        sums_, outs = carry
        values = v[at(j), :]
        new_sums, new_outs = [], []
        for h in range(2):
            p = jnp.exp(scores[h, j] - peaks[h])
            scores[h, j] = p
            new_sums.append(sums_[h] + p[:, :128] + p[:, 128:])
            new_outs.append(outs[h] + nn(p.astype(BF), values))
        return tuple(new_sums), tuple(new_outs)

    blank = jnp.zeros((BLOCK, 128), F32)
    totals, outs = lax.fori_loop(low[i], i + 1, weigh, ((blank, blank), (blank, blank)))
    inverse = [1.0 / jnp.sum(t, axis=1, keepdims=True) for t in totals]
    outs = [outs[h] * inverse[h] for h in range(2)]
    o_out[...] = jnp.where(masks[0], outs[0], outs[1]).astype(BF)
    deltas = [
        jnp.sum(outs[h] * grads[h].astype(F32), axis=1, keepdims=True) for h in range(2)
    ]

    def back(j, carry):
        keys, values = k[at(j), :], v[at(j), :]
        new = []
        dk, dv = dk_acc[at(j), :], dv_acc[at(j), :]
        for h in range(2):
            probs = scores[h, j] * inverse[h]
            d_probs = nt(grads[h], values)
            d_scores = (probs * (d_probs - deltas[h])).astype(BF)
            new.append(carry[h] + nn(d_scores, keys))
            dk += tn(d_scores, queries[h])
            dv += tn(probs.astype(BF), grads[h])
        dk_acc[at(j), :] = dk
        dv_acc[at(j), :] = dv
        return tuple(new)

    dq = lax.fori_loop(low[i], i + 1, back, (blank, blank))
    dq = jnp.where(masks[0], dq[0], dq[1]) * SCALE
    here = [tables[t, at(i), :] for t in range(3)]
    dq = rotated(dq, here, -1.0)
    dq_out[...] = dq.astype(BF)
    sums[0:1, :] += jnp.sum(dq, axis=0, keepdims=True)

    @pl.when(i == BLOCKS - 1)
    def _():
        for j in range(BLOCKS):
            rows = slice(j * BLOCK, (j + 1) * BLOCK)
            dk = rotated(dk_acc[rows], [tables[t, rows] for t in range(3)], -1.0)
            dv = dv_acc[rows]
            dk_out[rows, :] = dk.astype(BF)
            dv_out[rows, :] = dv.astype(BF)
            sums[1:2, :] += jnp.sum(dk, axis=0, keepdims=True)
            sums[2:3, :] += jnp.sum(dv, axis=0, keepdims=True)


def attend(low, q, k, v, d, start, tables):
    tile = pl.BlockSpec((BLOCK, 128), lambda i, o: (i, 0))
    full = pl.BlockSpec((SEQ, 128), lambda i, o: (0, 0))
    head = jax.ShapeDtypeStruct((SEQ, 128), BF)
    return pl.pallas_call(
        attend_kernel,
        grid_spec=pltpu.PrefetchScalarGridSpec(
            num_scalar_prefetch=1,
            grid=(BLOCKS,),
            in_specs=[
                tile,
                full,
                full,
                tile,
                tile,
                pl.BlockSpec((3, SEQ, 128), lambda i, o: (0, 0, 0)),
            ],
            out_specs=[tile, tile, full, full, pl.BlockSpec((8, 128), lambda i, o: (0, 0))],
            scratch_shapes=[
                pltpu.VMEM((2, BLOCKS, BLOCK, BLOCK), F32),
                pltpu.VMEM((SEQ, 128), F32),
                pltpu.VMEM((SEQ, 128), F32),
            ],
        ),
        out_shape=[head, head, head, head, jax.ShapeDtypeStruct((8, 128), F32)],
        compiler_params=params(),
        cost_estimate=cost(6 * 2 * 2 * SEQ * SEQ * 64, 8 * 1024 * 1024, SEQ * SEQ),
    )(low, q, k, v, d, start, tables)


def att_grad_kernel(n, c, dq, dk, dv, o, grad0, grad1, acc):
    step = pl.program_id(0)

    @pl.when(step == 0)
    def _():
        acc[...] = jnp.zeros_like(acc)

    acc[:384] += tn(jnp.concatenate([dq[...], dk[...], dv[...]], axis=1), n[...])
    acc[384:] += tn(o[...], c[...])

    @pl.when(step == SEQ // TILE - 1)
    def _():
        for part in range(4):
            store_grad(grad0, 64 * part, acc[128 * part : 128 * part + 64])
            store_grad(grad1, 64 * part, acc[128 * part + 64 : 128 * part + 128])


def att_grad(normed, cot, dq, dk, dv, o):
    tile = pl.BlockSpec((TILE, MODEL_WIDTH), lambda i: (i, 0))
    head = pl.BlockSpec((TILE, 128), lambda i: (i, 0))
    grad = whole((4, 256, 512))
    return pl.pallas_call(
        att_grad_kernel,
        grid=(SEQ // TILE,),
        in_specs=[tile, tile, head, head, head, head],
        out_specs=[grad, grad],
        out_shape=[jax.ShapeDtypeStruct((4, 256, 512), BF)] * 2,
        scratch_shapes=[pltpu.VMEM((512, MODEL_WIDTH), F32)],
        compiler_params=params(),
        cost_estimate=cost(2 * SEQ * MODEL_WIDTH * 512, 22 * 1024 * 1024),
    )(normed, cot, dq, dk, dv, o)


def project_kernel(parts, zl, *refs):
    count = len(parts)
    lefts, rights = refs[:count], refs[count : -3]
    near, same, joined = refs[-3:]

    @pl.when((pl.program_id(0) == 0) & (pl.program_id(1) == 0))
    def _():
        row, at = 0, 0
        for rows in parts:
            for first, size in rows:
                joined[row : row + size] = rights[at][first : first + size]
                row, at = row + size, at + 1

    left = jnp.concatenate([ref[...] for ref in lefts], axis=1)
    for out, pieces in ((near, (1, 3)), (same, (0, 2))):
        for at, r in enumerate(pieces):
            out[at, 0] = nn(left, joined[:, 512 * r : 512 * r + 512]).astype(BF)


def project(zl, items):
    parts = [[(first, size) for _, first, size in rows] for _, rows in items]
    depth = sum(size for rows in parts for _, size in rows)
    lefts = [left for left, _ in items]
    rights = [right for _, rows in items for right, _, _ in rows]
    half = SEQ // 2
    steps = half // TILE

    def tokens(z, t, s):
        return ((z ^ s[0]) * steps + t, 0)

    out = pl.BlockSpec((2, 1, TILE, 512), lambda z, t, s: (0, z, t, 0))
    shape = jax.ShapeDtypeStruct((2, 2, half, 512), BF)
    return pl.pallas_call(
        functools.partial(project_kernel, parts),
        grid_spec=pltpu.PrefetchScalarGridSpec(
            num_scalar_prefetch=1,
            grid=(2, steps),
            in_specs=[pl.BlockSpec((TILE, left.shape[1]), tokens) for left in lefts]
            + [
                pl.BlockSpec(
                    right.shape, lambda z, t, s: (0, 0), pipeline_mode=pl.Buffered(buffer_count=1)
                )
                for right in rights
            ],
            out_specs=[out, out],
            scratch_shapes=[pltpu.VMEM((depth, MODEL_WIDTH), BF)],
        ),
        out_shape=[shape, shape],
        compiler_params=params(),
        cost_estimate=cost(
            2 * SEQ * MODEL_WIDTH * depth, SEQ * (MODEL_WIDTH + depth) * 2 + 2 * depth * MODEL_WIDTH
        ),
    )(zl, *lefts, *rights)


def add(left, right):
    return (left.astype(F32) + right.astype(F32)).astype(BF)


def scatter_sum(near, same):
    both = add(same, swap(near, "c"))
    mid = both.shape[2] // 2
    from_z = swap(both[1, 1, :mid], "zl")
    from_y = swap(both[1, 1, mid:], "y")
    to_y = jnp.concatenate([add(both[1, 0, :mid], from_z), both[1, 0, mid:]], axis=0)
    to_z = jnp.concatenate([both[0, 1, :mid], add(both[0, 1, mid:], from_y)], axis=0)
    return both[0, 0].astype(F32) + swap(to_y, "y").astype(F32) + swap(to_z, "zl").astype(F32)


def more_dp(value):
    if lax.axis_size("xo") > 1:
        return lax.psum(value, "xo")
    return value


def reduce_grad(own, other):
    mine = add(own[0], swap(own[1], "x"))
    theirs = add(other[0], swap(other[1], "x"))
    back = swap(theirs, "zh")
    far = add(mine[2:], back[2:])
    same = add(mine[:2], back[:2])
    far, same = more_dp(far), more_dp(same)
    near = swap(far, "c")
    across = swap(jnp.stack([same[1], near[1]]), "y")
    first = jnp.concatenate([same[:1], near[:1], across], axis=0)
    return first, swap(first, "x")


def on_device(
    block_input,
    cotangent,
    doc_lengths,
    layernorm_gain,
    layernorm_bias,
    qkv_weight,
    qkv_bias,
    fc1_weight,
    fc1_bias,
    dense_weight,
    fc2_weight,
    out_bias,
):
    x, zh, zl = lax.axis_index("x"), lax.axis_index("zh"), lax.axis_index("zl")
    here = 2 * lax.axis_index("y") + lax.axis_index("c")
    place = jnp.stack([here ^ r for r in range(4)]).astype(jnp.int32)
    sx = x.astype(jnp.int32).reshape(1)
    sz = zl.astype(jnp.int32).reshape(1)

    tokens = lax.all_gather(block_input, ("zl", "y", "c"), axis=0, tiled=False)
    cotangents = lax.all_gather(cotangent, ("zl", "y", "c"), axis=0, tiled=False)

    order = jnp.stack([here ^ r for r in (1, 3, 2, 0)]).astype(jnp.int32)
    near, same, far = pack(order, sx, qkv_weight, fc1_weight, dense_weight, fc2_weight)
    near = swap(near, "c")
    weights = {"own": {}, "other": {}}
    for at, name in enumerate(("fc2", "fc1", "att")):
        rows = slice(512 * at, 512 * at + 512)
        across = swap(jnp.stack([far[rows], near[1, rows]]), "y")
        pieces = (same[rows], near[0, rows], across[0], across[1])
        halves = [
            jnp.concatenate([piece[256 * s : 256 * s + 256] for piece in pieces], axis=1)
            for s in range(2)
        ]
        weights["own"][name] = halves
        first = swap(halves[0], "zh")
        weights["other"][name] = [first, swap(first, "x")]

    scale = jnp.stack([layernorm_gain, layernorm_bias])
    scale = jnp.concatenate([scale, swap(scale, "c")], axis=0)
    scale = jnp.concatenate([scale, swap(scale, "y")], axis=0)
    heads_bias = qkv_bias.reshape(3, 2, HEAD_DIM)
    units_bias = fc1_bias.reshape(2, 256)
    heads_bias = jnp.where(x == 0, heads_bias, heads_bias[:, ::-1])
    units_bias = jnp.where(x == 0, units_bias, units_bias[::-1])
    bias = jnp.concatenate([heads_bias.reshape(1, 384), units_bias.reshape(1, 512)], axis=1)
    biases = {"own": bias, "other": swap(bias, "zh")}

    lengths = lax.dynamic_index_in_dim(doc_lengths, zh, 0, keepdims=False)
    ends = jnp.cumsum(lengths)
    spot = jnp.arange(SEQ, dtype=jnp.int32)
    begin = jnp.sum(jnp.where(spot[:, None] >= ends[None, :], lengths[None, :], 0), axis=1)
    low = (begin[::BLOCK] // BLOCK).astype(jnp.int32)
    start = jnp.broadcast_to(begin[:, None], (SEQ, 128)).astype(jnp.int32)
    freqs = jnp.exp(jnp.arange(ROT // 2, dtype=F32) * (-2.0 * math.log(10000.0) / ROT))
    angle = spot.astype(F32)[:, None] * freqs[None, :]
    cosine, sine = jnp.cos(angle), jnp.sin(angle)
    ones, none = jnp.ones((SEQ, ROT), F32), jnp.zeros((SEQ, ROT // 2), F32)
    tables = jnp.stack(
        [
            jnp.concatenate([cosine, cosine, ones] * 2, axis=1),
            jnp.concatenate([-sine, none, none, none] * 2, axis=1),
            jnp.concatenate([none, sine, none, none] * 2, axis=1),
        ]
    )

    normed, stats = norm_tokens(place, tokens.reshape(2, 4, SEQ // 2, 512), scale)
    cot = order_tokens(place, cotangents.reshape(2, 4, SEQ // 2, 512))

    done = {}
    for block in ("own", "other"):
        w, b = weights[block], biases[block]
        act, dfc, mlp0, mlp1, unit_sums = mlp(normed, cot, w["fc2"], w["fc1"], b[:, 384:])
        q, k, v, d = heads(normed, cot, w["att"], b[:, :384], tables)
        o, dq, dk, dv, head_sums = attend(low, q, k, v, d, start, tables)
        att0, att1 = att_grad(normed, cot, dq, dk, dv, o)
        sums = jnp.concatenate([head_sums[:3].reshape(1, 384), unit_sums], axis=1)
        done[block] = (act, dfc, o, dq, dk, dv, (mlp0, mlp1), (att0, att1), sums)
    own, other = done["own"], done["other"]

    def all_rows(block, name, first, size):
        return [(part, first, size) for part in weights[block][name]]

    branch = scatter_sum(
        *project(
            sz,
            [(own[0], all_rows("own", "fc2", 0, 256)), (other[0], all_rows("other", "fc2", 0, 256))]
            + [(own[2], all_rows("own", "att", 192, 64)), (other[2], all_rows("other", "att", 192, 64))],
        )
    )
    items = [(own[1], all_rows("own", "fc1", 0, 256)), (other[1], all_rows("other", "fc1", 0, 256))]
    for block, values in (("own", own), ("other", other)):
        for part in range(3):
            items.append((values[3 + part], all_rows(block, "att", 64 * part, 64)))
    normed_gradient = scatter_sum(*project(sz, items))

    input_single = block_input.astype(F32)
    result = (input_single + (branch + out_bias)).astype(BF)

    grad_order = place
    fc1_grad, fc2_grad = unpack_mlp(grad_order, sx, *reduce_grad(own[6], other[6]))
    qkv_grad, dense_grad = unpack_att(grad_order, sx, *reduce_grad(own[7], other[7]))

    sums = own[8] + swap(other[8], "zh")
    heads_sum, units_sum = sums[0, :384].reshape(3, 2, HEAD_DIM), sums[0, 384:].reshape(2, 256)
    heads_sum = jnp.where(x == 0, heads_sum, heads_sum[:, ::-1]).reshape(1, 384)
    units_sum = jnp.where(x == 0, units_sum, units_sum[::-1]).reshape(1, 512)
    sums = jnp.concatenate([heads_sum, units_sum], axis=1)
    sums = more_dp(sums + swap(sums, "x"))
    qkv_bias_grad, fc1_bias_grad = sums[0, :384].reshape(3, 128), sums[0, 384:]

    branch_gradient = cotangent.astype(F32)
    mine = lax.dynamic_slice_in_dim(stats, zl * (SEQ // 2), SEQ // 2, axis=0)
    average, inverse = mine[:, :1], mine[:, 128:129]
    centered = (input_single - average) * inverse
    centered_gradient = normed_gradient * layernorm_gain
    row_sums = jnp.stack(
        [jnp.sum(centered_gradient, axis=1), jnp.sum(centered_gradient * centered, axis=1)]
    )
    row_sums = row_sums + swap(row_sums, "c")
    row_sums = row_sums + swap(row_sums, "y")
    input_grad = branch_gradient + inverse * (
        centered_gradient
        - row_sums[0][:, None] / MODEL_WIDTH
        - centered * (row_sums[1][:, None] / MODEL_WIDTH)
    )
    col_sums = jnp.stack(
        [
            jnp.sum(normed_gradient * centered, axis=0),
            jnp.sum(normed_gradient, axis=0),
            jnp.sum(branch_gradient, axis=0),
        ]
    )
    for axis in ("zl", "zh", "x"):
        col_sums = col_sums + swap(col_sums, axis)
    col_sums = more_dp(col_sums)
    return (
        result,
        input_grad,
        col_sums[0],
        col_sums[1],
        qkv_grad,
        qkv_bias_grad,
        fc1_grad,
        fc1_bias_grad,
        dense_grad,
        fc2_grad,
        col_sums[2],
    )


def solution(mesh):
    dp, row, col = mesh.devices.shape
    assert dp % 2 == 0 and row == 4 and col == 4
    parts = Mesh(
        mesh.devices.reshape(dp // 2, 2, 2, 2, 2, 2), ("xo", "x", "zh", "zl", "y", "c")
    )
    data, rows, cols = ("xo", "x"), ("zh", "zl"), ("y", "c")
    return jax.shard_map(
        on_device,
        mesh=parts,
        in_specs=(
            P(data + rows, cols),
            P(data + rows, cols),
            P(data, None),
            P(cols),
            P(cols),
            P(None, rows, cols),
            P(None, rows + cols),
            P(rows, cols),
            P(rows + cols),
            P(cols, rows),
            P(cols, rows),
            P(cols),
        ),
        out_specs=(
            P(data + rows, cols),
            P(data + rows, cols),
            P(cols),
            P(cols),
            P(None, rows, cols),
            P(None, rows + cols),
            P(rows, cols),
            P(rows + cols),
            P(cols, rows),
            P(cols, rows),
            P(cols),
        ),
        check_vma=False,
    )
```

time: 1540 us -> 788 us (0.51)
  waiting for transfers between devices: 897 us -> 376 us
  matrix products: 370 us -> 0 us
  Pallas kernels: 0 us -> 260 us
  other arithmetic: 134 us -> 44.8 us
  starting transfers between devices: 0.92 us -> 58.2 us
  local copies, waits for them, and re-layouts: 67.8 us -> 29.4 us
  blocking collectives: 38.2 us -> 0 us
    reduce_scatter x5 -> x0, waiting for transfers between devices: 511 us -> none  [the longest x1 375 us: on_device(): lax.psum_scatter(times_transpose(flat_weight, normed_rows), 'col', scatte...]
    ppermute x0 -> x42, waiting for transfers between devices: none -> 374 us  [swap(): return lax.ppermute(value, axis, [(0, 1), (1, 0)])]
    dot_general x37 -> x0, matrix products: 370 us -> none  [the longest x15 180 us: times_transpose(): lax.dot_general(left, right, (((1,), (1,)), ((), ())), preferred_element_...]
    all_gather x5 -> x2, waiting for transfers between devices: 281 us -> 0.01 us  [the longest x1 0.01 us: on_device(): tokens = lax.all_gather(block_input, ('zl', 'y', 'c'), axis=0, tiled=False)]
    pallas_call x0 -> x15, Pallas kernels: none -> 260 us  [the longest x2 73.5 us: attend(): pl.pallas_call(attend_kernel, grid_spec=pltpu.PrefetchScalarGridSpec(num_...]
    psum x1 -> x0, waiting for transfers between devices: 104 us -> none  [on_device(): lax.psum(grad_dense.astype(jnp.bfloat16), 'dp').astype(jnp.float32)]
    ppermute x0 -> x42, starting transfers between devices: none -> 58.1 us  [swap(): return lax.ppermute(value, axis, [(0, 1), (1, 0)])]
    reduce_sum x8 -> x2, other arithmetic: 43.2 us -> 1.66 us  [the longest x1 1.57 us: on_device(): jnp.sum(normed_gradient * centered, axis=0)]
  transfers between devices with their start and end apart: 11 -> 44, of which waited for: 7 -> 18; matrix products, arithmetic and copies ran while one was open for 35% -> 9% of each run, Pallas kernels for 0% -> 32%
where the time goes in v1:
time: 788 us; the launch traced here: 783 us
  waiting for transfers between devices  376 us (48%)
  Pallas kernels  260 us (33%)
  starting transfers between devices  58.2 us (7%)
  other arithmetic  44.8 us (6%)
  local copies, waits for them, and re-layouts  29.4 us (4%)
  between operations  15 us (2%)
    ppermute x42, waiting for transfers between devices, swap(): return lax.ppermute(value, axis, [(0, 1), (1, 0)])  374 us
    pallas_call x2, Pallas kernels, attend(): pl.pallas_call(attend_kernel, grid_spec=pltpu.PrefetchScalarGridSpec(num_...  73.5 us
    ppermute x42, starting transfers between devices, swap(): return lax.ppermute(value, axis, [(0, 1), (1, 0)])  58.1 us
    pallas_call x2, Pallas kernels, mlp(): pl.pallas_call(mlp_kernel, grid=(SEQ // TILE,), in_specs=[tile, tile, wei...  56.4 us
    pallas_call x2, Pallas kernels, project(): pl.pallas_call(functools.partial(project_kernel, parts), grid_spec=pltpu....  43.7 us
    pallas_call x2, Pallas kernels, heads(): pl.pallas_call(heads_kernel, grid=(SEQ // TILE,), in_specs=[tile, tile, w...  23.8 us
    pallas_call x2, Pallas kernels, att_grad(): pl.pallas_call(att_grad_kernel, grid=(SEQ // TILE,), in_specs=[tile, tile...  21.2 us
    convert_element_type x10, other arithmetic, add(): return (left.astype(F32) + right.astype(F32)).astype(BF)  19.4 us
  transfers between devices with their start and end apart: 44, of which 18 were waited for; matrix products, arithmetic and copies ran while one was open for 9% of the time, Pallas kernels for 32%

profile of v1, /device:TPU:8, one launch (start us, length us, event | category | flops | bytes accessed | tf_op | source)
XLA Modules:
  0.0 783.2 jit_solution(8542461524061703279)
XLA Ops:
  9.3 7.6 shard_map.205
  20.2 5.4 multiply_cosine_fusion
  30.8 4.3 concatenate.80
  50.8 27.5 %collective-permute-done.10 = bf16[2,512,512]{2,1,0:T(8,128)(2,1)} collective-permute-done((bf16[2,512,512]{2,1,0:T(8,128)(2,1)}, bf16[2,512,512]{2,1,0:T(8,128)(2,1)}, u32[]{:S(2)}, u32[]{:S(2)}) %collective-permute-start.10) | collective-permute-done | bytes 1048608 | tf_op jit(solution)/shard_map/ppermute | solution.py:26
  82.9 32.9 %collective-permute-done.3 = bf16[2,512,512]{2,1,0:T(8,128)(2,1)S(1)} collective-permute-done((bf16[2,512,512]{2,1,0:T(8,128)(2,1)}, bf16[2,512,512]{2,1,0:T(8,128)(2,1)S(1)}, u32[]{:S(2)}, u32[]{:S(2)}) %collective-permute-start.3) | collective-permute-done | bytes 1048608 | tf_op jit(solution)/shard_map/ppermute | solution.py:26
  120.2 36.4 %collective-permute-done.4 = bf16[2,512,512]{2,1,0:T(8,128)(2,1)S(1)} collective-permute-done((bf16[2,512,512]{2,1,0:T(8,128)(2,1)S(1)}, bf16[2,512,512]{2,1,0:T(8,128)(2,1)S(1)}, u32[]{:S(2)}, u32[]{:S(2)}) %collective-permute-start.4) | collective-permute-done | bytes 1048608 | tf_op jit(solution)/shard_map/ppermute | solution.py:26
  170.6 25.4 %collective-permute-done.5.v0.refs_6_ = bf16[256,2048]{1,0:T(8,128)(2,1)} collective-permute-done((bf16[256,2048]{1,0:T(8,128)(2,1)}, bf16[256,2048]{1,0:T(8,128)(2,1)}, u32[]{:S(2)}, u32[]{:S(2)}) %collective-permute-start.5) | collective-permute-done | bytes 1048608 | tf_op jit(solution)/shard_map/ppermute | solution.py:26
  197.4 20.3 %collective-permute-done.7.w0.refs_10_ = bf16[256,2048]{1,0:T(8,128)(2,1)} collective-permute-done((bf16[256,2048]{1,0:T(8,128)(2,1)}, bf16[256,2048]{1,0:T(8,128)(2,1)}, u32[]{:S(2)}, u32[]{:S(2)}) %collective-permute-start.7) | collective-permute-done | bytes 1048608 | tf_op jit(solution)/shard_map/ppermute | solution.py:26
  219.1 9.8 %shard_map.204.c = bf16[2048,2048]{1,0:T(8,128)(2,1)} custom-call(s32[4]{0:T(128)} %pad_add_fusion.place.order, bf16[2,4,1024,512]{3,2,1,0:T(8,128)(2,1)} %bitcast.149), custom_call_target="tpu_custom_call" | custom-call | bytes 16777216 | tf_op jit(solution)/shard_map/pallas_call | solution.py:240
  228.9 12.3 %shard_map.203 = (bf16[2048,2048]{1,0:T(8,128)(2,1)}, f32[2048,256]{1,0:T(8,128)}) custom-call(s32[4]{0:T(128)} %pad_add_fusion.place.order, bf16[2,4,1024,512]{3,2,1,0:T(8,128)(2,1)} %bitcast.150, f32[8,512]{1,0:T(8,128)} %pad_maximum_fusion.18.scale), custom_call_target="tpu_custom_call" | custom-call | flops 33554432 | bytes 18874368 | tf_op jit(solution)/shard_map/pallas_call | solution.py:211
  241.2 11.9 %shard_map.208 = (bf16[2048,128]{1,0:T(8,128)(2,1)}, bf16[2048,128]{1,0:T(8,128)(2,1)}, bf16[2048,128]{1,0:T(8,128)(2,1)}, bf16[2048,128]{1,0:T(8,128)(2,1)}) custom-call(bf16[2048,2048]{1,0:T(8,128)(2,1)} %get-tuple-element.56.n, bf16[2048,2048]{1,0:T(8,128)(2,1)} %shard_map.204.c, bf16[256,2048]{1,0:T(8,128)(2,1)} %copy-done.5, ...), custom_call_target="tpu_custom_call" | custom-call | flops 4294967296 | bytes 25165824 | tf_op jit(solution)/shard_map/pallas_call | solution.py:344
  254.1 11.9 %shard_map.210 = (bf16[2048,128]{1,0:T(8,128)(2,1)}, bf16[2048,128]{1,0:T(8,128)(2,1)}, bf16[2048,128]{1,0:T(8,128)(2,1)}, bf16[2048,128]{1,0:T(8,128)(2,1)}) custom-call(bf16[2048,2048]{1,0:T(8,128)(2,1)} %get-tuple-element.56.n, bf16[2048,2048]{1,0:T(8,128)(2,1)} %shard_map.204.c, bf16[256,2048]{1,0:T(8,128)(2,1)} %copy-done.13, ...), custom_call_target="tpu_custom_call" | custom-call | flops 4294967296 | bytes 25165824 | tf_op jit(solution)/shard_map/pallas_call | solution.py:344
  267.2 36.9 %shard_map.211 = (bf16[2048,128]{1,0:T(8,128)(2,1)}, bf16[2048,128]{1,0:T(8,128)(2,1)}, bf16[2048,128]{1,0:T(8,128)(2,1)}, bf16[2048,128]{1,0:T(8,128)(2,1)}, f32[8,128]{1,0:T(8,128)}) custom-call(s32[8]{0:T(128)} %and_select_fusion.low, bf16[2048,128]{1,0:T(8,128)(2,1)} %get-tuple-element.67.q, bf16[2048,128]{1,0:T(8,128)(2,1)} %get-tuple-element.68.k, ...), custom_call_target="tpu_custom_call" | custom-call | flops 6442450944 | bytes 8388608 | tf_op jit(solution)/shard_map/pallas_call | solution.py:463
  304.1 36.6 %shard_map.209 = (bf16[2048,128]{1,0:T(8,128)(2,1)}, bf16[2048,128]{1,0:T(8,128)(2,1)}, bf16[2048,128]{1,0:T(8,128)(2,1)}, bf16[2048,128]{1,0:T(8,128)(2,1)}, f32[8,128]{1,0:T(8,128)}) custom-call(s32[8]{0:T(128)} %and_select_fusion.low, bf16[2048,128]{1,0:T(8,128)(2,1)} %get-tuple-element.62.q, bf16[2048,128]{1,0:T(8,128)(2,1)} %get-tuple-element.63.k, ...), custom_call_target="tpu_custom_call" | custom-call | flops 6442450944 | bytes 8388608 | tf_op jit(solution)/shard_map/pallas_call | solution.py:463
  340.8 10.6 %shard_map.214 = (bf16[4,256,512]{2,1,0:T(8,128)(2,1)}, bf16[4,256,512]{2,1,0:T(8,128)(2,1)}) custom-call(bf16[2048,2048]{1,0:T(8,128)(2,1)} %get-tuple-element.56.n, bf16[2048,2048]{1,0:T(8,128)(2,1)} %shard_map.204.c, bf16[2048,128]{1,0:T(8,128)(2,1)} %get-tuple-element.77.refs_2_.dq, bf16[2048,128]{1,0:T(8,128)(2,1)} %get-tuple-element.78.refs_3_.dk, ...), custom_call_target="tpu_custom_call" | custom-call | flops 4294967296 | bytes 23068672 | tf_op jit(solution)/shard_map/pallas_call | solution.py:510
  351.4 16.2 %collective-permute-start.28 = (bf16[4,256,512]{2,1,0:T(8,128)(2,1)}, bf16[4,256,512]{2,1,0:T(8,128)(2,1)}, u32[]{:S(2)}, u32[]{:S(2)}) collective-permute-start(bf16[4,256,512]{2,1,0:T(8,128)(2,1)} %get-tuple-element.86), channel_id=1, source_target_pairs={{0,16},{16,0},{1,17},{17,1},{2,18},{18,2},{3,19},{19,3},{4,20},{20... | collective-permute-start | bytes 3145736 | tf_op jit(solution)/shard_map/ppermute | solution.py:26
  367.6 10.6 %shard_map.215 = (bf16[4,256,512]{2,1,0:T(8,128)(2,1)}, bf16[4,256,512]{2,1,0:T(8,128)(2,1)}) custom-call(bf16[2048,2048]{1,0:T(8,128)(2,1)} %get-tuple-element.56.n, bf16[2048,2048]{1,0:T(8,128)(2,1)} %shard_map.204.c, bf16[2048,128]{1,0:T(8,128)(2,1)} %get-tuple-element.80.refs_5_.dq, bf16[2048,128]{1,0:T(8,128)(2,1)} %get-tuple-element.81.refs_6_.dk, ...), custom_call_target="tpu_custom_call" | custom-call | flops 4294967296 | bytes 23068672 | tf_op jit(solution)/shard_map/pallas_call | solution.py:510
  378.2 28.5 %shard_map.207 = (bf16[2048,512]{1,0:T(8,128)(2,1)}, bf16[2048,512]{1,0:T(8,128)(2,1)}, bf16[4,512,512]{2,1,0:T(8,128)(2,1)}, bf16[4,512,512]{2,1,0:T(8,128)(2,1)}, f32[1,512]{1,0:T(1,128)}) custom-call(bf16[2048,2048]{1,0:T(8,128)(2,1)} %get-tuple-element.56.n, bf16[2048,2048]{1,0:T(8,128)(2,1)} %shard_map.204.c, ...), custom_call_target="tpu_custom_call" | custom-call | flops 17179869184 | bytes 29360128 | tf_op jit(solution)/shard_map/pallas_call | solution.py:300
  409.6 28.0 %shard_map.206 = (bf16[2048,512]{1,0:T(8,128)(2,1)}, bf16[2048,512]{1,0:T(8,128)(2,1)}, bf16[4,512,512]{2,1,0:T(8,128)(2,1)}, bf16[4,512,512]{2,1,0:T(8,128)(2,1)}, f32[1,512]{1,0:T(1,128)}) custom-call(bf16[2048,2048]{1,0:T(8,128)(2,1)} %get-tuple-element.56.n, bf16[2048,2048]{1,0:T(8,128)(2,1)} %shard_map.204.c, ...), custom_call_target="tpu_custom_call" | custom-call | flops 17179869184 | bytes 29360128 | tf_op jit(solution)/shard_map/pallas_call | solution.py:300
  437.6 26.2 %shard_map.213 = (bf16[2,2,1024,512]{3,2,1,0:T(8,128)(2,1)}, bf16[2,2,1024,512]{3,2,1,0:T(8,128)(2,1)}) custom-call(s32[1]{0:T(128)} %bitcast.zl, bf16[2048,512]{1,0:T(8,128)(2,1)} %get-tuple-element.75.refs_0_, bf16[2048,512]{1,0:T(8,128)(2,1)} %get-tuple-element.76.refs_1_, bf16[2048,128]{1,0:T(8,128)(2,1)} %get-tuple-element.77.refs_2_.dq, ...), custom_call_target="tpu_custom_call" | custom-call | flops 15032385536 | bytes 23068672 | tf_op jit(solution)/shard_map/pallas_call | solution.py:554
  463.9 17.6 %shard_map.212 = (bf16[2,2,1024,512]{3,2,1,0:T(8,128)(2,1)}, bf16[2,2,1024,512]{3,2,1,0:T(8,128)(2,1)}) custom-call(s32[1]{0:T(128)} %bitcast.zl, bf16[2048,512]{1,0:T(8,128)(2,1)} %get-tuple-element.60.refs_0_, bf16[2048,512]{1,0:T(8,128)(2,1)} %get-tuple-element.61.refs_1_, bf16[2048,128]{1,0:T(8,128)(2,1)} %get-tuple-element.66.refs_2_.o, ...), custom_call_target="tpu_custom_call" | custom-call | flops 10737418240 | bytes 18874368 | tf_op jit(solution)/shard_map/pallas_call | solution.py:554
  496.5 83.8 %collective-permute-done.30 = bf16[4,256,512]{2,1,0:T(8,128)(2,1)} collective-permute-done((bf16[4,256,512]{2,1,0:T(8,128)(2,1)}, bf16[4,256,512]{2,1,0:T(8,128)(2,1)}, u32[]{:S(2)}, u32[]{:S(2)}) %collective-permute-start.30) | collective-permute-done | bytes 1048608 | tf_op jit(solution)/shard_map/ppermute | solution.py:26
  584.2 40.1 %collective-permute-done.38 = bf16[4,512,512]{2,1,0:T(8,128)(2,1)S(1)} collective-permute-done((bf16[4,512,512]{2,1,0:T(8,128)(2,1)}, bf16[4,512,512]{2,1,0:T(8,128)(2,1)S(1)}, u32[]{:S(2)}, u32[]{:S(2)}) %collective-permute-start.38) | collective-permute-done | bytes 2097184 | tf_op jit(solution)/shard_map/ppermute | solution.py:26
  637.4 7.0 collective-permute-done.19
  647.1 8.5 %collective-permute-done.14 = bf16[512,512]{1,0:T(8,128)(2,1)S(1)} collective-permute-done((bf16[512,512]{1,0:T(8,128)(2,1)S(1)}, bf16[512,512]{1,0:T(8,128)(2,1)S(1)}, u32[]{:S(2)}, u32[]{:S(2)}) %collective-permute-start.14) | collective-permute-done | bytes 524320 | tf_op jit(solution)/shard_map/ppermute | solution.py:26
  660.4 17.7 %collective-permute-done.22 = bf16[1024,512]{1,0:T(8,128)(2,1)S(1)} collective-permute-done((bf16[1024,512]{1,0:T(8,128)(2,1)S(1)}, bf16[1024,512]{1,0:T(8,128)(2,1)S(1)}, u32[]{:S(2)}, u32[]{:S(2)}) %collective-permute-start.22) | collective-permute-done | bytes 1048608 | tf_op jit(solution)/shard_map/ppermute | solution.py:26
  681.7 9.6 %collective-permute-done.32 = bf16[2,256,512]{2,1,0:T(8,128)(2,1)S(1)} collective-permute-done((bf16[2,256,512]{2,1,0:T(8,128)(2,1)S(1)}, bf16[2,256,512]{2,1,0:T(8,128)(2,1)S(1)}, u32[]{:S(2)}, u32[]{:S(2)}) %collective-permute-start.32) | collective-permute-done | bytes 524320 | tf_op jit(solution)/shard_map/ppermute | solution.py:26
  693.2 20.6 %collective-permute-done.40 = bf16[2,512,512]{2,1,0:T(8,128)(2,1)S(1)} collective-permute-done((bf16[2,512,512]{2,1,0:T(8,128)(2,1)S(1)}, bf16[2,512,512]{2,1,0:T(8,128)(2,1)S(1)}, u32[]{:S(2)}, u32[]{:S(2)}) %collective-permute-start.40) | collective-permute-done | bytes 1048608 | tf_op jit(solution)/shard_map/ppermute | solution.py:26
  715.3 20.4 %collective-permute-done.24 = f32[2,1024]{1,0:T(2,128)S(1)} collective-permute-done((f32[2,1024]{1,0:T(2,128)S(1)}, f32[2,1024]{1,0:T(2,128)S(1)}, u32[]{:S(2)}, u32[]{:S(2)}) %collective-permute-start.24) | collective-permute-done | bytes 8224 | tf_op jit(solution)/shard_map/ppermute | solution.py:26
  745.2 15.2 %collective-permute-done.35 = f32[1,896]{1,0:T(1,128)S(1)} collective-permute-done((f32[1,896]{1,0:T(1,128)S(1)}, f32[1,896]{1,0:T(1,128)S(1)}, u32[]{:S(2)}, u32[]{:S(2)}) %collective-permute-start.35) | collective-permute-done | bytes 3616 | tf_op jit(solution)/shard_map/ppermute | solution.py:26
  763.8 5.0 shard_map.216
  769.4 6.8 shard_map.217
  (250 shorter events, 117.2 us)
Async XLA Ops:
  7.2 212.0 %all-gather.7.cloned.1.call-start = ((), (), s32[]{:S(2)}) async-start(), calls=%async_computation.1 | async-start | bytes 9437184 | tf_op jit(solution)/shard_map/all_gather | solution.py:631
  7.9 221.0 %all-gather.5.cloned.1.call-start = ((), (), s32[]{:S(2)}) async-start(), calls=%async_computation | async-start | bytes 9437184 | tf_op jit(solution)/shard_map/all_gather | solution.py:630
  17.2 147.7 %collective-permute-start.9 = (f32[1,896]{1,0:T(1,128)S(1)}, f32[1,896]{1,0:T(1,128)S(1)}, u32[]{:S(2)}, u32[]{:S(2)}) collective-permute-start(f32[1,896]{1,0:T(1,128)S(1)} %pad_maximum_fusion.23), channel_id=1, source_target_pairs={{0,8},{8,0},{1,9},{9,1},{2,10},{10,2},{3,11},{11,3},{4,12},{12,4},... | collective-permute-start | bytes 10760 | tf_op jit(solution)/shard_map/ppermute | solution.py:26
  19.9 141.6 %collective-permute-start = (f32[2,512]{1,0:T(2,128)S(1)}, f32[2,512]{1,0:T(2,128)S(1)}, u32[]{:S(2)}, u32[]{:S(2)}) collective-permute-start(f32[2,512]{1,0:T(2,128)S(1)} %pad_maximum_fusion.22), channel_id=1, source_target_pairs={{0,1},{1,0},{2,3},{3,2},{4,5},{5,4},{6,7},{7,6},{8,9},{9,8},{10,11... | collective-permute-start | bytes 12296 | tf_op jit(solution)/shard_map/ppermute | solution.py:26
  39.4 38.9 %collective-permute-start.10 = (bf16[2,512,512]{2,1,0:T(8,128)(2,1)}, bf16[2,512,512]{2,1,0:T(8,128)(2,1)}, u32[]{:S(2)}, u32[]{:S(2)}) collective-permute-start(bf16[2,512,512]{2,1,0:T(8,128)(2,1)} %pad_maximum_fusion.8), channel_id=1, source_target_pairs={{0,2},{2,0},{1,3},{3,1},{4,6},{6,4},{5,7},{7,5},{8,10},{10,8},{9,1... | collective-permute-start | bytes 3145736 | tf_op jit(solution)/shard_map/ppermute | solution.py:26
  46.0 69.8 %collective-permute-start.3 = (bf16[2,512,512]{2,1,0:T(8,128)(2,1)}, bf16[2,512,512]{2,1,0:T(8,128)(2,1)S(1)}, u32[]{:S(2)}, u32[]{:S(2)}) collective-permute-start(bf16[2,512,512]{2,1,0:T(8,128)(2,1)} %pad_maximum_fusion.2), channel_id=1, source_target_pairs={{0,2},{2,0},{1,3},{3,1},{4,6},{6,4},{5,7},{7,5},{8,10},{10,8},{9,1... | collective-permute-start | bytes 3145736 | tf_op jit(solution)/shard_map/ppermute | solution.py:26
  47.2 109.4 %collective-permute-start.4 = (bf16[2,512,512]{2,1,0:T(8,128)(2,1)S(1)}, bf16[2,512,512]{2,1,0:T(8,128)(2,1)S(1)}, u32[]{:S(2)}, u32[]{:S(2)}) collective-permute-start(bf16[2,512,512]{2,1,0:T(8,128)(2,1)S(1)} %pad_maximum_fusion.5), channel_id=1, source_target_pairs={{0,2},{2,0},{1,3},{3,1},{4,6},{6,4},{5,7},{7,5},{8,10},{10,8},{9,1... | collective-permute-start | bytes 3145736 | tf_op jit(solution)/shard_map/ppermute | solution.py:26
  80.5 82.3 %collective-permute-start.11 = (bf16[256,2048]{1,0:T(8,128)(2,1)S(1)}, bf16[256,2048]{1,0:T(8,128)(2,1)S(1)}, u32[]{:S(2)}, u32[]{:S(2)}) collective-permute-start(bf16[256,2048]{1,0:T(8,128)(2,1)S(1)} %pad_maximum_fusion.9.w0.refs_8_.refs_12_.refs_14_.refs_16_), channel_id=1, source_target_pairs={{0,8},{8,0},{1,9},{9,1},{2,10},{10,2},{3,11},{11,3},{4,12},{12,4},... | collective-permute-start | bytes 3145736 | tf_op jit(solution)/shard_map/ppermute | solution.py:26
  117.8 78.2 %collective-permute-start.5 = (bf16[256,2048]{1,0:T(8,128)(2,1)}, bf16[256,2048]{1,0:T(8,128)(2,1)}, u32[]{:S(2)}, u32[]{:S(2)}) collective-permute-start(bf16[256,2048]{1,0:T(8,128)(2,1)} %pad_maximum_fusion.3.v0.refs_4_), channel_id=1, source_target_pairs={{0,8},{8,0},{1,9},{9,1},{2,10},{10,2},{3,11},{11,3},{4,12},{12,4},... | collective-permute-start | bytes 3145736 | tf_op jit(solution)/shard_map/ppermute | solution.py:26
  158.6 59.1 %collective-permute-start.7 = (bf16[256,2048]{1,0:T(8,128)(2,1)}, bf16[256,2048]{1,0:T(8,128)(2,1)}, u32[]{:S(2)}, u32[]{:S(2)}) collective-permute-start(bf16[256,2048]{1,0:T(8,128)(2,1)} %pad_maximum_fusion.6.w0.refs_8_), channel_id=1, source_target_pairs={{0,8},{8,0},{1,9},{9,1},{2,10},{10,2},{3,11},{11,3},{4,12},{12,4},... | collective-permute-start | bytes 3145736 | tf_op jit(solution)/shard_map/ppermute | solution.py:26
  162.8 90.3 %collective-permute-start.12 = (bf16[256,2048]{1,0:T(8,128)(2,1)S(1)}, bf16[256,2048]{1,0:T(8,128)(2,1)S(1)}, u32[]{:S(2)}, u32[]{:S(2)}) collective-permute-start(bf16[256,2048]{1,0:T(8,128)(2,1)S(1)} %collective-permute-done.11.w0.refs_10_.refs_18_.refs_20_.refs_22_), channel_id=1, source_target_pairs={{0,16},{16,0},{1,17},{17,1},{2,18},{18,2},{3,19},{19,3},{4,20},{20... | collective-permute-start | bytes 3145736 | tf_op jit(solution)/shard_map/ppermute | solution.py:26
  196.0 182.2 %collective-permute-start.6 = (bf16[256,2048]{1,0:T(8,128)(2,1)}, bf16[256,2048]{1,0:T(8,128)(2,1)}, u32[]{:S(2)}, u32[]{:S(2)}) collective-permute-start(bf16[256,2048]{1,0:T(8,128)(2,1)} %collective-permute-done.5.v0.refs_6_), channel_id=1, source_target_pairs={{0,16},{16,0},{1,17},{17,1},{2,18},{18,2},{3,19},{19,3},{4,20},{20... | collective-permute-start | bytes 3145736 | tf_op jit(solution)/shard_map/ppermute | solution.py:26
  217.7 160.5 %collective-permute-start.8 = (bf16[256,2048]{1,0:T(8,128)(2,1)}, bf16[256,2048]{1,0:T(8,128)(2,1)}, u32[]{:S(2)}, u32[]{:S(2)}) collective-permute-start(bf16[256,2048]{1,0:T(8,128)(2,1)} %collective-permute-done.7.w0.refs_10_), channel_id=1, source_target_pairs={{0,16},{16,0},{1,17},{17,1},{2,18},{18,2},{3,19},{19,3},{4,20},{20... | collective-permute-start | bytes 3145736 | tf_op jit(solution)/shard_map/ppermute | solution.py:26
  351.4 141.2 %collective-permute-start.28 = (bf16[4,256,512]{2,1,0:T(8,128)(2,1)}, bf16[4,256,512]{2,1,0:T(8,128)(2,1)}, u32[]{:S(2)}, u32[]{:S(2)}) collective-permute-start(bf16[4,256,512]{2,1,0:T(8,128)(2,1)} %get-tuple-element.86), channel_id=1, source_target_pairs={{0,16},{16,0},{1,17},{17,1},{2,18},{18,2},{3,19},{19,3},{4,20},{20... | collective-permute-start | bytes 3145736 | tf_op jit(solution)/shard_map/ppermute | solution.py:26
  378.1 107.1 %collective-permute-start.29 = (bf16[4,256,512]{2,1,0:T(8,128)(2,1)}, bf16[4,256,512]{2,1,0:T(8,128)(2,1)}, u32[]{:S(2)}, u32[]{:S(2)}) collective-permute-start(bf16[4,256,512]{2,1,0:T(8,128)(2,1)} %get-tuple-element.88), channel_id=1, source_target_pairs={{0,16},{16,0},{1,17},{17,1},{2,18},{18,2},{3,19},{19,3},{4,20},{20... | collective-permute-start | bytes 3145736 | tf_op jit(solution)/shard_map/ppermute | solution.py:26
  407.3 75.8 %collective-permute-start.34 = (f32[1,896]{1,0:T(1,128)S(1)}, f32[1,896]{1,0:T(1,128)S(1)}, u32[]{:S(2)}, u32[]{:S(2)}) collective-permute-start(f32[1,896]{1,0:T(1,128)S(1)} %pad_maximum_fusion.24), channel_id=1, source_target_pairs={{0,8},{8,0},{1,9},{9,1},{2,10},{10,2},{3,11},{11,3},{4,12},{12,4},... | collective-permute-start | bytes 10760 | tf_op jit(solution)/shard_map/ppermute | solution.py:26
  409.6 78.4 %collective-permute-start.37 = (bf16[4,512,512]{2,1,0:T(8,128)(2,1)}, bf16[4,512,512]{2,1,0:T(8,128)(2,1)}, u32[]{:S(2)}, u32[]{:S(2)}) collective-permute-start(bf16[4,512,512]{2,1,0:T(8,128)(2,1)} %get-tuple-element.97), channel_id=1, source_target_pairs={{0,16},{16,0},{1,17},{17,1},{2,18},{18,2},{3,19},{19,3},{4,20},{20... | collective-permute-start | bytes 6291464 | tf_op jit(solution)/shard_map/ppermute | solution.py:26
  463.8 161.2 %collective-permute-start.18 = (bf16[2,2,1024,512]{3,2,1,0:T(8,128)(2,1)}, bf16[2,2,1024,512]{3,2,1,0:T(8,128)(2,1)}, u32[]{:S(2)}, u32[]{:S(2)}) collective-permute-start(bf16[2,2,1024,512]{3,2,1,0:T(8,128)(2,1)} %get-tuple-element.84), channel_id=1, source_target_pairs={{0,1},{1,0},{2,3},{3,2},{4,5},{5,4},{6,7},{7,6},{8,9},{9,8},{10,11... | collective-permute-start | bytes 12582920 | tf_op jit(solution)/shard_map/ppermute | solution.py:26
  483.2 98.7 %collective-permute-start.36 = (bf16[4,512,512]{2,1,0:T(8,128)(2,1)}, bf16[4,512,512]{2,1,0:T(8,128)(2,1)}, u32[]{:S(2)}, u32[]{:S(2)}) collective-permute-start(bf16[4,512,512]{2,1,0:T(8,128)(2,1)} %get-tuple-element.95), channel_id=1, source_target_pairs={{0,16},{16,0},{1,17},{17,1},{2,18},{18,2},{3,19},{19,3},{4,20},{20... | collective-permute-start | bytes 6291464 | tf_op jit(solution)/shard_map/ppermute | solution.py:26
  485.2 146.4 %collective-permute-start.13 = (bf16[2,2,1024,512]{3,2,1,0:T(8,128)(2,1)}, bf16[2,2,1024,512]{3,2,1,0:T(8,128)(2,1)}, u32[]{:S(2)}, u32[]{:S(2)}) collective-permute-start(bf16[2,2,1024,512]{3,2,1,0:T(8,128)(2,1)} %get-tuple-element.73), channel_id=1, source_target_pairs={{0,1},{1,0},{2,3},{3,2},{4,5},{5,4},{6,7},{7,6},{8,9},{9,8},{10,11... | collective-permute-start | bytes 12582920 | tf_op jit(solution)/shard_map/ppermute | solution.py:26
  487.9 92.3 %collective-permute-start.30 = (bf16[4,256,512]{2,1,0:T(8,128)(2,1)}, bf16[4,256,512]{2,1,0:T(8,128)(2,1)}, u32[]{:S(2)}, u32[]{:S(2)}) collective-permute-start(bf16[4,256,512]{2,1,0:T(8,128)(2,1)} %add_convert_fusion.6), channel_id=1, source_target_pairs={{0,8},{8,0},{1,9},{9,1},{2,10},{10,2},{3,11},{11,3},{4,12},{12,4},... | collective-permute-start | bytes 3145736 | tf_op jit(solution)/shard_map/ppermute | solution.py:26
  492.6 131.7 %collective-permute-start.38 = (bf16[4,512,512]{2,1,0:T(8,128)(2,1)}, bf16[4,512,512]{2,1,0:T(8,128)(2,1)S(1)}, u32[]{:S(2)}, u32[]{:S(2)}) collective-permute-start(bf16[4,512,512]{2,1,0:T(8,128)(2,1)} %add_convert_fusion.2), channel_id=1, source_target_pairs={{0,8},{8,0},{1,9},{9,1},{2,10},{10,2},{3,11},{11,3},{4,12},{12,4},... | collective-permute-start | bytes 6291464 | tf_op jit(solution)/shard_map/ppermute | solution.py:26
  624.9 33.0 %collective-permute-start.39 = (bf16[2,512,512]{2,1,0:T(8,128)(2,1)S(1)}, bf16[2,512,512]{2,1,0:T(8,128)(2,1)S(1)}, u32[]{:S(2)}, u32[]{:S(2)}) collective-permute-start(bf16[2,512,512]{2,1,0:T(8,128)(2,1)S(1)} %get-tuple-element.108), channel_id=1, source_target_pairs={{0,1},{1,0},{2,3},{3,2},{4,5},{5,4},{6,7},{7,6},{8,9},{9,8},{10,11... | collective-permute-start | bytes 3145736 | tf_op jit(solution)/shard_map/ppermute | solution.py:26
  646.8 31.3 %collective-permute-start.22 = (bf16[1024,512]{1,0:T(8,128)(2,1)S(1)}, bf16[1024,512]{1,0:T(8,128)(2,1)S(1)}, u32[]{:S(2)}, u32[]{:S(2)}) collective-permute-start(bf16[1024,512]{1,0:T(8,128)(2,1)S(1)} %pad_maximum_fusion.14), channel_id=1, source_target_pairs={{0,4},{4,0},{1,5},{5,1},{2,6},{6,2},{3,7},{7,3},{8,12},{12,8},{9,1... | collective-permute-start | bytes 3145736 | tf_op jit(solution)/shard_map/ppermute | solution.py:26
  646.9 33.1 %collective-permute-start.20 = (bf16[1024,512]{1,0:T(8,128)(2,1)S(1)}, bf16[1024,512]{1,0:T(8,128)(2,1)S(1)}, u32[]{:S(2)}, u32[]{:S(2)}) collective-permute-start(bf16[1024,512]{1,0:T(8,128)(2,1)S(1)} %pad_maximum_fusion.13), channel_id=1, source_target_pairs={{0,2},{2,0},{1,3},{3,1},{4,6},{6,4},{5,7},{7,5},{8,10},{10,8},{9,1... | collective-permute-start | bytes 3145736 | tf_op jit(solution)/shard_map/ppermute | solution.py:26
  655.6 35.7 %collective-permute-start.32 = (bf16[2,256,512]{2,1,0:T(8,128)(2,1)S(1)}, bf16[2,256,512]{2,1,0:T(8,128)(2,1)S(1)}, u32[]{:S(2)}, u32[]{:S(2)}) collective-permute-start(bf16[2,256,512]{2,1,0:T(8,128)(2,1)S(1)} %pad_maximum_fusion.17), channel_id=1, source_target_pairs={{0,2},{2,0},{1,3},{3,1},{4,6},{6,4},{5,7},{7,5},{8,10},{10,8},{9,1... | collective-permute-start | bytes 1572872 | tf_op jit(solution)/shard_map/ppermute | solution.py:26
  658.1 55.7 %collective-permute-start.40 = (bf16[2,512,512]{2,1,0:T(8,128)(2,1)S(1)}, bf16[2,512,512]{2,1,0:T(8,128)(2,1)S(1)}, u32[]{:S(2)}, u32[]{:S(2)}) collective-permute-start(bf16[2,512,512]{2,1,0:T(8,128)(2,1)S(1)} %pad_maximum_fusion.16), channel_id=1, source_target_pairs={{0,2},{2,0},{1,3},{3,1},{4,6},{6,4},{5,7},{7,5},{8,10},{10,8},{9,1... | collective-permute-start | bytes 3145736 | tf_op jit(solution)/shard_map/ppermute | solution.py:26
  658.3 77.4 %collective-permute-start.17 = (bf16[1024,512]{1,0:T(8,128)(2,1)S(1)}, bf16[1024,512]{1,0:T(8,128)(2,1)S(1)}, u32[]{:S(2)}, u32[]{:S(2)}) collective-permute-start(bf16[1024,512]{1,0:T(8,128)(2,1)S(1)} %pad_maximum_fusion.12), channel_id=1, source_target_pairs={{0,4},{4,0},{1,5},{5,1},{2,6},{6,2},{3,7},{7,3},{8,12},{12,8},{9,1... | collective-permute-start | bytes 3145736 | tf_op jit(solution)/shard_map/ppermute | solution.py:26
  678.1 57.7 %collective-permute-start.15 = (bf16[1024,512]{1,0:T(8,128)(2,1)S(1)}, bf16[1024,512]{1,0:T(8,128)(2,1)S(1)}, u32[]{:S(2)}, u32[]{:S(2)}) collective-permute-start(bf16[1024,512]{1,0:T(8,128)(2,1)S(1)} %pad_maximum_fusion.11), channel_id=1, source_target_pairs={{0,2},{2,0},{1,3},{3,1},{4,6},{6,4},{5,7},{7,5},{8,10},{10,8},{9,1... | collective-permute-start | bytes 3145736 | tf_op jit(solution)/shard_map/ppermute | solution.py:26
  691.4 71.4 %collective-permute-start.33 = (bf16[4,256,512]{2,1,0:T(8,128)(2,1)S(1)}, bf16[4,256,512]{2,1,0:T(8,128)(2,1)S(1)}, u32[]{:S(2)}, u32[]{:S(2)}) collective-permute-start(bf16[4,256,512]{2,1,0:T(8,128)(2,1)S(1)} %pad_maximum_fusion.15.first), channel_id=1, source_target_pairs={{0,16},{16,0},{1,17},{17,1},{2,18},{18,2},{3,19},{19,3},{4,20},{20... | collective-permute-start | bytes 3145736 | tf_op jit(solution)/shard_map/ppermute | solution.py:26
  692.7 43.0 %collective-permute-start.24 = (f32[2,1024]{1,0:T(2,128)S(1)}, f32[2,1024]{1,0:T(2,128)S(1)}, u32[]{:S(2)}, u32[]{:S(2)}) collective-permute-start(f32[2,1024]{1,0:T(2,128)S(1)} %fusion.20), channel_id=1, source_target_pairs={{0,2},{2,0},{1,3},{3,1},{4,6},{6,4},{5,7},{7,5},{8,10},{10,8},{9,1... | collective-permute-start | bytes 24584 | tf_op jit(solution)/shard_map/ppermute | solution.py:26
  714.0 55.4 %collective-permute-start.41 = (bf16[4,512,512]{2,1,0:T(8,128)(2,1)S(1)}, bf16[4,512,512]{2,1,0:T(8,128)(2,1)}, u32[]{:S(2)}, u32[]{:S(2)}) collective-permute-start(bf16[4,512,512]{2,1,0:T(8,128)(2,1)S(1)} %pad_maximum_fusion.1.first), channel_id=1, source_target_pairs={{0,16},{16,0},{1,17},{17,1},{2,18},{18,2},{3,19},{19,3},{4,20},{20... | collective-permute-start | bytes 6291464 | tf_op jit(solution)/shard_map/ppermute | solution.py:26
  (48 other events, 754.7 us)
Sparse Core Ops, SparseCore 0:
  9.6 60.7 all-gather.6
  72.0 82.5 all-gather.4

commit v2 on v1

v2 whole, which is shorter than its diff:
```python
import math

import jax
import jax.numpy as jnp
from jax import lax
from jax.experimental import pallas as pl
from jax.experimental.pallas import tpu as pltpu
from jax.sharding import Mesh
from jax.sharding import PartitionSpec as P

MODEL_WIDTH = 2048
HEAD_DIM = 64
ROT = 32
SEQ = 2048
EPSILON = 1e-05
MASKED = -1e30
SCALE = HEAD_DIM ** (-0.5)
VMEM = 60 * 1024 * 1024

BF = jnp.bfloat16
F32 = jnp.float32


def swap(value, axis):
    return lax.ppermute(value, axis, [(0, 1), (1, 0)])


def swap_all(values, axis):
    return [swap(value, axis) for value in values]


def nt(left, right):
    return lax.dot_general(left, right, (((1,), (1,)), ((), ())), preferred_element_type=F32)


def tn(left, right):
    return lax.dot_general(left, right, (((0,), (0,)), ((), ())), preferred_element_type=F32)


def nn(left, right):
    return lax.dot_general(left, right, (((1,), (0,)), ((), ())), preferred_element_type=F32)


def shape(*dims, dtype=BF):
    return jax.ShapeDtypeStruct(dims, dtype)


def whole(*dims):
    return pl.BlockSpec(dims, lambda *_: (0,) * len(dims))


def call(body, grid, inputs, outputs, scratch=(), prefetch=(), after=(), carry=()):
    count, waits, kept = len(prefetch) + len(inputs), len(after) + len(carry), len(carry)
    results = len(outputs)

    def kernel(*refs):
        own, rest = refs[:count], refs[count + waits :]
        body(*own, *rest[:results], *rest[results + kept :])

    anywhere = pl.BlockSpec(memory_space=pl.ANY)
    results_ = pl.pallas_call(
        kernel,
        grid_spec=pltpu.PrefetchScalarGridSpec(
            num_scalar_prefetch=len(prefetch),
            grid=grid,
            in_specs=[spec for _, spec in inputs] + [anywhere] * waits,
            out_specs=[spec for _, spec in outputs] + [anywhere] * kept,
            scratch_shapes=list(scratch),
        ),
        out_shape=[out for out, _ in outputs] + [shape(*c.shape, dtype=c.dtype) for c in carry],
        input_output_aliases={count + len(after) + i: results + i for i in range(kept)},
        compiler_params=pltpu.CompilerParams(vmem_limit_bytes=VMEM),
        cost_estimate=pl.CostEstimate(flops=1000, bytes_accessed=1000, transcendentals=0),
    )(*prefetch, *[value for value, _ in inputs], *after, *carry)
    return list(results_)


def pack_kernel(order, sx, qkv, fc1, dense, fc2, near1, near3, far2, own):
    step = pl.program_id(0)
    x = sx[0]

    def write(put, parts):
        fc2_t = fc2[...].T
        dense_t = dense[...].T
        for s in range(parts):

            def pick(low, high, s=s):
                return jnp.where(x == s, low, high)

            put(s, 0, pick(fc2_t[:256], fc2_t[256:]))
            put(s, 256, pick(fc1[:256], fc1[256:]))
            for part in range(3):
                put(s, 512 + 64 * part, pick(qkv[part, :64], qkv[part, 64:]))
            put(s, 704, pick(dense_t[:64], dense_t[64:]))

    def both(ref):
        def put(s, row, value):
            ref[s, row : row + value.shape[0], :] = value

        return put

    def one(ref):
        def put(s, row, value):
            ref[row : row + value.shape[0], :] = value

        return put

    for at, (ref, parts) in enumerate(((near3, 1), (near1, 2), (far2, 1), (own, 2))):

        @pl.when(step == at)
        def _(ref=ref, parts=parts):
            write(both(ref) if parts == 2 else one(ref), parts)


def pack(order, sx, qkv, fc1, dense, fc2):
    return call(
        pack_kernel,
        (4,),
        [
            (qkv, pl.BlockSpec((3, 128, 512), lambda i, o, x: (0, o[i], 0))),
            (fc1, pl.BlockSpec((512, 512), lambda i, o, x: (o[i], 0))),
            (dense, pl.BlockSpec((512, 128), lambda i, o, x: (0, o[i]))),
            (fc2, pl.BlockSpec((512, 512), lambda i, o, x: (0, o[i]))),
        ],
        [
            (shape(2, 768, 512), whole(2, 768, 512)),
            (shape(768, 512), whole(768, 512)),
            (shape(768, 512), whole(768, 512)),
            (shape(2, 768, 512), whole(2, 768, 512)),
        ],
        prefetch=(order, sx),
    )


def stack(items, after=()):
    rows = items[0][3]

    def body(*refs):
        out = refs[-1]
        for at, ((_, lead, first, _), ref) in enumerate(zip(items, refs[:-1], strict=True)):
            if isinstance(lead, slice):
                size = ref.shape[1]
                for k in range(lead.start, lead.stop):
                    out[at, size * (k - lead.start) : size * (k - lead.start + 1), :] = ref[k]
            else:
                out[at] = ref[lead, first : first + rows, :]

    return call(
        body,
        (1,),
        [(array, whole(*array.shape)) for array, _, _, _ in items],
        [(shape(len(items), rows, 512), whole(len(items), rows, 512))],
        after=after,
    )[0]


def split_first(far2, near3, own, near1, after=()):
    def body(far2, near3, own, near1, to_y, att_y, z_mlp):
        for at, ref in enumerate((far2, near3)):
            to_y[at] = ref[:512, :]
            att_y[at] = ref[512:, :]
        for at, ref in enumerate((own, near1)):
            z_mlp[at] = ref[0, :512, :]

    flat, deep = whole(768, 512), whole(1, 768, 512)
    mlp_out = (shape(2, 512, 512), whole(2, 512, 512))
    return call(
        body,
        (1,),
        [(far2, flat), (near3, flat), (own, deep), (near1, deep)],
        [mlp_out, (shape(2, 256, 512), whole(2, 256, 512)), mlp_out],
        after=after,
    )


def stack_att(own, near1, far, after=()):
    def body(own, near1, far, out):
        for at, ref in enumerate((own, near1)):
            out[at] = ref[0, 512:, :]
            out[2 + at] = far[at]

    deep = whole(1, 768, 512)
    return call(
        body,
        (1,),
        [(own, deep), (near1, deep), (far, whole(2, 256, 512))],
        [(shape(4, 256, 512), whole(4, 256, 512))],
        after=after,
    )[0]


def gate(after, carry):
    def body(out):
        out[...] = jnp.zeros_like(out)

    token, *carry = call(
        body, (1,), [], [(shape(8, 128, dtype=F32), whole(8, 128))], after=after, carry=carry
    )
    return token, carry


def piece(array, lead, row, rows=256):
    return (
        array,
        pl.BlockSpec(
            (1, rows, 512),
            lambda *_: (lead, row, 0),
            pipeline_mode=pl.Buffered(buffer_count=1),
        ),
    )


def unpack_mlp_kernel(place, sx, first, second, fc1_out, fc2_out):
    x = sx[0]
    a, b = first[0].astype(F32), second[0].astype(F32)
    low, high = jnp.where(x == 0, a, b), jnp.where(x == 0, b, a)
    fc1_out[:256, :] = low[256:]
    fc1_out[256:, :] = high[256:]
    fc2_out[:, :256] = low[:256].T
    fc2_out[:, 256:] = high[:256].T


def unpack_mlp(place, sx, first, second, after=()):
    block = pl.BlockSpec((1, 512, 512), lambda i, o, x: (o[i], 0, 0))
    return call(
        unpack_mlp_kernel,
        (4,),
        [(first, block), (second, block)],
        [
            (shape(2048, 512, dtype=F32), pl.BlockSpec((512, 512), lambda i, o, x: (i, 0))),
            (shape(512, 2048, dtype=F32), pl.BlockSpec((512, 512), lambda i, o, x: (0, i))),
        ],
        prefetch=(place, sx),
        after=after,
    )


def unpack_att_kernel(place, sx, first, second, qkv_out, dense_out):
    x = sx[0]
    a, b = first[0].astype(F32), second[0].astype(F32)
    low, high = jnp.where(x == 0, a, b), jnp.where(x == 0, b, a)
    for part in range(3):
        qkv_out[part, :64, :] = low[64 * part : 64 * part + 64]
        qkv_out[part, 64:, :] = high[64 * part : 64 * part + 64]
    dense_out[...] = jnp.concatenate([low[192:], high[192:]], axis=0).T


def unpack_att(place, sx, first, second, after=()):
    block = pl.BlockSpec((1, 256, 512), lambda i, o, x: (o[i], 0, 0))
    return call(
        unpack_att_kernel,
        (4,),
        [(first, block), (second, block)],
        [
            (shape(3, 512, 512, dtype=F32), pl.BlockSpec((3, 128, 512), lambda i, o, x: (0, i, 0))),
            (shape(512, 512, dtype=F32), pl.BlockSpec((512, 128), lambda i, o, x: (0, i))),
        ],
        prefetch=(place, sx),
        after=after,
    )


def norm_kernel(place, xs, scale, normed, stats):
    total = jnp.zeros((256, 1), F32)
    square = jnp.zeros((256, 1), F32)
    for q in range(4):
        value = xs[0, q].astype(F32)
        total += jnp.sum(value, axis=1, keepdims=True)
        square += jnp.sum(value * value, axis=1, keepdims=True)
    average = total / MODEL_WIDTH
    inverse = lax.rsqrt(square / MODEL_WIDTH - average * average + EPSILON)
    for r in range(4):
        value = xs[0, place[r]].astype(F32)
        centered = (value - average) * inverse
        normed[:, 512 * r : 512 * r + 512] = (
            centered * scale[2 * r : 2 * r + 1, :] + scale[2 * r + 1 : 2 * r + 2, :]
        ).astype(BF)
    stats[:, :128] = jnp.broadcast_to(average, (256, 128))
    stats[:, 128:] = jnp.broadcast_to(inverse, (256, 128))


def norm_tokens(place, gathered, scale, after=()):
    return call(
        norm_kernel,
        (8,),
        [
            (gathered, pl.BlockSpec((1, 4, 256, 512), lambda i, o: (i // 4, 0, i % 4, 0))),
            (scale, whole(8, 512)),
        ],
        [
            (shape(SEQ, MODEL_WIDTH), pl.BlockSpec((256, 2048), lambda i, o: (i, 0))),
            (shape(SEQ, 256, dtype=F32), pl.BlockSpec((256, 256), lambda i, o: (i, 0))),
        ],
        prefetch=(place,),
        after=after,
    )


ROOT = math.sqrt(2.0 / math.pi)
CUBIC = 0.044715
TILE = 512
HALF = SEQ // 2


def token_inputs(normed, cot):
    per = HALF // TILE
    return [
        (normed, pl.BlockSpec((TILE, MODEL_WIDTH), lambda i, *_: (i, 0))),
        (cot, pl.BlockSpec((1, 4, TILE, 512), lambda i, *_: (i // per, 0, i % per, 0))),
    ]


def store_grad(out, row, value):
    for at, r in enumerate((0, 2, 1, 3)):
        out[at, row : row + value.shape[0], :] = value[:, 512 * r : 512 * r + 512].astype(BF)


def mlp_kernel(place, n, c, *refs):
    weights, (bias, act_out, dfc_out, *grads, sums, w1, w2, acc1, acc2) = refs[:8], refs[8:]
    step = pl.program_id(0)

    @pl.when(step == 0)
    def _():
        acc1[...] = jnp.zeros_like(acc1)
        acc2[...] = jnp.zeros_like(acc2)
        sums[...] = jnp.zeros_like(sums)
        for s in range(2):
            for r in range(4):
                rows, cols = slice(256 * s, 256 * s + 256), slice(512 * r, 512 * r + 512)
                w2[rows, cols] = weights[4 * s + r][0, :256, :]
                w1[rows, cols] = weights[4 * s + r][0, 256:, :]

    pre = nt(n[...], w1[...]) + bias[...]
    back = jnp.zeros((TILE, 512), F32)
    for r in range(4):
        back += nt(c[0, place[r]], w2[:, 512 * r : 512 * r + 512])
    square = pre * pre
    angle = jnp.tanh(ROOT * pre * (1.0 + CUBIC * square))
    half = 0.5 * (1.0 + angle)
    act = (pre * half).astype(BF)
    slope = half + 0.5 * pre * (1.0 - angle * angle) * (ROOT * (1.0 + 3.0 * CUBIC * square))
    dfc = back * slope
    sums[...] += jnp.sum(dfc, axis=0, keepdims=True)
    dfc = dfc.astype(BF)
    act_out[...] = act
    dfc_out[...] = dfc
    for r in range(4):
        acc2[:, 512 * r : 512 * r + 512] += tn(act, c[0, place[r]])
    acc1[...] += tn(dfc, n[...])

    @pl.when(step == SEQ // TILE - 1)
    def _():
        for s in range(2):
            store_grad(grads[s], 0, acc2[256 * s : 256 * s + 256])
            store_grad(grads[2 + s], 0, acc1[256 * s : 256 * s + 256])


def mlp(place, normed, cot, weights, bias, after=(), carry=()):
    units = pl.BlockSpec((TILE, 512), lambda i, *_: (i, 0))
    grad = (shape(4, 256, 512), whole(4, 256, 512))
    return call(
        mlp_kernel,
        (SEQ // TILE,),
        token_inputs(normed, cot)
        + [piece(array, lead, 0, 512) for array, lead in weights]
        + [(bias, whole(1, 512))],
        [(shape(SEQ, 512), units)] * 2
        + [grad] * 4
        + [(shape(1, 512, dtype=F32), whole(1, 512))],
        [
            pltpu.VMEM((512, MODEL_WIDTH), BF),
            pltpu.VMEM((512, MODEL_WIDTH), BF),
            pltpu.VMEM((512, MODEL_WIDTH), F32),
            pltpu.VMEM((512, MODEL_WIDTH), F32),
        ],
        prefetch=(place,),
        after=after,
        carry=carry,
    )


def rotated(value, tables, sign):
    return (
        value * tables[0]
        + pltpu.roll(value, 112, 1) * (sign * tables[1])
        + pltpu.roll(value, 16, 1) * (sign * tables[2])
    )


def heads_kernel(place, n, c, *refs):
    weights, (bias, tables, q_out, k_out, v0_out, v1_out, d_out, joined) = refs[:8], refs[8:]

    @pl.when(pl.program_id(0) == 0)
    def _():
        for s in range(2):
            for r in range(4):
                for part in range(4):
                    row = 128 * part + 64 * s
                    joined[row : row + 64, 512 * r : 512 * r + 512] = weights[4 * s + r][
                        0, 64 * part : 64 * part + 64, :
                    ]

    pre = nt(n[...], joined[:384]) + bias[...]
    q_out[...] = (rotated(pre[:, :128], tables, 1.0) * SCALE).astype(BF)
    k_out[...] = rotated(pre[:, 128:256], tables, 1.0).astype(BF)
    value = pre[:, 256:].astype(BF)
    lane = lax.broadcasted_iota(jnp.int32, value.shape, 1)
    one = jnp.ones_like(value)
    v0_out[...] = jnp.where(lane < HEAD_DIM, value, one)
    v1_out[...] = jnp.where(lane < HEAD_DIM, one, value)
    back = jnp.zeros((TILE, 128), F32)
    for r in range(4):
        back += nt(c[0, place[r]], joined[384:, 512 * r : 512 * r + 512])
    d_out[...] = back.astype(BF)


def heads(place, normed, cot, weights, bias, tables, after=()):
    head = pl.BlockSpec((TILE, 128), lambda i, *_: (i, 0))
    return call(
        heads_kernel,
        (SEQ // TILE,),
        token_inputs(normed, cot)
        + [piece(*weight) for weight in weights]
        + [
            (bias, whole(1, 384)),
            (tables, pl.BlockSpec((3, TILE, 128), lambda i, *_: (0, i, 0))),
        ],
        [(shape(SEQ, 128), head)] * 5,
        [pltpu.VMEM((512, MODEL_WIDTH), BF)],
        prefetch=(place,),
        after=after,
    )


BLOCK = 512
BLOCKS = SEQ // BLOCK


def attend_kernel(
    low, q, k, v0, v1, d, start, tables, o_out, dq_out, dk_out, dv_out, sums, scores, probs, dk_acc, dv_acc
):
    i = pl.program_id(0)

    @pl.when(i == 0)
    def _():
        dk_acc[...] = jnp.zeros_like(dk_acc)
        dv_acc[...] = jnp.zeros_like(dv_acc)
        sums[...] = jnp.zeros_like(sums)

    lane = lax.broadcasted_iota(jnp.int32, (BLOCK, 128), 1)
    masks = (lane < HEAD_DIM, lane >= HEAD_DIM)
    zero = jnp.zeros((BLOCK, 128), BF)
    queries = [jnp.where(m, q[...], zero) for m in masks]
    values = (v0, v1)
    col = lax.broadcasted_iota(jnp.int32, (BLOCK, BLOCK), 1)
    row = lax.broadcasted_iota(jnp.int32, (BLOCK, BLOCK), 0) + i * BLOCK
    begin = start[:, :1]

    def at(j):
        return pl.ds(pl.multiple_of(j * BLOCK, BLOCK), BLOCK)

    def score(j, peaks):
        keys = k[at(j), :]
        here = col + j * BLOCK
        allowed = (here >= begin) & (here <= row)
        new = []
        for h in range(2):
            s = jnp.where(allowed, nt(queries[h], keys), MASKED)
            scores[h, j] = s
            peak = peaks[h]
            for lanes in range(0, BLOCK, 128):
                peak = jnp.maximum(peak, s[:, lanes : lanes + 128])
            new.append(peak)
        return tuple(new)

    floor = jnp.full((BLOCK, 128), MASKED, F32)
    peaks = lax.fori_loop(low[i], i + 1, score, (floor, floor))
    peaks = [jnp.max(p, axis=1, keepdims=True) for p in peaks]

    def weigh(j, outs):
        new = []
        for h in range(2):
            p = jnp.exp(scores[h, j] - peaks[h]).astype(BF)
            probs[h, j] = p
            new.append(outs[h] + nn(p, values[h][at(j), :]))
        return tuple(new)

    blank = jnp.zeros((BLOCK, 128), F32)
    outs = lax.fori_loop(low[i], i + 1, weigh, (blank, blank))
    inverse = [1.0 / outs[0][:, HEAD_DIM : HEAD_DIM + 1], 1.0 / outs[1][:, :1]]
    outs = [outs[h] * inverse[h] for h in range(2)]
    o_out[...] = jnp.where(masks[0], outs[0], outs[1]).astype(BF)

    grads, shifted = [], []
    for h in range(2):
        grad = jnp.where(masks[h], d[...].astype(F32) * inverse[h], 0.0).astype(BF)
        wide = grad.astype(F32)
        delta = jnp.sum(wide * outs[h], axis=1, keepdims=True)
        coarse = delta.astype(BF).astype(F32)
        first = HEAD_DIM * (1 - h)
        wide = jnp.where(lane == first, -coarse, wide)
        shifted.append(jnp.where(lane == first + 1, coarse - delta, wide).astype(BF))
        grads.append(grad)

    def back(j, carry):
        keys = k[at(j), :]
        new = []
        dk, dv = dk_acc[at(j), :], dv_acc[at(j), :]
        for h in range(2):
            p = probs[h, j]
            d_scores = (p.astype(F32) * nt(shifted[h], values[h][at(j), :])).astype(BF)
            new.append(carry[h] + nn(d_scores, keys))
            dk += tn(d_scores, queries[h])
            dv += tn(p, grads[h])
        dk_acc[at(j), :] = dk
        dv_acc[at(j), :] = dv
        return tuple(new)

    dq = lax.fori_loop(low[i], i + 1, back, (blank, blank))
    dq = jnp.where(masks[0], dq[0], dq[1]) * SCALE
    dq = rotated(dq, [tables[t, at(i), :] for t in range(3)], -1.0)
    dq_out[...] = dq.astype(BF)
    sums[0:1, :] += jnp.sum(dq, axis=0, keepdims=True)

    @pl.when(i == BLOCKS - 1)
    def _():
        for j in range(8):
            rows = slice(j * 256, j * 256 + 256)
            dk = rotated(dk_acc[rows], [tables[t, rows] for t in range(3)], -1.0)
            dv = dv_acc[rows]
            dk_out[rows, :] = dk.astype(BF)
            dv_out[rows, :] = dv.astype(BF)
            sums[1:2, :] += jnp.sum(dk, axis=0, keepdims=True)
            sums[2:3, :] += jnp.sum(dv, axis=0, keepdims=True)


def attend(low, q, k, v0, v1, d, start, tables, after=()):
    tile = pl.BlockSpec((BLOCK, 128), lambda i, o: (i, 0))
    full = whole(SEQ, 128)
    head = shape(SEQ, 128)
    return call(
        attend_kernel,
        (BLOCKS,),
        [
            (q, tile),
            (k, full),
            (v0, full),
            (v1, full),
            (d, tile),
            (start, tile),
            (tables, whole(3, SEQ, 128)),
        ],
        [
            (head, tile),
            (head, tile),
            (head, full),
            (head, full),
            (shape(8, 128, dtype=F32), whole(8, 128)),
        ],
        [
            pltpu.VMEM((2, BLOCKS, BLOCK, BLOCK), F32),
            pltpu.VMEM((2, BLOCKS, BLOCK, BLOCK), BF),
            pltpu.VMEM((SEQ, 128), F32),
            pltpu.VMEM((SEQ, 128), F32),
        ],
        prefetch=(low,),
        after=after,
    )


def att_grad_kernel(place, n, c, dq, dk, dv, o, grad0, grad1, grad2, acc):
    step = pl.program_id(0)

    @pl.when(step == 0)
    def _():
        acc[...] = jnp.zeros_like(acc)

    acc[:384] += tn(jnp.concatenate([dq[...], dk[...], dv[...]], axis=1), n[...])
    for r in range(4):
        acc[384:, 512 * r : 512 * r + 512] += tn(o[...], c[0, place[r]])

    @pl.when(step == SEQ // TILE - 1)
    def _():
        for part in range(4):
            row, rows = 128 * part, slice(64 * part, 64 * part + 64)
            store_grad(grad0, 64 * part, acc[row : row + 64])
            value = acc[row + 64 : row + 128]
            for at, (grad, r) in enumerate(((grad1, 0), (grad1, 2), (grad2, 1), (grad2, 3))):
                grad[at % 2, rows, :] = value[:, 512 * r : 512 * r + 512].astype(BF)


def att_grad(place, normed, cot, dq, dk, dv, o, after=()):
    head = pl.BlockSpec((TILE, 128), lambda i, *_: (i, 0))
    return call(
        att_grad_kernel,
        (SEQ // TILE,),
        token_inputs(normed, cot) + [(value, head) for value in (dq, dk, dv, o)],
        [(shape(4, 256, 512), whole(4, 256, 512))] + [(shape(2, 256, 512), whole(2, 256, 512))] * 2,
        [pltpu.VMEM((512, MODEL_WIDTH), F32)],
        prefetch=(place,),
        after=after,
    )


def join(joined, spans, rights):
    row = 0
    for at, (first, size) in enumerate(spans):
        for r in range(4):
            joined[row : row + size, 512 * r : 512 * r + 512] = rights[4 * at + r][
                0, first : first + size, :
            ]
        row += size


def project(prefetch, items, tokens, outputs, store, after=()):
    lefts = [left for left, _ in items]
    parts = [part for _, rows in items for part in rows]
    spans = [(first, size) for _, first, size in parts]
    rights = [piece(*one) for pieces, _, _ in parts for one in pieces]

    def body(*refs):
        scalars, refs = refs[: len(prefetch)], refs[len(prefetch) :]
        left_refs, refs = refs[: len(lefts)], refs[len(lefts) :]
        right_refs, refs = refs[: len(rights)], refs[len(rights) :]
        *outs, joined = refs

        @pl.when(pl.program_id(0) == 0)
        def _():
            join(joined, spans, right_refs)

        left = jnp.concatenate([ref[...] for ref in left_refs], axis=1)
        store(scalars, outs, lambda r: nn(left, joined[:, 512 * r : 512 * r + 512]).astype(BF))

    return call(
        body,
        (SEQ // TILE,),
        [(left, pl.BlockSpec((TILE, left.shape[1]), tokens)) for left in lefts] + rights,
        outputs,
        [pltpu.VMEM((sum(size for _, size in spans), MODEL_WIDTH), BF)],
        prefetch=prefetch,
        after=after,
    )


def project_near(sz, items, after=()):
    per = HALF // TILE

    def store(scalars, outs, value):
        for out, pieces in zip(outs, ((1, 3), (0, 2)), strict=True):
            for at, r in enumerate(pieces):
                out[at, 0] = value(r)

    out = pl.BlockSpec((2, 1, TILE, 512), lambda i, *_: (0, i // per, i % per, 0))
    return project(
        (sz,),
        items,
        lambda i, s: (((i // per) ^ s[0]) * per + i % per, 0),
        [(shape(2, 2, HALF, 512), out)] * 2,
        store,
        after,
    )


def added(values):
    total = values[0].astype(F32)
    for value in values[1:]:
        total = total + value.astype(F32)
    return total.astype(BF)


def grad_inputs(values):
    block = pl.BlockSpec((1, 256, 512), lambda i: (i, 0, 0))
    inputs, reads = [], []
    for value in values:
        at = len(inputs)
        if isinstance(value, list):
            inputs += [(one, whole(2, 256, 512)) for one in value]
            reads.append(lambda refs, step, at=at: refs[at + step // 2][step % 2])
        else:
            inputs.append((value, block))
            reads.append(lambda refs, step, at=at: refs[at][0])
    return inputs, reads


def add(left, right, after=()):
    inputs, reads = grad_inputs([left, right])

    def body(*refs):
        for step in range(4):

            @pl.when(pl.program_id(0) == step)
            def _(step=step):
                refs[-1][0] = added([read(refs, step) for read in reads])

    block = pl.BlockSpec((1, 256, 512), lambda i: (i, 0, 0))
    return call(body, (4,), inputs, [(shape(4, 256, 512), block)], after=after)


def total_grad(groups, after=()):
    inputs, reads = [], []
    for group in groups:
        found, read = grad_inputs(group)
        reads.append((len(inputs), len(found), read))
        inputs += found
    rows = 256 * len(groups)

    def body(*refs):
        near, same = refs[-2:]
        for step in range(4):

            @pl.when(pl.program_id(0) == step)
            def _(step=step):
                out = same if step < 2 else near
                for g, (at, size, read) in enumerate(reads):
                    mine = refs[at : at + size]
                    out[step % 2, 256 * g : 256 * g + 256, :] = added([one(mine, step) for one in read])

    out = (shape(2, rows, 512), whole(2, rows, 512))
    return call(body, (4,), inputs, [out, out], after=after)


def quarters(value):
    return [value[256 * k : 256 * k + 256, :] for k in range(value.shape[0] // 256)]


def received(same, near, to_z, to_y, own, for_y, for_z, at=0):
    own[...] = added([same[0, 0], near[0, 0]])
    for_z[...] = added([same[0, 1], near[0, 1]])
    for_y[...] = added([same[1, 0], near[1, 0]])
    far = quarters(added([same[1, 1], near[1, 1]]))
    for k in range(2):
        to_z[at + k] = far[k]
        to_y[at + k] = far[2 + k]


def passed_on(for_y, from_z, for_z, from_y, to_y, to_z, at=0):
    for k in range(4):
        rows = slice(256 * k, 256 * k + 256)
        to_y[k] = added([for_y[rows, :], from_z[at + k]]) if k < 2 else for_y[rows, :]
        to_z[k] = added([for_z[rows, :], from_y[at + k - 2]]) if k >= 2 else for_z[rows, :]


def blocks(count):
    return (shape(count, 256, 512), whole(count, 256, 512))


def scatter_first(same, near, grad_same, grad_near, after=()):
    def body(same, near, grad_same, grad_near, to_z, to_y, own, for_y, for_z):
        received(same, near, to_z, to_y, own, for_y, for_z)
        for at, ref in enumerate((grad_same, grad_near)):
            to_y[2 + 2 * at] = ref[1, :256, :]
            to_y[3 + 2 * at] = ref[1, 256:, :]

    both, pair = whole(2, 2, HALF, 512), whole(2, 512, 512)
    full = (shape(HALF, 512), whole(HALF, 512))
    return call(
        body,
        (1,),
        [(same, both), (near, both), (grad_same, pair), (grad_near, pair)],
        [blocks(2), blocks(6), full, full, full],
        after=after,
    )


def scatter_both(for_y, from_z, for_z, from_y, same, near, grad_same, grad_near, after=()):
    def body(for_y, from_z, for_z, from_y, same, near, grad_same, grad_near, to_z, to_y, *kept):
        passed_on(for_y, from_z, for_z, from_y, to_y, to_z)
        received(same, near, to_z, to_y, *kept, at=4)
        to_y[6] = grad_same[1]
        to_y[7] = grad_near[1]

    both, pair = whole(2, 2, HALF, 512), whole(2, 256, 512)
    flat, full = whole(HALF, 512), (shape(HALF, 512), whole(HALF, 512))
    return call(
        body,
        (1,),
        [
            (for_y, flat),
            (from_z, pair),
            (for_z, flat),
            (from_y, whole(6, 256, 512)),
            (same, both),
            (near, both),
            (grad_same, pair),
            (grad_near, pair),
        ],
        [blocks(6), blocks(8), full, full, full],
        after=after,
    )


def scatter_last(for_y, from_z, for_z, from_y, after=()):
    def body(for_y, from_z, for_z, from_y, to_z, to_y):
        passed_on(for_y, from_z, for_z, from_y, to_y, to_z, at=4)

    flat = whole(HALF, 512)
    return call(
        body,
        (1,),
        [
            (for_y, flat),
            (from_z, whole(6, 256, 512)),
            (for_z, flat),
            (from_y, whole(8, 256, 512)),
        ],
        [blocks(4), blocks(4)],
        after=after,
    )


def more_dp(value):
    if lax.axis_size("xo") > 1:
        return lax.psum(value, "xo")
    return value


def on_device(
    block_input,
    cotangent,
    doc_lengths,
    layernorm_gain,
    layernorm_bias,
    qkv_weight,
    qkv_bias,
    fc1_weight,
    fc1_bias,
    dense_weight,
    fc2_weight,
    out_bias,
):
    x, zh, zl = lax.axis_index("x"), lax.axis_index("zh"), lax.axis_index("zl")
    here = 2 * lax.axis_index("y") + lax.axis_index("c")
    place = jnp.stack([here ^ r for r in range(4)]).astype(jnp.int32)
    sx = x.astype(jnp.int32).reshape(1)
    sz = zl.astype(jnp.int32).reshape(1)

    tokens = lax.all_gather(block_input, ("zl", "y", "c"), axis=0, tiled=False)
    cot = lax.all_gather(cotangent, ("zl", "y", "c"), axis=0, tiled=False)
    tokens, cot = (value.reshape(2, 4, HALF, 512) for value in (tokens, cot))

    scale = jnp.stack([layernorm_gain, layernorm_bias])
    scale = jnp.concatenate([scale, swap(scale, "c")], axis=0)
    heads_bias = qkv_bias.reshape(3, 2, HEAD_DIM)
    units_bias = fc1_bias.reshape(2, 256)
    heads_bias = jnp.where(x == 0, heads_bias, heads_bias[:, ::-1])
    units_bias = jnp.where(x == 0, units_bias, units_bias[::-1])
    own_bias = jnp.concatenate([heads_bias.reshape(1, 384), units_bias.reshape(1, 512)], axis=1)
    other_bias = swap(own_bias, "zh")

    order = jnp.stack([here ^ r for r in (3, 1, 2, 0)]).astype(jnp.int32)
    near1, near3, far2, r0 = pack(order, sx, qkv_weight, fc1_weight, dense_weight, fc2_weight)
    near3 = swap(near3, "c")
    r1 = swap(near1, "c")

    lengths = lax.dynamic_index_in_dim(doc_lengths, zh, 0, keepdims=False)
    ends = jnp.cumsum(lengths)
    spot = jnp.arange(SEQ, dtype=jnp.int32)
    begin = jnp.sum(jnp.where(spot[:, None] >= ends[None, :], lengths[None, :], 0), axis=1)
    low = (begin[::BLOCK] // BLOCK).astype(jnp.int32)
    start = jnp.broadcast_to(begin[:, None], (SEQ, 128)).astype(jnp.int32)
    freqs = jnp.exp(jnp.arange(ROT // 2, dtype=F32) * (-2.0 * math.log(10000.0) / ROT))
    angle = spot.astype(F32)[:, None] * freqs[None, :]
    cosine, sine = jnp.cos(angle), jnp.sin(angle)
    ones, none = jnp.ones((SEQ, ROT), F32), jnp.zeros((SEQ, ROT // 2), F32)
    tables = jnp.stack(
        [
            jnp.concatenate([cosine, cosine, ones] * 2, axis=1),
            jnp.concatenate([-sine, none, none, none] * 2, axis=1),
            jnp.concatenate([none, sine, none, none] * 2, axis=1),
        ]
    )

    def rows(weights, row, first, size):
        return [
            ([(*one[:2], one[2] if row is None else row) for one in weights[4 * s : 4 * s + 4]], first, size)
            for s in range(2)
        ]

    input_single = block_input.astype(F32)
    branch_gradient = cotangent.astype(F32)

    to_y, att_y, other01 = split_first(far2, near3, r0, r1, after=[scale, other_bias])
    r23, other01, att23 = swap(to_y, "y"), swap(other01, "zh"), swap(att_y, "y")
    scale = jnp.concatenate([scale, swap(scale, "y")], axis=0)
    token, (r23, att23, other01) = gate([to_y, scale, tables, start], [r23, att23, other01])

    other23 = swap(r23, "zh")
    own23, next01 = swap(r23, "x"), swap(other01, "x")
    other_r = stack_att(r0, r1, att23, after=[token])
    normed, stats = norm_tokens(place, tokens, scale, after=[token, other_r])
    token, (other23, own23, next01) = gate([stats], [other23, own23, next01])
    mine = lax.dynamic_slice_in_dim(stats, zl * HALF, HALF, axis=0)
    average, inverse = mine[:, :1], mine[:, 128:129]
    centered = (input_single - average) * inverse

    other_r = swap(other_r, "zh")
    next23, next_att23 = swap(other23, "x"), swap(att23, "x")
    own_w = [(r0, 0), (r1, 0), (r23, 0), (r23, 1), (r0, 1), (r1, 1), (own23, 0), (own23, 1)]
    other_w = [(array, i) for array in (other01, other23, next01, next23) for i in range(2)]
    own_act, own_dfc, *own_mlp, own_units = mlp(
        place, normed, cot, own_w, own_bias[:, 384:], after=[token]
    )
    token, (other_r, next23, next_att23, *own_mlp) = gate(
        [own_units], [other_r, next23, next_att23, *own_mlp]
    )
    other_w[6:] = [(next23, 0), (next23, 1)]

    next_r = swap(other_r, "x")
    other_act, other_dfc, *other_mlp, other_units = mlp(
        place, normed, cot, other_w, other_bias[:, 384:], after=[token]
    )
    token, (next_r, *other_mlp) = gate([other_units], [next_r, *other_mlp])

    own_a = [(r0, 0, 2), (r1, 0, 2), (att23, 0, 0), (att23, 1, 0)]
    own_a += [(r0, 1, 2), (r1, 1, 2), (next_att23, 0, 0), (next_att23, 1, 0)]
    other_a = [(array, i, 0) for array in (other_r, next_r) for i in range(4)]
    from_x = swap(other_mlp[1], "x")
    own_heads = heads(place, normed, cot, own_a, own_bias[:, :384], tables, after=[token])
    other_heads = heads(
        place, normed, cot, other_a, other_bias[:, :384], tables, after=[own_heads[0]]
    )
    token, (from_x, other_mlp[3], own_mlp[1]) = gate(
        [other_heads[0]], [from_x, other_mlp[3], own_mlp[1]]
    )

    fc2 = add(other_mlp[0], from_x, after=[token])[0]
    to_fc2 = swap(fc2, "zh")
    from_x, own_fc2 = swap(other_mlp[3], "x"), swap(own_mlp[1], "x")
    other_o, other_dq, other_dk, other_dv, other_sums = attend(
        low, *other_heads, start, tables, after=[fc2]
    )
    other_att = att_grad(
        place, normed, cot, other_dq, other_dk, other_dv, other_o, after=[other_sums]
    )
    other_sums = jnp.concatenate([other_sums[:3].reshape(1, 384), other_units], axis=1)
    token, (to_fc2, from_x, own_fc2, other_att[1], other_att[2], own_mlp[3], other_sums) = gate(
        [other_att[0]], [to_fc2, from_x, own_fc2, *other_att[1:], own_mlp[3], other_sums]
    )

    fc1 = add(other_mlp[2], from_x, after=[token])[0]
    to_fc1 = swap(fc1, "zh")
    other_sums = swap(other_sums, "zh")
    from_x, own_fc1 = swap_all(other_att[1:], "x"), swap(own_mlp[3], "x")
    own_o, own_dq, own_dk, own_dv, own_sums = attend(
        low, *own_heads, start, tables, after=[fc1]
    )
    items = [(own_dfc, rows(own_w, 1, 0, 256)), (other_dfc, rows(other_w, 1, 0, 256))]
    for part, (left, right) in enumerate(
        ((own_dq, other_dq), (own_dk, other_dk), (own_dv, other_dv))
    ):
        items.append((left, rows(own_a, None, 64 * part, 64)))
        items.append((right, rows(other_a, None, 64 * part, 64)))
    dn_near, dn_same = project_near(sz, items, after=[own_sums])
    own_sums = jnp.concatenate([own_sums[:3].reshape(1, 384), own_units], axis=1)
    token, (to_fc1, from_x[0], from_x[1], own_fc1, other_sums, dn_near) = gate(
        [dn_same, own_sums], [to_fc1, *from_x, own_fc1, other_sums, dn_near]
    )

    dn_near = swap(dn_near, "c")
    mlp_near, mlp_same = total_grad(
        [[own_mlp[0], own_fc2, to_fc2], [own_mlp[2], own_fc1, to_fc1]], after=[token]
    )
    mlp_near, mlp_same = swap(more_dp(mlp_near), "c"), more_dp(mlp_same)
    att = add(other_att[0], from_x, after=[mlp_same])[0]
    to_att = swap(att, "zh")
    own_att = att_grad(place, normed, cot, own_dq, own_dk, own_dv, own_o, after=[att])
    own_from_att = swap_all(own_att[1:], "x")
    items = [
        (own_act, rows(own_w, 0, 0, 256)),
        (other_act, rows(other_w, 0, 0, 256)),
        (own_o, rows(own_a, None, 192, 64)),
        (other_o, rows(other_a, None, 192, 64)),
    ]
    near, same = project_near(sz, items, after=[own_att[0]])
    sums = own_sums + other_sums
    heads_sum, units_sum = sums[0, :384].reshape(3, 2, HEAD_DIM), sums[0, 384:].reshape(2, 256)
    heads_sum = jnp.where(x == 0, heads_sum, heads_sum[:, ::-1]).reshape(1, 384)
    units_sum = jnp.where(x == 0, units_sum, units_sum[::-1]).reshape(1, 512)
    sums = jnp.concatenate([heads_sum, units_sum], axis=1)
    token, (to_att, own_from_att[0], own_from_att[1], mlp_near, dn_near, near) = gate(
        [same], [to_att, *own_from_att, mlp_near, dn_near, near]
    )

    near = swap(near, "c")
    to_z, to_y, dn, for_y, for_z = scatter_first(dn_same, dn_near, mlp_same, mlp_near, after=[token])
    from_z, from_y = swap(to_z, "zl"), swap(to_y, "y")
    att_near, att_same = total_grad([[own_att[0], own_from_att, to_att]], after=[dn])
    att_near, att_same = swap(more_dp(att_near), "c"), more_dp(att_same)
    token, (near, from_z, from_y, att_near) = gate([att_same], [near, from_z, from_y, att_near])

    to_z, to_y, branch, branch_y, branch_z = scatter_both(
        for_y, from_z, for_z, from_y, same, near, att_same, att_near, after=[token]
    )
    dn_z, dn_y = swap(to_z, "zl"), swap(to_y, "y")
    mlp_first = stack(
        [(mlp_same, 0, 0, 512), (mlp_near, 0, 0, 512), (from_y, slice(2, 4), 0, 512)]
        + [(from_y, slice(4, 6), 0, 512)],
        after=[to_y],
    )
    mlp_second, sums_x = swap(mlp_first, "x"), swap(sums, "x")
    token, (dn_y, dn_z, mlp_second, sums_x) = gate(
        [mlp_first, sums], [dn_y, dn_z, mlp_second, sums_x]
    )

    dn = dn.astype(F32) + dn_y[:4].reshape(HALF, 512).astype(F32) + dn_z[:4].reshape(HALF, 512).astype(F32)
    row_sums = jnp.stack(
        [jnp.sum(dn * layernorm_gain, axis=1), jnp.sum(dn * layernorm_gain * centered, axis=1)]
    )
    row_sums = row_sums + swap(row_sums, "c")
    row_sums = row_sums + swap(row_sums, "y")
    to_z, to_y = scatter_last(branch_y, dn_z, branch_z, dn_y, after=[token, row_sums])
    branch_z, branch_y = swap(to_z, "zl"), swap(to_y, "y")
    att_first = stack(
        [(att_same, 0, 0, 256), (att_near, 0, 0, 256), (dn_y, 6, 0, 256), (dn_y, 7, 0, 256)],
        after=[to_y],
    )
    att_second = swap(att_first, "x")
    fc1_grad, fc2_grad = unpack_mlp(place, sx, mlp_first, mlp_second, after=[att_first])
    qkv_grad, dense_grad = unpack_att(place, sx, att_first, att_second, after=[fc1_grad])
    sums = more_dp(sums + sums_x)

    qkv_bias_grad, fc1_bias_grad = sums[0, :384].reshape(3, 128), sums[0, 384:]

    branch = branch.astype(F32) + branch_y.reshape(HALF, 512).astype(F32) + branch_z.reshape(HALF, 512).astype(F32)
    result = (input_single + (branch + out_bias)).astype(BF)
    input_grad = branch_gradient + inverse * (
        dn * layernorm_gain
        - row_sums[0][:, None] / MODEL_WIDTH
        - centered * (row_sums[1][:, None] / MODEL_WIDTH)
    )
    col_sums = jnp.stack(
        [
            jnp.sum(dn * centered, axis=0),
            jnp.sum(dn, axis=0),
            jnp.sum(branch_gradient, axis=0),
        ]
    )
    for axis in ("zl", "zh", "x"):
        col_sums = col_sums + swap(col_sums, axis)
    col_sums = more_dp(col_sums)
    return (
        result,
        input_grad,
        col_sums[0],
        col_sums[1],
        qkv_grad,
        qkv_bias_grad,
        fc1_grad,
        fc1_bias_grad,
        dense_grad,
        fc2_grad,
        col_sums[2],
    )


def solution(mesh):
    dp, row, col = mesh.devices.shape
    assert dp % 2 == 0 and row == 4 and col == 4
    parts = Mesh(
        mesh.devices.reshape(dp // 2, 2, 2, 2, 2, 2), ("xo", "x", "zh", "zl", "y", "c")
    )
    data, rows, cols = ("xo", "x"), ("zh", "zl"), ("y", "c")
    return jax.shard_map(
        on_device,
        mesh=parts,
        in_specs=(
            P(data + rows, cols),
            P(data + rows, cols),
            P(data, None),
            P(cols),
            P(cols),
            P(None, rows, cols),
            P(None, rows + cols),
            P(rows, cols),
            P(rows + cols),
            P(cols, rows),
            P(cols, rows),
            P(cols),
        ),
        out_specs=(
            P(data + rows, cols),
            P(data + rows, cols),
            P(cols),
            P(cols),
            P(None, rows, cols),
            P(None, rows + cols),
            P(rows, cols),
            P(rows + cols),
            P(cols, rows),
            P(cols, rows),
            P(cols),
        ),
        check_vma=False,
    )
```

time: 788 us -> 627 us (0.80)
  waiting for transfers between devices: 376 us -> 197 us
  Pallas kernels: 260 us -> 296 us
  other arithmetic: 44.8 us -> 20.6 us
    ppermute x42 -> x45, waiting for transfers between devices: 374 us -> 182 us  [swap(): return lax.ppermute(value, axis, [(0, 1), (1, 0)])]
    pallas_call x15 -> x36, Pallas kernels: 260 us -> 296 us  [call(): pl.pallas_call(kernel, grid_spec=pltpu.PrefetchScalarGridSpec(num_scalar_...]
    convert_element_type x10 -> x0, other arithmetic: 19.4 us -> none  [add(): return (left.astype(F32) + right.astype(F32)).astype(BF)]
    all_gather x1, waiting for transfers between devices: 0.01 us -> 13.6 us  [on_device(): cot = lax.all_gather(cotangent, ('zl', 'y', 'c'), axis=0, tiled=False)]
    unnamed x79 -> x123, local copies, waits for them, and re-layouts: 2.62 us -> 13.5 us
    slice x12 -> x4, local copies, waits for them, and re-layouts: 11.2 us -> 2.65 us  [the longest x1 1.44 us: on_device(): dn_z[:4].reshape(HALF, 512).astype(F32)]
    ppermute x42 -> x45, starting transfers between devices: 58.1 us -> 53.5 us  [swap(): return lax.ppermute(value, axis, [(0, 1), (1, 0)])]
  transfers between devices with their start and end apart: 44 -> 47, of which waited for: 18 -> 21; matrix products, arithmetic and copies ran while one was open for 9% -> 6% of each run, Pallas kernels for 32% -> 43%
where the time goes in v2:
time: 627 us; the launch traced here: 616 us
  Pallas kernels  296 us (47%)
  waiting for transfers between devices  197 us (31%)
  starting transfers between devices  53.6 us (9%)
  local copies, waits for them, and re-layouts  34 us (5%)
  other arithmetic  20.6 us (3%)
  between operations  15.1 us (2%)
    pallas_call x36, Pallas kernels, call(): pl.pallas_call(kernel, grid_spec=pltpu.PrefetchScalarGridSpec(num_scalar_...  296 us
    ppermute x45, waiting for transfers between devices, swap(): return lax.ppermute(value, axis, [(0, 1), (1, 0)])  182 us
    ppermute x45, starting transfers between devices, swap(): return lax.ppermute(value, axis, [(0, 1), (1, 0)])  53.5 us
    all_gather x1, waiting for transfers between devices, on_device(): cot = lax.all_gather(cotangent, ('zl', 'y', 'c'), axis=0, tiled=False)  13.6 us
    unnamed x123, local copies, waits for them, and re-layouts  13.5 us
  transfers between devices with their start and end apart: 47, of which 21 were waited for; matrix products, arithmetic and copies ran while one was open for 6% of the time, Pallas kernels for 43%

profile of v2, /device:TPU:8, one launch (start us, length us, event | category | flops | bytes accessed | tf_op | source)
XLA Modules:
  0.0 616.0 jit_solution(4713607213811808792)
XLA Ops:
  9.3 7.0 %shard_map.203 = (bf16[2,768,512]{2,1,0:T(8,128)(2,1)}, bf16[768,512]{1,0:T(8,128)(2,1)}, bf16[768,512]{1,0:T(8,128)(2,1)}, bf16[2,768,512]{2,1,0:T(8,128)(2,1)}) custom-call(s32[4]{0:T(128)} %pad_add_fusion.1.refs_0_, s32[1]{0:T(128)} %bitcast.8.refs_1_, bf16[3,512,512]{2,1,0:T(8,128)(2,1)} %refs_2_.1, bf16[2048,512]{1,0:T(8,128)(2,1)} %refs_3_.1, ...), custom_call_target="tpu_custom_call" | custom-call | flops 1000 | bytes 1000 | tf_op jit(solution)/shard_map/pallas_call | solution.py:61
  30.7 5.5 multiply_cosine_fusion
  37.3 4.5 concatenate.35
  43.9 4.6 concatenate.38
  55.1 34.2 %collective-permute-done.1 = f32[4,512]{1,0:T(4,128)S(1)} collective-permute-done((f32[4,512]{1,0:T(4,128)S(1)}, f32[4,512]{1,0:T(4,128)S(1)}, u32[]{:S(2)}, u32[]{:S(2)}) %collective-permute-start.1) | collective-permute-done | bytes 8224 | tf_op jit(solution)/shard_map/ppermute | solution.py:25
  100.5 12.3 %shard_map.207 = (bf16[2048,2048]{1,0:T(8,128)(2,1)}, f32[2048,256]{1,0:T(8,128)}) custom-call(s32[4]{0:T(128)} %pad_add_fusion.refs_0_, bf16[2,4,1024,512]{3,2,1,0:T(8,128)(2,1)} %bitcast.88, f32[8,512]{1,0:T(8,128)} %pad_maximum_fusion.1.refs_1_.refs_2_, f32[8,128]{1,0:T(8,128)} %get-tuple-element.149.refs_3_, bf16[4,256,512]{2,1,0:T(8,128)(2,1)} %shard_map.206.refs_4_), custom_call_target="tpu_custom_call" | custom-call | flops 1000 | bytes 1000 | tf_op jit(solution)/shard_map/pallas_call | solution.py:61
  112.8 5.9 collective-permute-done.10.refs_3_
  118.7 21.0 %collective-permute-done.9.refs_2_ = bf16[2,512,512]{2,1,0:T(8,128)(2,1)} collective-permute-done((bf16[2,512,512]{2,1,0:T(8,128)(2,1)}, bf16[2,512,512]{2,1,0:T(8,128)(2,1)}, u32[]{:S(2)}, u32[]{:S(2)}) %collective-permute-start.9) | collective-permute-done | bytes 1048608 | tf_op jit(solution)/shard_map/ppermute | solution.py:25
  139.7 4.3 collective-permute-done.8.refs_1_
  147.6 13.6 %all-gather.7.cloned.1.call-done = bf16[8192,512]{1,0:T(8,128)(2,1)} async-done(((bf16[1024,512]{1,0:T(8,128)(2,1)}), bf16[8192,512]{1,0:T(8,128)(2,1)}) %all-gather.7.cloned.1.call-update) | async-done | bytes 8388624 | tf_op jit(solution)/shard_map/all_gather | solution.py:838
  161.2 27.6 %shard_map.209 = (bf16[2048,512]{1,0:T(8,128)(2,1)}, bf16[2048,512]{1,0:T(8,128)(2,1)}, bf16[4,256,512]{2,1,0:T(8,128)(2,1)}, bf16[4,256,512]{2,1,0:T(8,128)(2,1...) custom-call(s32[4]{0:T(128)} %pad_add_fusion.refs_0_, ...), custom_call_target="tpu_custom_call" | custom-call | flops 1000 | bytes 1000 | tf_op jit(solution)/shard_map/pallas_call | solution.py:61
  193.6 28.0 %shard_map.211 = (bf16[2048,512]{1,0:T(8,128)(2,1)}, bf16[2048,512]{1,0:T(8,128)(2,1)}, bf16[4,256,512]{2,1,0:T(8,128)(2,1)}, bf16[4,256,512]{2,1,0:T(8,128)(2,1...) custom-call(s32[4]{0:T(128)} %pad_add_fusion.refs_0_, ...), custom_call_target="tpu_custom_call" | custom-call | flops 1000 | bytes 1000 | tf_op jit(solution)/shard_map/pallas_call | solution.py:61
  223.8 12.6 %shard_map.213 = (bf16[2048,128]{1,0:T(8,128)(2,1)}, bf16[2048,128]{1,0:T(8,128)(2,1)}, bf16[2048,128]{1,0:T(8,128)(2,1)}, bf16[2048,128]{1,0:T(8,128)(2,1)}, bf16[2048,128]{1,0:T(8,128)(2,1)}) custom-call(s32[4]{0:T(128)} %pad_add_fusion.refs_0_, bf16[2048,2048]{1,0:T(8,128)(2,1)} %get-tuple-element.151.refs_1_, bf16[2,4,1024,512]{3,2,1,0:T(8,128)(2,1)} %bitcast.84, ...), custom_call_target="tpu_custom_call" | custom-call | flops 1000 | bytes 1000 | tf_op jit(solution)/shard_map/pallas_call | solution.py:61
  236.4 12.6 %shard_map.214 = (bf16[2048,128]{1,0:T(8,128)(2,1)}, bf16[2048,128]{1,0:T(8,128)(2,1)}, bf16[2048,128]{1,0:T(8,128)(2,1)}, bf16[2048,128]{1,0:T(8,128)(2,1)}, bf16[2048,128]{1,0:T(8,128)(2,1)}) custom-call(s32[4]{0:T(128)} %pad_add_fusion.refs_0_, bf16[2048,2048]{1,0:T(8,128)(2,1)} %get-tuple-element.151.refs_1_, bf16[2,4,1024,512]{3,2,1,0:T(8,128)(2,1)} %bitcast.85, ...), custom_call_target="tpu_custom_call" | custom-call | flops 1000 | bytes 1000 | tf_op jit(solution)/shard_map/pallas_call | solution.py:61
  260.6 29.5 %shard_map.217 = (bf16[2048,128]{1,0:T(8,128)(2,1)}, bf16[2048,128]{1,0:T(8,128)(2,1)}, bf16[2048,128]{1,0:T(8,128)(2,1)}, bf16[2048,128]{1,0:T(8,128)(2,1)}, f32[8,128]{1,0:T(8,128)}) custom-call(s32[4]{0:T(128)} %and_select_fusion.refs_0_, bf16[2048,128]{1,0:T(8,128)(2,1)} %get-tuple-element.183.refs_0_.refs_1_, ...), custom_call_target="tpu_custom_call" | custom-call | flops 1000 | bytes 1000 | tf_op jit(solution)/shard_map/pallas_call | solution.py:61
  290.1 11.4 %shard_map.218 = (bf16[4,256,512]{2,1,0:T(8,128)(2,1)}, bf16[2,256,512]{2,1,0:T(8,128)(2,1)}, bf16[2,256,512]{2,1,0:T(8,128)(2,1)}) custom-call(s32[4]{0:T(128)} %pad_add_fusion.refs_0_, bf16[2048,2048]{1,0:T(8,128)(2,1)} %get-tuple-element.151.refs_1_, bf16[2,4,1024,512]{3,2,1,0:T(8,128)(2,1)} %bitcast.86, ...), custom_call_target="tpu_custom_call" | custom-call | flops 1000 | bytes 1000 | tf_op jit(solution)/shard_map/pallas_call | solution.py:61
  316.0 29.4 %shard_map.221 = (bf16[2048,128]{1,0:T(8,128)(2,1)}, bf16[2048,128]{1,0:T(8,128)(2,1)}, bf16[2048,128]{1,0:T(8,128)(2,1)}, bf16[2048,128]{1,0:T(8,128)(2,1)}, f32[8,128]{1,0:T(8,128)}) custom-call(s32[4]{0:T(128)} %and_select_fusion.refs_0_, bf16[2048,128]{1,0:T(8,128)(2,1)} %get-tuple-element.176.refs_13_.refs_1_, ...), custom_call_target="tpu_custom_call" | custom-call | flops 1000 | bytes 1000 | tf_op jit(solution)/shard_map/pallas_call | solution.py:61
  346.1 26.3 %shard_map.222 = (bf16[2,2,1024,512]{3,2,1,0:T(8,128)(2,1)}, bf16[2,2,1024,512]{3,2,1,0:T(8,128)(2,1)}) custom-call(s32[1]{0:T(128)} %bitcast.refs_0_, bf16[2048,512]{1,0:T(8,128)(2,1)} %get-tuple-element.157.refs_1_, bf16[2048,512]{1,0:T(8,128)(2,1)} %get-tuple-element.167.refs_2_, bf16[2048,128]{1,0:T(8,128)(2,1)} %get-tuple-element.207.refs_3_, ...), custom_call_target="tpu_custom_call" | custom-call | flops 1000 | bytes 1000 | tf_op jit(solution)/shard_map/pallas_call | solution.py:61
  374.6 5.0 shard_map.224
  385.9 11.2 %shard_map.226 = (bf16[4,256,512]{2,1,0:T(8,128)(2,1)}, bf16[2,256,512]{2,1,0:T(8,128)(2,1)}, bf16[2,256,512]{2,1,0:T(8,128)(2,1)}) custom-call(s32[4]{0:T(128)} %pad_add_fusion.refs_0_, bf16[2048,2048]{1,0:T(8,128)(2,1)} %get-tuple-element.151.refs_1_, bf16[2,4,1024,512]{3,2,1,0:T(8,128)(2,1)} %bitcast.87, bf16[2048,128]{1,0:T(8,128)(2,1)} %get-tuple-element.207.refs_3_, ...), custom_call_target="tpu_custom_call" | custom-call | flops 1000 | bytes 1000 | tf_op jit(solution)/shard_map/pallas_call | solution.py:61
  399.2 17.7 %shard_map.227 = (bf16[2,2,1024,512]{3,2,1,0:T(8,128)(2,1)}, bf16[2,2,1024,512]{3,2,1,0:T(8,128)(2,1)}) custom-call(s32[1]{0:T(128)} %bitcast.refs_0_, bf16[2048,512]{1,0:T(8,128)(2,1)} %get-tuple-element.212.refs_1_, bf16[2048,512]{1,0:T(8,128)(2,1)} %get-tuple-element.213.refs_2_, bf16[2048,128]{1,0:T(8,128)(2,1)} %get-tuple-element.214.refs_6_.refs_3_, ...), custom_call_target="tpu_custom_call" | custom-call | flops 1000 | bytes 1000 | tf_op jit(solution)/shard_map/pallas_call | solution.py:61
  416.9 5.8 collective-permute-done.26.refs_3_
  422.7 8.6 %collective-permute-done.24.refs_1_ = bf16[4,256,512]{2,1,0:T(8,128)(2,1)S(1)} collective-permute-done((bf16[4,256,512]{2,1,0:T(8,128)(2,1)}, bf16[4,256,512]{2,1,0:T(8,128)(2,1)S(1)}, u32[]{:S(2)}, u32[]{:S(2)}) %collective-permute-start.24) | collective-permute-done | bytes 1048608 | tf_op jit(solution)/shard_map/ppermute | solution.py:25
  433.3 6.6 %shard_map.229 = (bf16[2,256,512]{2,1,0:T(8,128)(2,1)}, bf16[6,256,512]{2,1,0:T(8,128)(2,1)}, bf16[1024,512]{1,0:T(8,128)(2,1)}, bf16[1024,512]{1,0:T(8,128)(2,1)}, bf16[1024,512]{1,0:T(8,128)(2,1)}) custom-call(bf16[2,2,1024,512]{3,2,1,0:T(8,128)(2,1)} %get-tuple-element.211.refs_0_, bf16[2,2,1024,512]{3,2,1,0:T(8,128)(2,1)} %get-tuple-element.237.refs_1_, ...), custom_call_target="tpu_custom_call" | custom-call | flops 1000 | bytes 1000 | tf_op jit(solution)/shard_map/pallas_call | solution.py:61
  447.6 8.4 %collective-permute-done.30.refs_2_ = bf16[2,256,512]{2,1,0:T(8,128)(2,1)S(1)} collective-permute-done((bf16[2,256,512]{2,1,0:T(8,128)(2,1)}, bf16[2,256,512]{2,1,0:T(8,128)(2,1)S(1)}, u32[]{:S(2)}, u32[]{:S(2)}) %collective-permute-start.30) | collective-permute-done | bytes 524320 | tf_op jit(solution)/shard_map/ppermute | solution.py:25
  455.9 20.9 %collective-permute-done.31.refs_3_ = bf16[6,256,512]{2,1,0:T(8,128)(2,1)S(1)} collective-permute-done((bf16[6,256,512]{2,1,0:T(8,128)(2,1)}, bf16[6,256,512]{2,1,0:T(8,128)(2,1)S(1)}, u32[]{:S(2)}, u32[]{:S(2)}) %collective-permute-start.31) | collective-permute-done | bytes 1572896 | tf_op jit(solution)/shard_map/ppermute | solution.py:25
  478.6 8.0 %shard_map.232 = (bf16[6,256,512]{2,1,0:T(8,128)(2,1)}, bf16[8,256,512]{2,1,0:T(8,128)(2,1)}, bf16[1024,512]{1,0:T(8,128)(2,1)}, bf16[1024,512]{1,0:T(8,128)(2,1)}, bf16[1024,512]{1,0:T(8,128)(2,1)}) custom-call(bf16[1024,512]{1,0:T(8,128)(2,1)} %get-tuple-element.240.refs_0_, bf16[2,256,512]{2,1,0:T(8,128)(2,1)} %get-tuple-element.250.refs_1_, ...), custom_call_target="tpu_custom_call" | custom-call | flops 1000 | bytes 1000 | tf_op jit(solution)/shard_map/pallas_call | solution.py:61
  498.2 40.0 %collective-permute-done.36.refs_5_ = f32[1,896]{1,0:T(1,128)S(1)} collective-permute-done((f32[1,896]{1,0:T(1,128)S(1)}, f32[1,896]{1,0:T(1,128)S(1)}, u32[]{:S(2)}, u32[]{:S(2)}) %collective-permute-start.36) | collective-permute-done | bytes 3616 | tf_op jit(solution)/shard_map/ppermute | solution.py:25
  562.6 17.0 %collective-permute-done.40 = bf16[4,256,512]{2,1,0:T(8,128)(2,1)} collective-permute-done((bf16[4,256,512]{2,1,0:T(8,128)(2,1)}, bf16[4,256,512]{2,1,0:T(8,128)(2,1)}, u32[]{:S(2)}, u32[]{:S(2)}) %collective-permute-start.40) | collective-permute-done | bytes 1048608 | tf_op jit(solution)/shard_map/ppermute | solution.py:25
  581.1 4.6 convert_reduce_fusion
  596.4 6.8 %shard_map.237 = (f32[2048,512]{1,0:T(8,128)}, f32[512,2048]{1,0:T(8,128)}) custom-call(s32[4]{0:T(128)} %pad_add_fusion.refs_0_, s32[1]{0:T(128)} %bitcast.8.refs_1_, bf16[4,512,512]{2,1,0:T(8,128)(2,1)} %shard_map.233.refs_0_.refs_2_, bf16[4,512,512]{2,1,0:T(8,128)(2,1)} %get-tuple-element.267.refs_3_, bf16[4,256,512]{2,1,0:T(8,128)(2,1)} %shard_map.236.refs_4_.refs_2_), custom_call_target="tpu_custom_call" | custom-call | flops 1000 | bytes 1000 | tf_op jit(solution)/shard_map/pallas_call | solution.py:61
  603.2 5.0 shard_map.238
  (285 shorter events, 145.2 us)
Async XLA Ops:
  7.2 93.3 %all-gather.5.cloned.1.call-start = ((), (), s32[]{:S(2)}) async-start(), calls=%async_computation | async-start | bytes 9437184 | tf_op jit(solution)/shard_map/all_gather | solution.py:837
  7.9 153.3 %all-gather.7.cloned.1.call-start = ((), (), s32[]{:S(2)}) async-start(), calls=%async_computation.1 | async-start | bytes 9437184 | tf_op jit(solution)/shard_map/all_gather | solution.py:838
  26.5 63.5 %collective-permute-start.7 = (bf16[2,512,512]{2,1,0:T(8,128)(2,1)}, bf16[2,512,512]{2,1,0:T(8,128)(2,1)S(1)}, u32[]{:S(2)}, u32[]{:S(2)}) collective-permute-start(bf16[2,512,512]{2,1,0:T(8,128)(2,1)} %get-tuple-element.148), channel_id=1, source_target_pairs={{0,8},{8,0},{1,9},{9,1},{2,10},{10,2},{3,11},{11,3},{4,12},{12,4},... | collective-permute-start | bytes 3145736 | tf_op jit(solution)/shard_map/ppermute | solution.py:25
  29.2 60.8 %collective-permute-start.5 = (bf16[2,512,512]{2,1,0:T(8,128)(2,1)}, bf16[2,512,512]{2,1,0:T(8,128)(2,1)S(1)}, u32[]{:S(2)}, u32[]{:S(2)}) collective-permute-start(bf16[2,512,512]{2,1,0:T(8,128)(2,1)} %get-tuple-element.146.refs_0_), channel_id=1, source_target_pairs={{0,2},{2,0},{1,3},{3,1},{4,6},{6,4},{5,7},{7,5},{8,10},{10,8},{9,1... | collective-permute-start | bytes 3145736 | tf_op jit(solution)/shard_map/ppermute | solution.py:25
  51.1 38.9 %collective-permute-start.6 = (bf16[2,256,512]{2,1,0:T(8,128)(2,1)S(1)}, bf16[2,256,512]{2,1,0:T(8,128)(2,1)S(1)}, u32[]{:S(2)}, u32[]{:S(2)}) collective-permute-start(bf16[2,256,512]{2,1,0:T(8,128)(2,1)S(1)} %copy-done.57), channel_id=1, source_target_pairs={{0,2},{2,0},{1,3},{3,1},{4,6},{6,4},{5,7},{7,5},{8,10},{10,8},{9,1... | collective-permute-start | bytes 1572872 | tf_op jit(solution)/shard_map/ppermute | solution.py:25
  53.5 35.9 %collective-permute-start.1 = (f32[4,512]{1,0:T(4,128)S(1)}, f32[4,512]{1,0:T(4,128)S(1)}, u32[]{:S(2)}, u32[]{:S(2)}) collective-permute-start(f32[4,512]{1,0:T(4,128)S(1)} %copy-done.35), channel_id=1, source_target_pairs={{0,2},{2,0},{1,3},{3,1},{4,6},{6,4},{5,7},{7,5},{8,10},{10,8},{9,1... | collective-permute-start | bytes 24584 | tf_op jit(solution)/shard_map/ppermute | solution.py:25
  92.4 26.3 %collective-permute-start.10 = (bf16[2,512,512]{2,1,0:T(8,128)(2,1)}, bf16[2,512,512]{2,1,0:T(8,128)(2,1)S(1)}, u32[]{:S(2)}, u32[]{:S(2)}) collective-permute-start(bf16[2,512,512]{2,1,0:T(8,128)(2,1)} %get-tuple-element.154.refs_3_.refs_4_.refs_17_.refs_18_.refs_13_.refs_14_), channel_id=1, source_target_pairs={{0,16},{16,0},{1,17},{17,1},{2,18},{18,2},{3,19},{19,3},{4,20},{20... | collective-permute-start | bytes 3145736 | tf_op jit(solution)/shard_map/ppermute | solution.py:25
  93.9 45.8 %collective-permute-start.9 = (bf16[2,512,512]{2,1,0:T(8,128)(2,1)}, bf16[2,512,512]{2,1,0:T(8,128)(2,1)}, u32[]{:S(2)}, u32[]{:S(2)}) collective-permute-start(bf16[2,512,512]{2,1,0:T(8,128)(2,1)} %get-tuple-element.152.refs_5_.refs_6_.refs_11_.refs_12_.refs_7_.refs_8_), channel_id=1, source_target_pairs={{0,16},{16,0},{1,17},{17,1},{2,18},{18,2},{3,19},{19,3},{4,20},{20... | collective-permute-start | bytes 3145736 | tf_op jit(solution)/shard_map/ppermute | solution.py:25
  94.5 49.6 %collective-permute-start.8 = (bf16[2,512,512]{2,1,0:T(8,128)(2,1)}, bf16[2,512,512]{2,1,0:T(8,128)(2,1)S(1)}, u32[]{:S(2)}, u32[]{:S(2)}) collective-permute-start(bf16[2,512,512]{2,1,0:T(8,128)(2,1)} %get-tuple-element.152.refs_5_.refs_6_.refs_11_.refs_12_.refs_7_.refs_8_), channel_id=1, source_target_pairs={{0,8},{8,0},{1,9},{9,1},{2,10},{10,2},{3,11},{11,3},{4,12},{12,4},... | collective-permute-start | bytes 3145736 | tf_op jit(solution)/shard_map/ppermute | solution.py:25
  100.0 88.8 %collective-permute-start.11 = (bf16[4,256,512]{2,1,0:T(8,128)(2,1)}, bf16[4,256,512]{2,1,0:T(8,128)(2,1)S(1)}, u32[]{:S(2)}, u32[]{:S(2)}) collective-permute-start(bf16[4,256,512]{2,1,0:T(8,128)(2,1)} %shard_map.206.refs_4_), channel_id=1, source_target_pairs={{0,8},{8,0},{1,9},{9,1},{2,10},{10,2},{3,11},{11,3},{4,12},{12,4},... | collective-permute-start | bytes 3145736 | tf_op jit(solution)/shard_map/ppermute | solution.py:25
  145.6 43.2 %collective-permute-start.12 = (bf16[2,512,512]{2,1,0:T(8,128)(2,1)}, bf16[2,512,512]{2,1,0:T(8,128)(2,1)S(1)}, u32[]{:S(2)}, u32[]{:S(2)}) collective-permute-start(bf16[2,512,512]{2,1,0:T(8,128)(2,1)} %get-tuple-element.158.refs_5_.refs_6_.refs_19_.refs_20_.refs_15_.refs_16_), channel_id=1, source_target_pairs={{0,16},{16,0},{1,17},{17,1},{2,18},{18,2},{3,19},{19,3},{4,20},{20... | collective-permute-start | bytes 3145736 | tf_op jit(solution)/shard_map/ppermute | solution.py:25
  147.1 41.7 %collective-permute-start.13 = (bf16[2,256,512]{2,1,0:T(8,128)(2,1)S(1)}, bf16[2,256,512]{2,1,0:T(8,128)(2,1)S(1)}, u32[]{:S(2)}, u32[]{:S(2)}) collective-permute-start(bf16[2,256,512]{2,1,0:T(8,128)(2,1)S(1)} %copy-done.4), channel_id=1, source_target_pairs={{0,16},{16,0},{1,17},{17,1},{2,18},{18,2},{3,19},{19,3},{4,20},{20... | collective-permute-start | bytes 1572872 | tf_op jit(solution)/shard_map/ppermute | solution.py:25
  190.9 30.7 %collective-permute-start.14 = (bf16[4,256,512]{2,1,0:T(8,128)(2,1)}, bf16[4,256,512]{2,1,0:T(8,128)(2,1)S(1)}, u32[]{:S(2)}, u32[]{:S(2)}) collective-permute-start(bf16[4,256,512]{2,1,0:T(8,128)(2,1)} %get-tuple-element.170.refs_3_.refs_4_.refs_5_.refs_6_.refs_33_.refs_34_.refs_35_.refs_36_.refs_49_.refs_50, ...), channel_id=1, source_target_pairs={{0,16},{16,0},{1,17},{17,1},{2,18},{18,2},{3,19},{19,3},{4,20},{20... | collective-permute-start | bytes 3145736 | tf_op jit(solution)/shard_map/ppermute | solution.py:25
  223.2 25.9 %collective-permute-start.15 = (bf16[4,256,512]{2,1,0:T(8,128)(2,1)}, bf16[4,256,512]{2,1,0:T(8,128)(2,1)S(1)}, u32[]{:S(2)}, u32[]{:S(2)}) collective-permute-start(bf16[4,256,512]{2,1,0:T(8,128)(2,1)} %get-tuple-element.189), channel_id=1, source_target_pairs={{0,16},{16,0},{1,17},{17,1},{2,18},{18,2},{3,19},{19,3},{4,20},{20... | collective-permute-start | bytes 3145736 | tf_op jit(solution)/shard_map/ppermute | solution.py:25
  254.4 48.7 %collective-permute-start.16 = (bf16[4,256,512]{2,1,0:T(8,128)(2,1)}, bf16[4,256,512]{2,1,0:T(8,128)(2,1)}, u32[]{:S(2)}, u32[]{:S(2)}) collective-permute-start(bf16[4,256,512]{2,1,0:T(8,128)(2,1)} %shard_map.216.refs_8_), channel_id=1, source_target_pairs={{0,8},{8,0},{1,9},{9,1},{2,10},{10,2},{3,11},{11,3},{4,12},{12,4},... | collective-permute-start | bytes 3145736 | tf_op jit(solution)/shard_map/ppermute | solution.py:25
  258.0 45.1 %collective-permute-start.17 = (bf16[4,256,512]{2,1,0:T(8,128)(2,1)S(1)}, bf16[4,256,512]{2,1,0:T(8,128)(2,1)S(1)}, u32[]{:S(2)}, u32[]{:S(2)}) collective-permute-start(bf16[4,256,512]{2,1,0:T(8,128)(2,1)S(1)} %copy-done.20), channel_id=1, source_target_pairs={{0,16},{16,0},{1,17},{17,1},{2,18},{18,2},{3,19},{19,3},{4,20},{20... | collective-permute-start | bytes 3145736 | tf_op jit(solution)/shard_map/ppermute | solution.py:25
  259.7 45.4 %collective-permute-start.18 = (bf16[4,256,512]{2,1,0:T(8,128)(2,1)S(1)}, bf16[4,256,512]{2,1,0:T(8,128)(2,1)}, u32[]{:S(2)}, u32[]{:S(2)}) collective-permute-start(bf16[4,256,512]{2,1,0:T(8,128)(2,1)S(1)} %copy-done.18), channel_id=1, source_target_pairs={{0,16},{16,0},{1,17},{17,1},{2,18},{18,2},{3,19},{19,3},{4,20},{20... | collective-permute-start | bytes 3145736 | tf_op jit(solution)/shard_map/ppermute | solution.py:25
  309.4 63.1 %collective-permute-start.19 = (bf16[4,256,512]{2,1,0:T(8,128)(2,1)}, bf16[4,256,512]{2,1,0:T(8,128)(2,1)S(1)}, u32[]{:S(2)}, u32[]{:S(2)}) collective-permute-start(bf16[4,256,512]{2,1,0:T(8,128)(2,1)} %shard_map.220.refs_8_), channel_id=1, source_target_pairs={{0,8},{8,0},{1,9},{9,1},{2,10},{10,2},{3,11},{11,3},{4,12},{12,4},... | collective-permute-start | bytes 3145736 | tf_op jit(solution)/shard_map/ppermute | solution.py:25
  311.8 60.8 %collective-permute-start.22 = (bf16[4,256,512]{2,1,0:T(8,128)(2,1)S(1)}, bf16[4,256,512]{2,1,0:T(8,128)(2,1)S(1)}, u32[]{:S(2)}, u32[]{:S(2)}) collective-permute-start(bf16[4,256,512]{2,1,0:T(8,128)(2,1)S(1)} %copy-done.19), channel_id=1, source_target_pairs={{0,16},{16,0},{1,17},{17,1},{2,18},{18,2},{3,19},{19,3},{4,20},{20... | collective-permute-start | bytes 3145736 | tf_op jit(solution)/shard_map/ppermute | solution.py:25
  313.4 59.0 %collective-permute-start.23 = (f32[1,896]{1,0:T(1,128)S(1)}, f32[1,896]{1,0:T(1,128)S(1)}, u32[]{:S(2)}, u32[]{:S(2)}) collective-permute-start(f32[1,896]{1,0:T(1,128)S(1)} %copy-done.42), channel_id=1, source_target_pairs={{0,8},{8,0},{1,9},{9,1},{2,10},{10,2},{3,11},{11,3},{4,12},{12,4},... | collective-permute-start | bytes 10760 | tf_op jit(solution)/shard_map/ppermute | solution.py:25
  314.0 58.5 %collective-permute-start.20 = (bf16[2,256,512]{2,1,0:T(8,128)(2,1)}, bf16[2,256,512]{2,1,0:T(8,128)(2,1)S(1)}, u32[]{:S(2)}, u32[]{:S(2)}) collective-permute-start(bf16[2,256,512]{2,1,0:T(8,128)(2,1)} %get-tuple-element.215), channel_id=1, source_target_pairs={{0,16},{16,0},{1,17},{17,1},{2,18},{18,2},{3,19},{19,3},{4,20},{20... | collective-permute-start | bytes 1572872 | tf_op jit(solution)/shard_map/ppermute | solution.py:25
  314.4 58.1 %collective-permute-start.21 = (bf16[2,256,512]{2,1,0:T(8,128)(2,1)}, bf16[2,256,512]{2,1,0:T(8,128)(2,1)}, u32[]{:S(2)}, u32[]{:S(2)}) collective-permute-start(bf16[2,256,512]{2,1,0:T(8,128)(2,1)} %get-tuple-element.216), channel_id=1, source_target_pairs={{0,16},{16,0},{1,17},{17,1},{2,18},{18,2},{3,19},{19,3},{4,20},{20... | collective-permute-start | bytes 1572872 | tf_op jit(solution)/shard_map/ppermute | solution.py:25
  374.6 56.8 %collective-permute-start.28 = (bf16[2,2,1024,512]{3,2,1,0:T(8,128)(2,1)}, bf16[2,2,1024,512]{3,2,1,0:T(8,128)(2,1)}, u32[]{:S(2)}, u32[]{:S(2)}) collective-permute-start(bf16[2,2,1024,512]{3,2,1,0:T(8,128)(2,1)} %get-tuple-element.235), channel_id=1, source_target_pairs={{0,1},{1,0},{2,3},{3,2},{4,5},{5,4},{6,7},{7,6},{8,9},{9,8},{10,11... | collective-permute-start | bytes 12582920 | tf_op jit(solution)/shard_map/ppermute | solution.py:25
  383.3 48.0 %collective-permute-start.24 = (bf16[4,256,512]{2,1,0:T(8,128)(2,1)}, bf16[4,256,512]{2,1,0:T(8,128)(2,1)S(1)}, u32[]{:S(2)}, u32[]{:S(2)}) collective-permute-start(bf16[4,256,512]{2,1,0:T(8,128)(2,1)} %shard_map.225.refs_7_), channel_id=1, source_target_pairs={{0,8},{8,0},{1,9},{9,1},{2,10},{10,2},{3,11},{11,3},{4,12},{12,4},... | collective-permute-start | bytes 3145736 | tf_op jit(solution)/shard_map/ppermute | solution.py:25
  385.7 45.6 %collective-permute-start.27 = (bf16[2,512,512]{2,1,0:T(8,128)(2,1)}, bf16[2,512,512]{2,1,0:T(8,128)(2,1)S(1)}, u32[]{:S(2)}, u32[]{:S(2)}) collective-permute-start(bf16[2,512,512]{2,1,0:T(8,128)(2,1)} %get-tuple-element.234), channel_id=1, source_target_pairs={{0,1},{1,0},{2,3},{3,2},{4,5},{5,4},{6,7},{7,6},{8,9},{9,8},{10,11... | collective-permute-start | bytes 3145736 | tf_op jit(solution)/shard_map/ppermute | solution.py:25
  433.2 43.6 %collective-permute-start.29 = (bf16[2,2,1024,512]{3,2,1,0:T(8,128)(2,1)}, bf16[2,2,1024,512]{3,2,1,0:T(8,128)(2,1)}, u32[]{:S(2)}, u32[]{:S(2)}) collective-permute-start(bf16[2,2,1024,512]{3,2,1,0:T(8,128)(2,1)} %get-tuple-element.246), channel_id=1, source_target_pairs={{0,1},{1,0},{2,3},{3,2},{4,5},{5,4},{6,7},{7,6},{8,9},{9,8},{10,11... | collective-permute-start | bytes 12582920 | tf_op jit(solution)/shard_map/ppermute | solution.py:25
  439.9 36.9 %collective-permute-start.31 = (bf16[6,256,512]{2,1,0:T(8,128)(2,1)}, bf16[6,256,512]{2,1,0:T(8,128)(2,1)S(1)}, u32[]{:S(2)}, u32[]{:S(2)}) collective-permute-start(bf16[6,256,512]{2,1,0:T(8,128)(2,1)} %get-tuple-element.248), channel_id=1, source_target_pairs={{0,2},{2,0},{1,3},{3,1},{4,6},{6,4},{5,7},{7,5},{8,10},{10,8},{9,1... | collective-permute-start | bytes 4718600 | tf_op jit(solution)/shard_map/ppermute | solution.py:25
  490.6 47.5 %collective-permute-start.35 = (bf16[4,512,512]{2,1,0:T(8,128)(2,1)}, bf16[4,512,512]{2,1,0:T(8,128)(2,1)}, u32[]{:S(2)}, u32[]{:S(2)}) collective-permute-start(bf16[4,512,512]{2,1,0:T(8,128)(2,1)} %shard_map.233.refs_0_.refs_2_), channel_id=1, source_target_pairs={{0,16},{16,0},{1,17},{17,1},{2,18},{18,2},{3,19},{19,3},{4,20},{20... | collective-permute-start | bytes 6291464 | tf_op jit(solution)/shard_map/ppermute | solution.py:25
  491.2 47.1 %collective-permute-start.33 = (bf16[8,256,512]{2,1,0:T(8,128)(2,1)}, bf16[8,256,512]{2,1,0:T(8,128)(2,1)S(1)}, u32[]{:S(2)}, u32[]{:S(2)}) collective-permute-start(bf16[8,256,512]{2,1,0:T(8,128)(2,1)} %get-tuple-element.258.refs_4_), channel_id=1, source_target_pairs={{0,2},{2,0},{1,3},{3,1},{4,6},{6,4},{5,7},{7,5},{8,10},{10,8},{9,1... | collective-permute-start | bytes 6291464 | tf_op jit(solution)/shard_map/ppermute | solution.py:25
  492.3 45.8 %collective-permute-start.34 = (bf16[6,256,512]{2,1,0:T(8,128)(2,1)}, bf16[6,256,512]{2,1,0:T(8,128)(2,1)}, u32[]{:S(2)}, u32[]{:S(2)}) collective-permute-start(bf16[6,256,512]{2,1,0:T(8,128)(2,1)} %get-tuple-element.260), channel_id=1, source_target_pairs={{0,4},{4,0},{1,5},{5,1},{2,6},{6,2},{3,7},{7,3},{8,12},{12,8},{9,1... | collective-permute-start | bytes 4718600 | tf_op jit(solution)/shard_map/ppermute | solution.py:25
  495.1 43.0 %collective-permute-start.36 = (f32[1,896]{1,0:T(1,128)S(1)}, f32[1,896]{1,0:T(1,128)S(1)}, u32[]{:S(2)}, u32[]{:S(2)}) collective-permute-start(f32[1,896]{1,0:T(1,128)S(1)} %constant_dynamic-update-slice_fusion.2.refs_1_), channel_id=1, source_target_pairs={{0,16},{16,0},{1,17},{17,1},{2,18},{18,2},{3,19},{19,3},{4,20},{20... | collective-permute-start | bytes 10760 | tf_op jit(solution)/shard_map/ppermute | solution.py:25
  561.6 41.6 %collective-permute-start.44 = (bf16[4,256,512]{2,1,0:T(8,128)(2,1)}, bf16[4,256,512]{2,1,0:T(8,128)(2,1)}, u32[]{:S(2)}, u32[]{:S(2)}) collective-permute-start(bf16[4,256,512]{2,1,0:T(8,128)(2,1)} %shard_map.236.refs_4_.refs_2_), channel_id=1, source_target_pairs={{0,16},{16,0},{1,17},{17,1},{2,18},{18,2},{3,19},{19,3},{4,20},{20... | collective-permute-start | bytes 3145736 | tf_op jit(solution)/shard_map/ppermute | solution.py:25
  (73 other events, 583.7 us)
Sparse Core Ops, SparseCore 0:
  9.6 71.6 all-gather.4
  82.9 78.2 all-gather.6

commit v3 on v2

--- a/solution.py
+++ b/solution.py
@@ -132,61 +132,25 @@
     )
 
 
-def stack(items, after=()):
-    rows = items[0][3]
-
-    def body(*refs):
-        out = refs[-1]
-        for at, ((_, lead, first, _), ref) in enumerate(zip(items, refs[:-1], strict=True)):
-            if isinstance(lead, slice):
-                size = ref.shape[1]
-                for k in range(lead.start, lead.stop):
-                    out[at, size * (k - lead.start) : size * (k - lead.start + 1), :] = ref[k]
-            else:
-                out[at] = ref[lead, first : first + rows, :]
-
-    return call(
-        body,
-        (1,),
-        [(array, whole(*array.shape)) for array, _, _, _ in items],
-        [(shape(len(items), rows, 512), whole(len(items), rows, 512))],
-        after=after,
-    )[0]
-
-
 def split_first(far2, near3, own, near1, after=()):
-    def body(far2, near3, own, near1, to_y, att_y, z_mlp):
+    def body(far2, near3, own, near1, to_y, att_y, z_mlp, z_att):
         for at, ref in enumerate((far2, near3)):
             to_y[at] = ref[:512, :]
             att_y[at] = ref[512:, :]
         for at, ref in enumerate((own, near1)):
             z_mlp[at] = ref[0, :512, :]
+            z_att[at] = ref[0, 512:, :]
 
     flat, deep = whole(768, 512), whole(1, 768, 512)
     mlp_out = (shape(2, 512, 512), whole(2, 512, 512))
+    att_out = (shape(2, 256, 512), whole(2, 256, 512))
     return call(
         body,
         (1,),
         [(far2, flat), (near3, flat), (own, deep), (near1, deep)],
-        [mlp_out, (shape(2, 256, 512), whole(2, 256, 512)), mlp_out],
-        after=after,
-    )
-
-
-def stack_att(own, near1, far, after=()):
-    def body(own, near1, far, out):
-        for at, ref in enumerate((own, near1)):
-            out[at] = ref[0, 512:, :]
-            out[2 + at] = far[at]
-
-    deep = whole(1, 768, 512)
-    return call(
-        body,
-        (1,),
-        [(own, deep), (near1, deep), (far, whole(2, 256, 512))],
-        [(shape(4, 256, 512), whole(4, 256, 512))],
-        after=after,
-    )[0]
+        [mlp_out, att_out, mlp_out, att_out],
+        after=after,
+    )
 
 
 def gate(after, carry):
@@ -210,54 +174,58 @@
     )
 
 
-def unpack_mlp_kernel(place, sx, first, second, fc1_out, fc2_out):
-    x = sx[0]
-    a, b = first[0].astype(F32), second[0].astype(F32)
-    low, high = jnp.where(x == 0, a, b), jnp.where(x == 0, b, a)
-    fc1_out[:256, :] = low[256:]
-    fc1_out[256:, :] = high[256:]
-    fc2_out[:, :256] = low[:256].T
-    fc2_out[:, 256:] = high[:256].T
-
-
-def unpack_mlp(place, sx, first, second, after=()):
-    block = pl.BlockSpec((1, 512, 512), lambda i, o, x: (o[i], 0, 0))
-    return call(
-        unpack_mlp_kernel,
+def unpack(place, sx, pieces, select, outputs, store, after=()):
+    def body(place, sx, *refs):
+        for r in range(4):
+
+            @pl.when(place[pl.program_id(0)] == r)
+            def _(r=r):
+                a = select(refs[r // 2], r % 2).astype(F32)
+                b = select(refs[2 + r // 2], r % 2).astype(F32)
+                store(jnp.where(sx[0] == 0, a, b), jnp.where(sx[0] == 0, b, a), *refs[4:])
+
+    return call(
+        body,
         (4,),
-        [(first, block), (second, block)],
-        [
-            (shape(2048, 512, dtype=F32), pl.BlockSpec((512, 512), lambda i, o, x: (i, 0))),
-            (shape(512, 2048, dtype=F32), pl.BlockSpec((512, 512), lambda i, o, x: (0, i))),
-        ],
+        [(value, whole(*value.shape)) for value in pieces],
+        outputs,
         prefetch=(place, sx),
         after=after,
     )
 
 
-def unpack_att_kernel(place, sx, first, second, qkv_out, dense_out):
-    x = sx[0]
-    a, b = first[0].astype(F32), second[0].astype(F32)
-    low, high = jnp.where(x == 0, a, b), jnp.where(x == 0, b, a)
-    for part in range(3):
-        qkv_out[part, :64, :] = low[64 * part : 64 * part + 64]
-        qkv_out[part, 64:, :] = high[64 * part : 64 * part + 64]
-    dense_out[...] = jnp.concatenate([low[192:], high[192:]], axis=0).T
-
-
-def unpack_att(place, sx, first, second, after=()):
-    block = pl.BlockSpec((1, 256, 512), lambda i, o, x: (o[i], 0, 0))
-    return call(
-        unpack_att_kernel,
-        (4,),
-        [(first, block), (second, block)],
-        [
-            (shape(3, 512, 512, dtype=F32), pl.BlockSpec((3, 128, 512), lambda i, o, x: (0, i, 0))),
-            (shape(512, 512, dtype=F32), pl.BlockSpec((512, 128), lambda i, o, x: (0, i))),
-        ],
-        prefetch=(place, sx),
-        after=after,
-    )
+def unpack_fc2(place, sx, pieces, after=()):
+    def store(low, high, out):
+        out[:, :256] = low.T
+        out[:, 256:] = high.T
+
+    block = pl.BlockSpec((512, 512), lambda i, o, x: (0, i))
+    out = [(shape(512, 2048, dtype=F32), block)]
+    return unpack(place, sx, pieces, lambda ref, k: ref[2 * k], out, store, after)[0]
+
+
+def unpack_fc1(place, sx, pieces, after=()):
+    def store(low, high, out):
+        out[:256, :] = low
+        out[256:, :] = high
+
+    block = pl.BlockSpec((512, 512), lambda i, o, x: (i, 0))
+    out = [(shape(2048, 512, dtype=F32), block)]
+    return unpack(place, sx, pieces, lambda ref, k: ref[2 * k + 1], out, store, after)[0]
+
+
+def unpack_att(place, sx, pieces, after=()):
+    def store(low, high, qkv_out, dense_out):
+        for part in range(3):
+            qkv_out[part, :64, :] = low[64 * part : 64 * part + 64]
+            qkv_out[part, 64:, :] = high[64 * part : 64 * part + 64]
+        dense_out[...] = jnp.concatenate([low[192:], high[192:]], axis=0).T
+
+    outputs = [
+        (shape(3, 512, 512, dtype=F32), pl.BlockSpec((3, 128, 512), lambda i, o, x: (0, i, 0))),
+        (shape(512, 512, dtype=F32), pl.BlockSpec((512, 128), lambda i, o, x: (0, i))),
+    ]
+    return unpack(place, sx, pieces, lambda ref, k: ref[k], outputs, store, after)
 
 
 def norm_kernel(place, xs, scale, normed, stats):
@@ -388,30 +356,36 @@
 
 
 def heads_kernel(place, n, c, *refs):
-    weights, (bias, tables, q_out, k_out, v0_out, v1_out, d_out, joined) = refs[:8], refs[8:]
+    weights, refs = refs[:16], refs[16:]
+    bias, tables, *outs, joined = refs
 
     @pl.when(pl.program_id(0) == 0)
     def _():
-        for s in range(2):
-            for r in range(4):
-                for part in range(4):
-                    row = 128 * part + 64 * s
-                    joined[row : row + 64, 512 * r : 512 * r + 512] = weights[4 * s + r][
-                        0, 64 * part : 64 * part + 64, :
-                    ]
-
-    pre = nt(n[...], joined[:384]) + bias[...]
-    q_out[...] = (rotated(pre[:, :128], tables, 1.0) * SCALE).astype(BF)
-    k_out[...] = rotated(pre[:, 128:256], tables, 1.0).astype(BF)
-    value = pre[:, 256:].astype(BF)
-    lane = lax.broadcasted_iota(jnp.int32, value.shape, 1)
-    one = jnp.ones_like(value)
-    v0_out[...] = jnp.where(lane < HEAD_DIM, value, one)
-    v1_out[...] = jnp.where(lane < HEAD_DIM, one, value)
-    back = jnp.zeros((TILE, 128), F32)
+        for block in range(2):
+            for s in range(2):
+                for r in range(4):
+                    for part in range(4):
+                        row = 384 * block + 128 * part if part < 3 else 768 + 128 * block
+                        row += 64 * s
+                        joined[row : row + 64, 512 * r : 512 * r + 512] = weights[
+                            8 * block + 4 * s + r
+                        ][0, 64 * part : 64 * part + 64, :]
+
+    pre = nt(n[...], joined[:768]) + bias[...]
+    back = jnp.zeros((TILE, 256), F32)
     for r in range(4):
-        back += nt(c[0, place[r]], joined[384:, 512 * r : 512 * r + 512])
-    d_out[...] = back.astype(BF)
+        back += nt(c[0, place[r]], joined[768:, 512 * r : 512 * r + 512])
+    lane = lax.broadcasted_iota(jnp.int32, (TILE, 128), 1)
+    one = jnp.ones((TILE, 128), BF)
+    for block in range(2):
+        q_out, k_out, v0_out, v1_out, d_out = outs[5 * block : 5 * block + 5]
+        mine = pre[:, 384 * block : 384 * block + 384]
+        q_out[...] = (rotated(mine[:, :128], tables, 1.0) * SCALE).astype(BF)
+        k_out[...] = rotated(mine[:, 128:256], tables, 1.0).astype(BF)
+        value = mine[:, 256:].astype(BF)
+        v0_out[...] = jnp.where(lane < HEAD_DIM, value, one)
+        v1_out[...] = jnp.where(lane < HEAD_DIM, one, value)
+        d_out[...] = back[:, 128 * block : 128 * block + 128].astype(BF)
 
 
 def heads(place, normed, cot, weights, bias, tables, after=()):
@@ -422,11 +396,11 @@
         token_inputs(normed, cot)
         + [piece(*weight) for weight in weights]
         + [
-            (bias, whole(1, 384)),
+            (bias, whole(1, 768)),
             (tables, pl.BlockSpec((3, TILE, 128), lambda i, *_: (0, i, 0))),
         ],
-        [(shape(SEQ, 128), head)] * 5,
-        [pltpu.VMEM((512, MODEL_WIDTH), BF)],
+        [(shape(SEQ, 128), head)] * 10,
+        [pltpu.VMEM((1024, MODEL_WIDTH), BF)],
         prefetch=(place,),
         after=after,
     )
@@ -436,132 +410,134 @@
 BLOCKS = SEQ // BLOCK
 
 
-def attend_kernel(
-    low, q, k, v0, v1, d, start, tables, o_out, dq_out, dk_out, dv_out, sums, scores, probs, dk_acc, dv_acc
-):
+def attend_kernel(low, *refs):
+    ins, (start, tables), refs = refs[:10], refs[10:12], refs[12:]
+    outs, refs = refs[:10], refs[10:]
+    scores, probs, dk_acc, dv_acc, peak_acc, o_acc, dq_acc = refs
     i = pl.program_id(0)
 
     @pl.when(i == 0)
     def _():
         dk_acc[...] = jnp.zeros_like(dk_acc)
         dv_acc[...] = jnp.zeros_like(dv_acc)
-        sums[...] = jnp.zeros_like(sums)
+        for block in range(2):
+            outs[5 * block + 4][...] = jnp.zeros_like(outs[5 * block + 4])
 
     lane = lax.broadcasted_iota(jnp.int32, (BLOCK, 128), 1)
     masks = (lane < HEAD_DIM, lane >= HEAD_DIM)
     zero = jnp.zeros((BLOCK, 128), BF)
-    queries = [jnp.where(m, q[...], zero) for m in masks]
-    values = (v0, v1)
+    queries = [jnp.where(masks[h % 2], ins[5 * (h // 2)][...], zero) for h in range(4)]
+    keys = [ins[5 * (h // 2) + 1] for h in range(4)]
+    values = [ins[5 * (h // 2) + 2 + h % 2] for h in range(4)]
     col = lax.broadcasted_iota(jnp.int32, (BLOCK, BLOCK), 1)
     row = lax.broadcasted_iota(jnp.int32, (BLOCK, BLOCK), 0) + i * BLOCK
     begin = start[:, :1]
 
-    def at(j):
-        return pl.ds(pl.multiple_of(j * BLOCK, BLOCK), BLOCK)
-
-    def score(j, peaks):
-        keys = k[at(j), :]
+    def each(step):
+        for j in range(BLOCKS):
+
+            @pl.when((j >= low[i]) & (j <= i))
+            def _(j=j):
+                step(j, slice(j * BLOCK, j * BLOCK + BLOCK))
+
+    peak_acc[...] = jnp.full_like(peak_acc, MASKED)
+    o_acc[...] = jnp.zeros_like(o_acc)
+    dq_acc[...] = jnp.zeros_like(dq_acc)
+
+    def score(j, at):
         here = col + j * BLOCK
         allowed = (here >= begin) & (here <= row)
-        new = []
-        for h in range(2):
-            s = jnp.where(allowed, nt(queries[h], keys), MASKED)
+        for h in range(4):
+            s = jnp.where(allowed, nt(queries[h], keys[h][at, :]), MASKED)
             scores[h, j] = s
-            peak = peaks[h]
+            peak = peak_acc[h]
             for lanes in range(0, BLOCK, 128):
                 peak = jnp.maximum(peak, s[:, lanes : lanes + 128])
-            new.append(peak)
-        return tuple(new)
-
-    floor = jnp.full((BLOCK, 128), MASKED, F32)
-    peaks = lax.fori_loop(low[i], i + 1, score, (floor, floor))
-    peaks = [jnp.max(p, axis=1, keepdims=True) for p in peaks]
-
-    def weigh(j, outs):
-        new = []
-        for h in range(2):
+            peak_acc[h] = peak
+
+    each(score)
+    peaks = [jnp.max(peak_acc[h], axis=1, keepdims=True) for h in range(4)]
+
+    def weigh(j, at):
+        for h in range(4):
             p = jnp.exp(scores[h, j] - peaks[h]).astype(BF)
             probs[h, j] = p
-            new.append(outs[h] + nn(p, values[h][at(j), :]))
-        return tuple(new)
-
-    blank = jnp.zeros((BLOCK, 128), F32)
-    outs = lax.fori_loop(low[i], i + 1, weigh, (blank, blank))
-    inverse = [1.0 / outs[0][:, HEAD_DIM : HEAD_DIM + 1], 1.0 / outs[1][:, :1]]
-    outs = [outs[h] * inverse[h] for h in range(2)]
-    o_out[...] = jnp.where(masks[0], outs[0], outs[1]).astype(BF)
-
+            o_acc[h] += nn(p, values[h][at, :])
+
+    each(weigh)
     grads, shifted = [], []
-    for h in range(2):
-        grad = jnp.where(masks[h], d[...].astype(F32) * inverse[h], 0.0).astype(BF)
-        wide = grad.astype(F32)
-        delta = jnp.sum(wide * outs[h], axis=1, keepdims=True)
-        coarse = delta.astype(BF).astype(F32)
-        first = HEAD_DIM * (1 - h)
-        wide = jnp.where(lane == first, -coarse, wide)
-        shifted.append(jnp.where(lane == first + 1, coarse - delta, wide).astype(BF))
-        grads.append(grad)
-
-    def back(j, carry):
-        keys = k[at(j), :]
-        new = []
-        dk, dv = dk_acc[at(j), :], dv_acc[at(j), :]
+    for block in range(2):
+        scaled = []
         for h in range(2):
+            out = o_acc[2 * block + h]
+            first = HEAD_DIM * (1 - h)
+            inverse = 1.0 / out[:, first : first + 1]
+            out = out * inverse
+            grad = jnp.where(masks[h], ins[5 * block + 4][...].astype(F32) * inverse, 0.0).astype(BF)
+            wide = grad.astype(F32)
+            delta = jnp.sum(wide * out, axis=1, keepdims=True)
+            coarse = delta.astype(BF).astype(F32)
+            wide = jnp.where(lane == first, -coarse, wide)
+            shifted.append(jnp.where(lane == first + 1, coarse - delta, wide).astype(BF))
+            grads.append(grad)
+            scaled.append(out)
+        outs[5 * block][...] = jnp.where(masks[0], *scaled).astype(BF)
+
+    def back(j, at):
+        for h in range(4):
             p = probs[h, j]
-            d_scores = (p.astype(F32) * nt(shifted[h], values[h][at(j), :])).astype(BF)
-            new.append(carry[h] + nn(d_scores, keys))
-            dk += tn(d_scores, queries[h])
-            dv += tn(p, grads[h])
-        dk_acc[at(j), :] = dk
-        dv_acc[at(j), :] = dv
-        return tuple(new)
-
-    dq = lax.fori_loop(low[i], i + 1, back, (blank, blank))
-    dq = jnp.where(masks[0], dq[0], dq[1]) * SCALE
-    dq = rotated(dq, [tables[t, at(i), :] for t in range(3)], -1.0)
-    dq_out[...] = dq.astype(BF)
-    sums[0:1, :] += jnp.sum(dq, axis=0, keepdims=True)
+            d_scores = (p.astype(F32) * nt(shifted[h], values[h][at, :])).astype(BF)
+            dq_acc[h] += nn(d_scores, keys[h][at, :])
+            dk_acc[h // 2, at, :] += tn(d_scores, queries[h])
+            dv_acc[h // 2, at, :] += tn(p, grads[h])
+
+    each(back)
+    rows = pl.ds(pl.multiple_of(i * BLOCK, BLOCK), BLOCK)
+    for block in range(2):
+        dq = jnp.where(masks[0], dq_acc[2 * block], dq_acc[2 * block + 1]) * SCALE
+        dq = rotated(dq, [tables[t, rows, :] for t in range(3)], -1.0)
+        outs[5 * block + 1][...] = dq.astype(BF)
+        outs[5 * block + 4][0:1, :] += jnp.sum(dq, axis=0, keepdims=True)
 
     @pl.when(i == BLOCKS - 1)
     def _():
-        for j in range(8):
-            rows = slice(j * 256, j * 256 + 256)
-            dk = rotated(dk_acc[rows], [tables[t, rows] for t in range(3)], -1.0)
-            dv = dv_acc[rows]
-            dk_out[rows, :] = dk.astype(BF)
-            dv_out[rows, :] = dv.astype(BF)
-            sums[1:2, :] += jnp.sum(dk, axis=0, keepdims=True)
-            sums[2:3, :] += jnp.sum(dv, axis=0, keepdims=True)
-
-
-def attend(low, q, k, v0, v1, d, start, tables, after=()):
+        for block in range(2):
+            _, _, dk_out, dv_out, sums = outs[5 * block : 5 * block + 5]
+            for j in range(8):
+                rows = slice(j * 256, j * 256 + 256)
+                dk = rotated(dk_acc[block, rows], [tables[t, rows] for t in range(3)], -1.0)
+                dv = dv_acc[block, rows]
+                dk_out[rows, :] = dk.astype(BF)
+                dv_out[rows, :] = dv.astype(BF)
+                sums[1:2, :] += jnp.sum(dk, axis=0, keepdims=True)
+                sums[2:3, :] += jnp.sum(dv, axis=0, keepdims=True)
+
+
+def attend(low, heads, start, tables, after=()):
     tile = pl.BlockSpec((BLOCK, 128), lambda i, o: (i, 0))
     full = whole(SEQ, 128)
     head = shape(SEQ, 128)
     return call(
         attend_kernel,
         (BLOCKS,),
-        [
-            (q, tile),
-            (k, full),
-            (v0, full),
-            (v1, full),
-            (d, tile),
-            (start, tile),
-            (tables, whole(3, SEQ, 128)),
-        ],
+        [(value, (tile, full, full, full, tile)[at % 5]) for at, value in enumerate(heads)]
+        + [(start, tile), (tables, whole(3, SEQ, 128))],
         [
             (head, tile),
             (head, tile),
             (head, full),
             (head, full),
             (shape(8, 128, dtype=F32), whole(8, 128)),
-        ],
+        ]
+        * 2,
         [
-            pltpu.VMEM((2, BLOCKS, BLOCK, BLOCK), F32),
-            pltpu.VMEM((2, BLOCKS, BLOCK, BLOCK), BF),
-            pltpu.VMEM((SEQ, 128), F32),
-            pltpu.VMEM((SEQ, 128), F32),
+            pltpu.VMEM((4, BLOCKS, BLOCK, BLOCK), F32),
+            pltpu.VMEM((4, BLOCKS, BLOCK, BLOCK), BF),
+            pltpu.VMEM((2, SEQ, 128), F32),
+            pltpu.VMEM((2, SEQ, 128), F32),
+            pltpu.VMEM((4, BLOCK, 128), F32),
+            pltpu.VMEM((4, BLOCK, 128), F32),
+            pltpu.VMEM((4, BLOCK, 128), F32),
         ],
         prefetch=(low,),
         after=after,
@@ -669,7 +645,6 @@
 
 
 def grad_inputs(values):
-    block = pl.BlockSpec((1, 256, 512), lambda i: (i, 0, 0))
     inputs, reads = [], []
     for value in values:
         at = len(inputs)
@@ -677,8 +652,8 @@
             inputs += [(one, whole(2, 256, 512)) for one in value]
             reads.append(lambda refs, step, at=at: refs[at + step // 2][step % 2])
         else:
-            inputs.append((value, block))
-            reads.append(lambda refs, step, at=at: refs[at][0])
+            inputs.append((value, whole(4, 256, 512)))
+            reads.append(lambda refs, step, at=at: refs[at][step])
     return inputs, reads
 
 
@@ -687,13 +662,11 @@
 
     def body(*refs):
         for step in range(4):
-
-            @pl.when(pl.program_id(0) == step)
-            def _(step=step):
-                refs[-1][0] = added([read(refs, step) for read in reads])
-
-    block = pl.BlockSpec((1, 256, 512), lambda i: (i, 0, 0))
-    return call(body, (4,), inputs, [(shape(4, 256, 512), block)], after=after)
+            refs[-1][step] = added([read(refs, step) for read in reads])
+
+    return call(
+        body, (1,), inputs, [(shape(4, 256, 512), whole(4, 256, 512))], after=after
+    )
 
 
 def total_grad(groups, after=()):
@@ -707,103 +680,100 @@
     def body(*refs):
         near, same = refs[-2:]
         for step in range(4):
-
-            @pl.when(pl.program_id(0) == step)
-            def _(step=step):
-                out = same if step < 2 else near
-                for g, (at, size, read) in enumerate(reads):
-                    mine = refs[at : at + size]
-                    out[step % 2, 256 * g : 256 * g + 256, :] = added([one(mine, step) for one in read])
+            out = same if step < 2 else near
+            for g, (at, size, read) in enumerate(reads):
+                mine = refs[at : at + size]
+                out[step % 2, 256 * g : 256 * g + 256, :] = added([one(mine, step) for one in read])
 
     out = (shape(2, rows, 512), whole(2, rows, 512))
-    return call(body, (4,), inputs, [out, out], after=after)
+    return call(body, (1,), inputs, [out, out], after=after)
 
 
 def quarters(value):
     return [value[256 * k : 256 * k + 256, :] for k in range(value.shape[0] // 256)]
 
 
-def received(same, near, to_z, to_y, own, for_y, for_z, at=0):
+def received(same, near, far_out, own, for_y, for_z):
     own[...] = added([same[0, 0], near[0, 0]])
     for_z[...] = added([same[0, 1], near[0, 1]])
     for_y[...] = added([same[1, 0], near[1, 0]])
     far = quarters(added([same[1, 1], near[1, 1]]))
-    for k in range(2):
-        to_z[at + k] = far[k]
-        to_y[at + k] = far[2 + k]
-
-
-def passed_on(for_y, from_z, for_z, from_y, to_y, to_z, at=0):
-    for k in range(4):
-        rows = slice(256 * k, 256 * k + 256)
-        to_y[k] = added([for_y[rows, :], from_z[at + k]]) if k < 2 else for_y[rows, :]
-        to_z[k] = added([for_z[rows, :], from_y[at + k - 2]]) if k >= 2 else for_z[rows, :]
+    for value, (ref, at) in zip(far, far_out, strict=True):
+        ref[at] = value
 
 
 def blocks(count):
     return (shape(count, 256, 512), whole(count, 256, 512))
 
 
+FLAT = (shape(HALF, 512), whole(HALF, 512))
+
+
 def scatter_first(same, near, grad_same, grad_near, after=()):
-    def body(same, near, grad_same, grad_near, to_z, to_y, own, for_y, for_z):
-        received(same, near, to_z, to_y, own, for_y, for_z)
-        for at, ref in enumerate((grad_same, grad_near)):
-            to_y[2 + 2 * at] = ref[1, :256, :]
-            to_y[3 + 2 * at] = ref[1, 256:, :]
+    def body(same, near, grad_same, grad_near, to_z, to_y, to_x, own, for_y, for_z):
+        received(same, near, [(to_z, k) for k in range(4)], own, for_y, for_z)
+        for out, at in ((to_x, 0), (to_y, 1)):
+            for k, ref in enumerate((grad_same, grad_near)):
+                out[2 * k] = ref[at, :256, :]
+                out[2 * k + 1] = ref[at, 256:, :]
 
     both, pair = whole(2, 2, HALF, 512), whole(2, 512, 512)
-    full = (shape(HALF, 512), whole(HALF, 512))
     return call(
         body,
         (1,),
         [(same, both), (near, both), (grad_same, pair), (grad_near, pair)],
-        [blocks(2), blocks(6), full, full, full],
-        after=after,
-    )
-
-
-def scatter_both(for_y, from_z, for_z, from_y, same, near, grad_same, grad_near, after=()):
-    def body(for_y, from_z, for_z, from_y, same, near, grad_same, grad_near, to_z, to_y, *kept):
-        passed_on(for_y, from_z, for_z, from_y, to_y, to_z)
-        received(same, near, to_z, to_y, *kept, at=4)
-        to_y[6] = grad_same[1]
-        to_y[7] = grad_near[1]
-
-    both, pair = whole(2, 2, HALF, 512), whole(2, 256, 512)
-    flat, full = whole(HALF, 512), (shape(HALF, 512), whole(HALF, 512))
+        [blocks(4)] * 3 + [FLAT] * 3,
+        after=after,
+    )
+
+
+def scatter_second(for_y, from_z, after=()):
+    def body(for_y, from_z, to_y):
+        for k in range(4):
+            rows = slice(256 * k, 256 * k + 256)
+            to_y[rows, :] = added([for_y[rows, :], from_z[k]])
+
     return call(
         body,
         (1,),
-        [
-            (for_y, flat),
-            (from_z, pair),
-            (for_z, flat),
-            (from_y, whole(6, 256, 512)),
-            (same, both),
-            (near, both),
-            (grad_same, pair),
-            (grad_near, pair),
-        ],
-        [blocks(6), blocks(8), full, full, full],
-        after=after,
-    )
-
-
-def scatter_last(for_y, from_z, for_z, from_y, after=()):
-    def body(for_y, from_z, for_z, from_y, to_z, to_y):
-        passed_on(for_y, from_z, for_z, from_y, to_y, to_z, at=4)
-
-    flat = whole(HALF, 512)
+        [(for_y, FLAT[1]), (from_z, whole(4, 256, 512))],
+        [FLAT],
+        after=after,
+    )[0]
+
+
+def scatter_third(same, near, grad_same, grad_near, after=()):
+    def body(same, near, grad_same, grad_near, to_z, to_y, to_x, *kept):
+        received(same, near, [(to_z, 0), (to_z, 1), (to_z, 2), (to_y, 0)], *kept)
+        for k, ref in enumerate((grad_same, grad_near)):
+            to_x[k] = ref[0]
+            to_y[1 + k] = ref[1]
+
+    both, pair = whole(2, 2, HALF, 512), whole(2, 256, 512)
     return call(
         body,
         (1,),
-        [
-            (for_y, flat),
-            (from_z, whole(6, 256, 512)),
-            (for_z, flat),
-            (from_y, whole(8, 256, 512)),
-        ],
-        [blocks(4), blocks(4)],
+        [(same, both), (near, both), (grad_same, pair), (grad_near, pair)],
+        [blocks(3), blocks(3), blocks(2)] + [FLAT] * 3,
+        after=after,
+    )
+
+
+def scatter_last(for_y, from_z, for_z, from_y, after=()):
+    def body(for_y, from_z, for_z, from_y, to_z, to_y, kept):
+        for k in range(4):
+            rows = slice(256 * k, 256 * k + 256)
+            to_y[rows, :] = added([for_y[rows, :], from_z[k]]) if k < 3 else for_y[rows, :]
+            to_z[rows, :] = for_z[rows, :] if k < 3 else added([for_z[rows, :], from_y[0]])
+        for k in range(2):
+            kept[k] = from_y[1 + k]
+
+    three = whole(3, 256, 512)
+    return call(
+        body,
+        (1,),
+        [(for_y, FLAT[1]), (from_z, three), (for_z, FLAT[1]), (from_y, three)],
+        [FLAT, FLAT, blocks(2)],
         after=after,
     )
 
@@ -845,7 +815,6 @@
     heads_bias = jnp.where(x == 0, heads_bias, heads_bias[:, ::-1])
     units_bias = jnp.where(x == 0, units_bias, units_bias[::-1])
     own_bias = jnp.concatenate([heads_bias.reshape(1, 384), units_bias.reshape(1, 512)], axis=1)
-    other_bias = swap(own_bias, "zh")
 
     order = jnp.stack([here ^ r for r in (3, 1, 2, 0)]).astype(jnp.int32)
     near1, near3, far2, r0 = pack(order, sx, qkv_weight, fc1_weight, dense_weight, fc2_weight)
@@ -879,82 +848,77 @@
     input_single = block_input.astype(F32)
     branch_gradient = cotangent.astype(F32)
 
-    to_y, att_y, other01 = split_first(far2, near3, r0, r1, after=[scale, other_bias])
-    r23, other01, att23 = swap(to_y, "y"), swap(other01, "zh"), swap(att_y, "y")
+    to_y, att_y, other01, att01 = split_first(far2, near3, r0, r1, after=[scale])
+    r23, other01 = swap(to_y, "y"), swap(other01, "zh")
     scale = jnp.concatenate([scale, swap(scale, "y")], axis=0)
-    token, (r23, att23, other01) = gate([to_y, scale, tables, start], [r23, att23, other01])
-
-    other23 = swap(r23, "zh")
+    other_bias = swap(own_bias, "zh")
+    token, (r23, other01, att_y, att01) = gate(
+        [to_y, scale, other_bias, tables, start], [r23, other01, att_y, att01]
+    )
+
+    other23, att23 = swap(r23, "zh"), swap(att_y, "y")
     own23, next01 = swap(r23, "x"), swap(other01, "x")
-    other_r = stack_att(r0, r1, att23, after=[token])
-    normed, stats = norm_tokens(place, tokens, scale, after=[token, other_r])
-    token, (other23, own23, next01) = gate([stats], [other23, own23, next01])
+    normed, stats = norm_tokens(place, tokens, scale, after=[token])
+    token, (other23, att23, att01) = gate([stats, own23, next01], [other23, att23, att01])
     mine = lax.dynamic_slice_in_dim(stats, zl * HALF, HALF, axis=0)
     average, inverse = mine[:, :1], mine[:, 128:129]
     centered = (input_single - average) * inverse
 
-    other_r = swap(other_r, "zh")
-    next23, next_att23 = swap(other23, "x"), swap(att23, "x")
+    next23, att01 = swap(other23, "x"), swap(att01, "zh")
+    token, (att01, att23) = gate([token, next23], [att01, att23])
+
     own_w = [(r0, 0), (r1, 0), (r23, 0), (r23, 1), (r0, 1), (r1, 1), (own23, 0), (own23, 1)]
     other_w = [(array, i) for array in (other01, other23, next01, next23) for i in range(2)]
+    next_att01, other_att23, next_att23 = swap(att01, "x"), swap(att23, "zh"), swap(att23, "x")
+    other_act, other_dfc, *other_mlp, other_units = mlp(
+        place, normed, cot, other_w, other_bias[:, 384:], after=[token]
+    )
+    token, (other_att23, other_mlp[1]) = gate(
+        [other_units, next_att01, next_att23], [other_att23, other_mlp[1]]
+    )
+
+    from_x, next_other23 = swap(other_mlp[1], "x"), swap(other_att23, "x")
     own_act, own_dfc, *own_mlp, own_units = mlp(
         place, normed, cot, own_w, own_bias[:, 384:], after=[token]
     )
-    token, (other_r, next23, next_att23, *own_mlp) = gate(
-        [own_units], [other_r, next23, next_att23, *own_mlp]
-    )
-    other_w[6:] = [(next23, 0), (next23, 1)]
-
-    next_r = swap(other_r, "x")
-    other_act, other_dfc, *other_mlp, other_units = mlp(
-        place, normed, cot, other_w, other_bias[:, 384:], after=[token]
-    )
-    token, (next_r, *other_mlp) = gate([other_units], [next_r, *other_mlp])
+    token, (other_mlp[3], own_mlp[1]) = gate(
+        [own_units, from_x, next_other23], [other_mlp[3], own_mlp[1]]
+    )
 
     own_a = [(r0, 0, 2), (r1, 0, 2), (att23, 0, 0), (att23, 1, 0)]
     own_a += [(r0, 1, 2), (r1, 1, 2), (next_att23, 0, 0), (next_att23, 1, 0)]
-    other_a = [(array, i, 0) for array in (other_r, next_r) for i in range(4)]
-    from_x = swap(other_mlp[1], "x")
-    own_heads = heads(place, normed, cot, own_a, own_bias[:, :384], tables, after=[token])
-    other_heads = heads(
-        place, normed, cot, other_a, other_bias[:, :384], tables, after=[own_heads[0]]
-    )
-    token, (from_x, other_mlp[3], own_mlp[1]) = gate(
-        [other_heads[0]], [from_x, other_mlp[3], own_mlp[1]]
-    )
-
+    other_a = [
+        (array, i, 0) for array in (att01, other_att23, next_att01, next_other23) for i in range(2)
+    ]
     fc2 = add(other_mlp[0], from_x, after=[token])[0]
     to_fc2 = swap(fc2, "zh")
     from_x, own_fc2 = swap(other_mlp[3], "x"), swap(own_mlp[1], "x")
-    other_o, other_dq, other_dk, other_dv, other_sums = attend(
-        low, *other_heads, start, tables, after=[fc2]
-    )
-    other_att = att_grad(
-        place, normed, cot, other_dq, other_dk, other_dv, other_o, after=[other_sums]
-    )
+    bias = jnp.concatenate([own_bias[:, :384], other_bias[:, :384]], axis=1)
+    qkv = heads(place, normed, cot, own_a + other_a, bias, tables, after=[fc2])
+    attended = attend(low, qkv, start, tables)
+    own_o, own_dq, own_dk, own_dv, own_sums = attended[:5]
+    other_o, other_dq, other_dk, other_dv, other_sums = attended[5:]
     other_sums = jnp.concatenate([other_sums[:3].reshape(1, 384), other_units], axis=1)
-    token, (to_fc2, from_x, own_fc2, other_att[1], other_att[2], own_mlp[3], other_sums) = gate(
-        [other_att[0]], [to_fc2, from_x, own_fc2, *other_att[1:], own_mlp[3], other_sums]
+    token, (own_mlp[3], other_sums) = gate(
+        [own_o, to_fc2, from_x, own_fc2], [own_mlp[3], other_sums]
     )
 
     fc1 = add(other_mlp[2], from_x, after=[token])[0]
     to_fc1 = swap(fc1, "zh")
+    other_att = att_grad(
+        place, normed, cot, other_dq, other_dk, other_dv, other_o, after=[fc1]
+    )
     other_sums = swap(other_sums, "zh")
     from_x, own_fc1 = swap_all(other_att[1:], "x"), swap(own_mlp[3], "x")
-    own_o, own_dq, own_dk, own_dv, own_sums = attend(
-        low, *own_heads, start, tables, after=[fc1]
-    )
     items = [(own_dfc, rows(own_w, 1, 0, 256)), (other_dfc, rows(other_w, 1, 0, 256))]
     for part, (left, right) in enumerate(
         ((own_dq, other_dq), (own_dk, other_dk), (own_dv, other_dv))
     ):
         items.append((left, rows(own_a, None, 64 * part, 64)))
         items.append((right, rows(other_a, None, 64 * part, 64)))
-    dn_near, dn_same = project_near(sz, items, after=[own_sums])
+    dn_near, dn_same = project_near(sz, items, after=[other_att[0]])
     own_sums = jnp.concatenate([own_sums[:3].reshape(1, 384), own_units], axis=1)
-    token, (to_fc1, from_x[0], from_x[1], own_fc1, other_sums, dn_near) = gate(
-        [dn_same, own_sums], [to_fc1, *from_x, own_fc1, other_sums, dn_near]
-    )
+    token, (dn_near,) = gate([dn_same, own_sums, to_fc1, *from_x, own_fc1, other_sums], [dn_near])
 
     dn_near = swap(dn_near, "c")
     mlp_near, mlp_same = total_grad(
@@ -977,56 +941,30 @@
     heads_sum = jnp.where(x == 0, heads_sum, heads_sum[:, ::-1]).reshape(1, 384)
     units_sum = jnp.where(x == 0, units_sum, units_sum[::-1]).reshape(1, 512)
     sums = jnp.concatenate([heads_sum, units_sum], axis=1)
-    token, (to_att, own_from_att[0], own_from_att[1], mlp_near, dn_near, near) = gate(
-        [same], [to_att, *own_from_att, mlp_near, dn_near, near]
-    )
+    token, (near,) = gate([same, to_att, *own_from_att, mlp_near, dn_near], [near])
 
     near = swap(near, "c")
-    to_z, to_y, dn, for_y, for_z = scatter_first(dn_same, dn_near, mlp_same, mlp_near, after=[token])
-    from_z, from_y = swap(to_z, "zl"), swap(to_y, "y")
+    to_z, to_y, mlp01, dn, for_y, for_z = scatter_first(
+        dn_same, dn_near, mlp_same, mlp_near, after=[token]
+    )
+    from_z, mlp23, next01 = swap(to_z, "zl"), swap(to_y, "y"), swap(mlp01, "x")
     att_near, att_same = total_grad([[own_att[0], own_from_att, to_att]], after=[dn])
     att_near, att_same = swap(more_dp(att_near), "c"), more_dp(att_same)
-    token, (near, from_z, from_y, att_near) = gate([att_same], [near, from_z, from_y, att_near])
-
-    to_z, to_y, branch, branch_y, branch_z = scatter_both(
-        for_y, from_z, for_z, from_y, same, near, att_same, att_near, after=[token]
-    )
-    dn_z, dn_y = swap(to_z, "zl"), swap(to_y, "y")
-    mlp_first = stack(
-        [(mlp_same, 0, 0, 512), (mlp_near, 0, 0, 512), (from_y, slice(2, 4), 0, 512)]
-        + [(from_y, slice(4, 6), 0, 512)],
-        after=[to_y],
-    )
-    mlp_second, sums_x = swap(mlp_first, "x"), swap(sums, "x")
-    token, (dn_y, dn_z, mlp_second, sums_x) = gate(
-        [mlp_first, sums], [dn_y, dn_z, mlp_second, sums_x]
-    )
-
-    dn = dn.astype(F32) + dn_y[:4].reshape(HALF, 512).astype(F32) + dn_z[:4].reshape(HALF, 512).astype(F32)
+    token, (mlp23,) = gate([att_same, near, from_z, next01, att_near], [mlp23])
+
+    to_y, to_z = scatter_second(for_y, from_z, after=[token]), for_z
+    dn_z, dn_y, next23, sums_x = swap(to_z, "zl"), swap(to_y, "y"), swap(mlp23, "x"), swap(sums, "x")
+    to_z, to_y, att01, branch, branch_y, branch_z = scatter_third(
+        same, near, att_same, att_near, after=[to_y]
+    )
+    token, (to_z, to_y, att01) = gate(
+        [branch, sums, dn_y, dn_z, next23, sums_x], [to_z, to_y, att01]
+    )
+
+    from_z, from_y, next_att01 = swap(to_z, "zl"), swap(to_y, "y"), swap(att01, "x")
+    dn = dn.astype(F32) + dn_y.astype(F32) + dn_z.astype(F32)
     row_sums = jnp.stack(
         [jnp.sum(dn * layernorm_gain, axis=1), jnp.sum(dn * layernorm_gain * centered, axis=1)]
-    )
-    row_sums = row_sums + swap(row_sums, "c")
-    row_sums = row_sums + swap(row_sums, "y")
-    to_z, to_y = scatter_last(branch_y, dn_z, branch_z, dn_y, after=[token, row_sums])
-    branch_z, branch_y = swap(to_z, "zl"), swap(to_y, "y")
-    att_first = stack(
-        [(att_same, 0, 0, 256), (att_near, 0, 0, 256), (dn_y, 6, 0, 256), (dn_y, 7, 0, 256)],
-        after=[to_y],
-    )
-    att_second = swap(att_first, "x")
-    fc1_grad, fc2_grad = unpack_mlp(place, sx, mlp_first, mlp_second, after=[att_first])
-    qkv_grad, dense_grad = unpack_att(place, sx, att_first, att_second, after=[fc1_grad])
-    sums = more_dp(sums + sums_x)
-
-    qkv_bias_grad, fc1_bias_grad = sums[0, :384].reshape(3, 128), sums[0, 384:]
-
-    branch = branch.astype(F32) + branch_y.reshape(HALF, 512).astype(F32) + branch_z.reshape(HALF, 512).astype(F32)
-    result = (input_single + (branch + out_bias)).astype(BF)
-    input_grad = branch_gradient + inverse * (
-        dn * layernorm_gain
-        - row_sums[0][:, None] / MODEL_WIDTH
-        - centered * (row_sums[1][:, None] / MODEL_WIDTH)
     )
     col_sums = jnp.stack(
         [
@@ -1035,8 +973,34 @@
             jnp.sum(branch_gradient, axis=0),
         ]
     )
-    for axis in ("zl", "zh", "x"):
-        col_sums = col_sums + swap(col_sums, axis)
+    row_sums = row_sums + swap(row_sums, "c")
+    col_sums = col_sums + swap(col_sums, "x")
+    token, (row_sums, col_sums) = gate([token, from_z, from_y, next_att01], [row_sums, col_sums])
+
+    row_sums = row_sums + swap(row_sums, "y")
+    col_sums = col_sums + swap(col_sums, "zl")
+    to_z, to_y, att23 = scatter_last(
+        branch_y, from_z, branch_z, from_y, after=[token, row_sums, col_sums]
+    )
+    col_sums = col_sums + swap(col_sums, "zh")
+    branch_z, branch_y, next_att23 = swap(to_z, "zl"), swap(to_y, "y"), swap(att23, "x")
+    mlp_pieces = (mlp01, mlp23, next01, next23)
+    fc2_grad = unpack_fc2(place, sx, mlp_pieces, after=[to_y])
+    fc1_grad = unpack_fc1(place, sx, mlp_pieces, after=[fc2_grad])
+    qkv_grad, dense_grad = unpack_att(
+        place, sx, (att01, att23, next_att01, next_att23), after=[fc1_grad]
+    )
+    sums = more_dp(sums + sums_x)
+
+    qkv_bias_grad, fc1_bias_grad = sums[0, :384].reshape(3, 128), sums[0, 384:]
+
+    branch = branch.astype(F32) + branch_y.astype(F32) + branch_z.astype(F32)
+    result = (input_single + (branch + out_bias)).astype(BF)
+    input_grad = branch_gradient + inverse * (
+        dn * layernorm_gain
+        - row_sums[0][:, None] / MODEL_WIDTH
+        - centered * (row_sums[1][:, None] / MODEL_WIDTH)
+    )
     col_sums = more_dp(col_sums)
     return (
         result,

time: 627 us -> 568 us (0.906)
  waiting for transfers between devices: 197 us -> 148 us
  Pallas kernels: 296 us -> 266 us
  starting transfers between devices: 53.6 us -> 70.8 us
    ppermute x45 -> x51, waiting for transfers between devices: 182 us -> 147 us  [swap(): return lax.ppermute(value, axis, [(0, 1), (1, 0)])]
    pallas_call x36 -> x34, Pallas kernels: 296 us -> 266 us  [call(): pl.pallas_call(kernel, grid_spec=pltpu.PrefetchScalarGridSpec(num_scalar_...]
    ppermute x45 -> x51, starting transfers between devices: 53.5 us -> 70.7 us  [swap(): return lax.ppermute(value, axis, [(0, 1), (1, 0)])]
    all_gather x1, waiting for transfers between devices: 13.6 us -> 0.01 us  [on_device(): cot = lax.all_gather(cotangent, ('zl', 'y', 'c'), axis=0, tiled=False)]
    add x3 -> x4, other arithmetic: 0.03 us -> 6.43 us  [the longest x1 4.53 us: on_device(): branch_gradient + inverse * (dn * layernorm_gain - row_sums[0][:, None] /...]
    unnamed x123 -> x137, local copies, waits for them, and re-layouts: 13.5 us -> 14.3 us
  transfers between devices with their start and end apart: 47 -> 53, of which waited for: 21 -> 24; matrix products, arithmetic and copies ran while one was open for 6% -> 7% of each run, Pallas kernels for 43% -> 45%
where the time goes in v3:
time: 568 us; the launch traced here: 559 us
  Pallas kernels  266 us (47%)
  waiting for transfers between devices  148 us (26%)
  starting transfers between devices  70.8 us (12%)
  local copies, waits for them, and re-layouts  32.7 us (6%)
  other arithmetic  26.1 us (5%)
  between operations  14.9 us (3%)
    pallas_call x34, Pallas kernels, call(): pl.pallas_call(kernel, grid_spec=pltpu.PrefetchScalarGridSpec(num_scalar_...  266 us
    ppermute x51, waiting for transfers between devices, swap(): return lax.ppermute(value, axis, [(0, 1), (1, 0)])  147 us
    ppermute x51, starting transfers between devices, swap(): return lax.ppermute(value, axis, [(0, 1), (1, 0)])  70.7 us
    unnamed x137, local copies, waits for them, and re-layouts  14.3 us
  transfers between devices with their start and end apart: 53, of which 24 were waited for; matrix products, arithmetic and copies ran while one was open for 7% of the time, Pallas kernels for 45%

profile of v3, /device:TPU:8, one launch (start us, length us, event | category | flops | bytes accessed | tf_op | source)
XLA Modules:
  0.0 558.5 jit_solution(6279619159715198519)
XLA Ops:
  9.3 7.0 %shard_map.203 = (bf16[2,768,512]{2,1,0:T(8,128)(2,1)}, bf16[768,512]{1,0:T(8,128)(2,1)}, bf16[768,512]{1,0:T(8,128)(2,1)}, bf16[2,768,512]{2,1,0:T(8,128)(2,1)}) custom-call(s32[4]{0:T(128)} %pad_add_fusion.1.refs_0_, s32[1]{0:T(128)} %bitcast.8.refs_1_, bf16[3,512,512]{2,1,0:T(8,128)(2,1)} %refs_2_.1, bf16[2048,512]{1,0:T(8,128)(2,1)} %refs_3_.1, ...), custom_call_target="tpu_custom_call" | custom-call | flops 1000 | bytes 1000 | tf_op jit(solution)/shard_map/pallas_call | solution.py:61
  30.2 5.5 multiply_cosine_fusion
  36.7 4.5 concatenate.38
  43.3 4.7 concatenate.41
  53.1 24.2 %collective-permute-done.1 = f32[4,512]{1,0:T(4,128)S(1)} collective-permute-done((f32[4,512]{1,0:T(4,128)S(1)}, f32[4,512]{1,0:T(4,128)S(1)}, u32[]{:S(2)}, u32[]{:S(2)}) %collective-permute-start.1) | collective-permute-done | bytes 8224 | tf_op jit(solution)/shard_map/ppermute | solution.py:25
  85.3 12.6 %shard_map.206 = (bf16[2048,2048]{1,0:T(8,128)(2,1)}, f32[2048,256]{1,0:T(8,128)}) custom-call(s32[4]{0:T(128)} %pad_add_fusion.refs_0_, bf16[2,4,1024,512]{3,2,1,0:T(8,128)(2,1)} %bitcast.55, f32[8,512]{1,0:T(8,128)} %pad_maximum_fusion.1.refs_1_.refs_2_, f32[8,128]{1,0:T(8,128)} %get-tuple-element.128.refs_3_), custom_call_target="tpu_custom_call" | custom-call | flops 1000 | bytes 1000 | tf_op jit(solution)/shard_map/pallas_call | solution.py:61
  100.3 6.3 %collective-permute-done.8.refs_2_.refs_7_.refs_8_.refs_21_.refs_22_.refs_17_.refs_18_ = bf16[2,512,512]{2,1,0:T(8,128)(2,1)S(1)} collective-permute-done((bf16[2,512,512]{2,1,0:T(8,128)(2,1)}, bf16[2,512,512]{2,1,0:T(8,128)(2,1)S(1)}, u32[]{:S(2)}, u32[]{:S(2)}) %collective-permute-start.8) | collective-permute-done | bytes 1048608 | tf_op jit(solution)/shard_map/ppermute | solution.py:25
  106.5 20.2 %collective-permute-done.9.refs_3_ = bf16[2,512,512]{2,1,0:T(8,128)(2,1)S(1)} collective-permute-done((bf16[2,512,512]{2,1,0:T(8,128)(2,1)}, bf16[2,512,512]{2,1,0:T(8,128)(2,1)S(1)}, u32[]{:S(2)}, u32[]{:S(2)}) %collective-permute-start.9) | collective-permute-done | bytes 1048608 | tf_op jit(solution)/shard_map/ppermute | solution.py:25
  132.2 20.9 %collective-permute-done.12.refs_2_ = bf16[2,256,512]{2,1,0:T(8,128)(2,1)S(1)} collective-permute-done((bf16[2,256,512]{2,1,0:T(8,128)(2,1)}, bf16[2,256,512]{2,1,0:T(8,128)(2,1)S(1)}, u32[]{:S(2)}, u32[]{:S(2)}) %collective-permute-start.12) | collective-permute-done | bytes 524320 | tf_op jit(solution)/shard_map/ppermute | solution.py:25
  161.1 27.6 %shard_map.209 = (bf16[2048,512]{1,0:T(8,128)(2,1)}, bf16[2048,512]{1,0:T(8,128)(2,1)}, bf16[4,256,512]{2,1,0:T(8,128)(2,1)}, bf16[4,256,512]{2,1,0:T(8,128)(2,1...) custom-call(s32[4]{0:T(128)} %pad_add_fusion.refs_0_, ...), custom_call_target="tpu_custom_call" | custom-call | flops 1000 | bytes 1000 | tf_op jit(solution)/shard_map/pallas_call | solution.py:61
  192.7 28.0 %shard_map.211 = (bf16[2048,512]{1,0:T(8,128)(2,1)}, bf16[2048,512]{1,0:T(8,128)(2,1)}, bf16[4,256,512]{2,1,0:T(8,128)(2,1)}, bf16[4,256,512]{2,1,0:T(8,128)(2,1...) custom-call(s32[4]{0:T(128)} %pad_add_fusion.refs_0_, ...), custom_call_target="tpu_custom_call" | custom-call | flops 1000 | bytes 1000 | tf_op jit(solution)/shard_map/pallas_call | solution.py:61
  220.6 5.3 collective-permute-done.16.refs_2_.refs_17_.refs_18_.refs_39_.refs_40_.refs_55_.refs_56_.refs_71_.refs_72_.refs_35_.refs_36_
  230.5 4.3 collective-permute-start.19
  238.1 15.8 %shard_map.214 = (bf16[2048,128]{1,0:T(8,128)(2,1)}, bf16[2048,128]{1,0:T(8,128)(2,1)}, bf16[2048,128]{1,0:T(8,128)(2,1)}, bf16[2048,128]{1,0:T(8,128)(2,1)}, bf...) custom-call(s32[4]{0:T(128)} %pad_add_fusion.refs_0_, ...), custom_call_target="tpu_custom_call" | custom-call | flops 1000 | bytes 1000 | tf_op jit(solution)/shard_map/pallas_call | solution.py:61
  254.0 46.9 %shard_map.215 = (bf16[2048,128]{1,0:T(8,128)(2,1)}, bf16[2048,128]{1,0:T(8,128)(2,1)}, bf16[2048,128]{1,0:T(8,128)(2,1)}, bf16[2048,128]{1,0:T(8,128)(2,1)}, f3...) custom-call(s32[4]{0:T(128)} %and_select_fusion.refs_0_, ...), custom_call_target="tpu_custom_call" | custom-call | flops 1000 | bytes 1000 | tf_op jit(solution)/shard_map/pallas_call | solution.py:61
  307.2 8.0 %collective-permute-start.24 = (bf16[4,256,512]{2,1,0:T(8,128)(2,1)}, bf16[4,256,512]{2,1,0:T(8,128)(2,1)S(1)}, u32[]{:S(2)}, u32[]{:S(2)}) collective-permute-start(bf16[4,256,512]{2,1,0:T(8,128)(2,1)} %shard_map.217.refs_7_), channel_id=1, source_target_pairs={{0,8},{8,0},{1,9},{9,1},{2,10},{10,2},{3,11},{11,3},{4,12},{12,4},... | collective-permute-start | bytes 3145736 | tf_op jit(solution)/shard_map/ppermute | solution.py:25
  316.7 11.3 %shard_map.218 = (bf16[4,256,512]{2,1,0:T(8,128)(2,1)}, bf16[2,256,512]{2,1,0:T(8,128)(2,1)}, bf16[2,256,512]{2,1,0:T(8,128)(2,1)}) custom-call(s32[4]{0:T(128)} %pad_add_fusion.refs_0_, bf16[2048,2048]{1,0:T(8,128)(2,1)} %get-tuple-element.129.refs_1_, bf16[2,4,1024,512]{3,2,1,0:T(8,128)(2,1)} %bitcast.53, ...), custom_call_target="tpu_custom_call" | custom-call | flops 1000 | bytes 1000 | tf_op jit(solution)/shard_map/pallas_call | solution.py:61
  333.1 26.0 %shard_map.219 = (bf16[2,2,1024,512]{3,2,1,0:T(8,128)(2,1)}, bf16[2,2,1024,512]{3,2,1,0:T(8,128)(2,1)}) custom-call(s32[1]{0:T(128)} %bitcast.refs_0_, bf16[2048,512]{1,0:T(8,128)(2,1)} %get-tuple-element.184.refs_1_, bf16[2048,512]{1,0:T(8,128)(2,1)} %get-tuple-element.185.refs_2_, bf16[2048,128]{1,0:T(8,128)(2,1)} %get-tuple-element.166.refs_3_, ...), custom_call_target="tpu_custom_call" | custom-call | flops 1000 | bytes 1000 | tf_op jit(solution)/shard_map/pallas_call | solution.py:61
  363.6 4.5 shard_map.221
  373.8 11.2 %shard_map.223 = (bf16[4,256,512]{2,1,0:T(8,128)(2,1)}, bf16[2,256,512]{2,1,0:T(8,128)(2,1)}, bf16[2,256,512]{2,1,0:T(8,128)(2,1)}) custom-call(s32[4]{0:T(128)} %pad_add_fusion.refs_0_, bf16[2048,2048]{1,0:T(8,128)(2,1)} %get-tuple-element.129.refs_1_, bf16[2,4,1024,512]{3,2,1,0:T(8,128)(2,1)} %bitcast.54, bf16[2048,128]{1,0:T(8,128)(2,1)} %get-tuple-element.166.refs_3_, ...), custom_call_target="tpu_custom_call" | custom-call | flops 1000 | bytes 1000 | tf_op jit(solution)/shard_map/pallas_call | solution.py:61
  387.0 17.8 %shard_map.224 = (bf16[2,2,1024,512]{3,2,1,0:T(8,128)(2,1)}, bf16[2,2,1024,512]{3,2,1,0:T(8,128)(2,1)}) custom-call(s32[1]{0:T(128)} %bitcast.refs_0_, bf16[2048,512]{1,0:T(8,128)(2,1)} %get-tuple-element.145.refs_1_, bf16[2048,512]{1,0:T(8,128)(2,1)} %get-tuple-element.146.refs_2_, bf16[2048,128]{1,0:T(8,128)(2,1)} %get-tuple-element.164.refs_0_.refs_6_.refs_3_, ...), custom_call_target="tpu_custom_call" | custom-call | flops 1000 | bytes 1000 | tf_op jit(solution)/shard_map/pallas_call | solution.py:61
  404.8 5.2 collective-permute-done.28.refs_3_.refs_2_
  410.0 6.8 %collective-permute-done.26.refs_1_.refs_3_ = bf16[4,256,512]{2,1,0:T(8,128)(2,1)S(1)} collective-permute-done((bf16[4,256,512]{2,1,0:T(8,128)(2,1)}, bf16[4,256,512]{2,1,0:T(8,128)(2,1)S(1)}, u32[]{:S(2)}, u32[]{:S(2)}) %collective-permute-start.26) | collective-permute-done | bytes 1048608 | tf_op jit(solution)/shard_map/ppermute | solution.py:25
  418.3 7.0 %shard_map.226 = (bf16[4,256,512]{2,1,0:T(8,128)(2,1)}, bf16[4,256,512]{2,1,0:T(8,128)(2,1)}, bf16[4,256,512]{2,1,0:T(8,128)(2,1)}, bf16[1024,512]{1,0:T(8,128)(...) custom-call(bf16[2,2,1024,512]{3,2,1,0:T(8,128)(2,1)} %get-tuple-element.186.refs_0_, ...), custom_call_target="tpu_custom_call" | custom-call | flops 1000 | bytes 1000 | tf_op jit(solution)/shard_map/pallas_call | solution.py:61
  437.9 15.1 %collective-permute-done.33.refs_2_.refs_1_ = bf16[4,256,512]{2,1,0:T(8,128)(2,1)S(1)} collective-permute-done((bf16[4,256,512]{2,1,0:T(8,128)(2,1)}, bf16[4,256,512]{2,1,0:T(8,128)(2,1)S(1)}, u32[]{:S(2)}, u32[]{:S(2)}) %collective-permute-start.33) | collective-permute-done | bytes 1048608 | tf_op jit(solution)/shard_map/ppermute | solution.py:25
  465.6 6.2 %shard_map.230 = (bf16[3,256,512]{2,1,0:T(8,128)(2,1)}, bf16[3,256,512]{2,1,0:T(8,128)(2,1)}, bf16[2,256,512]{2,1,0:T(8,128)(2,1)}, bf16[1024,512]{1,0:T(8,128)(...) custom-call(bf16[2,2,1024,512]{3,2,1,0:T(8,128)(2,1)} %get-tuple-element.193.refs_0_, ...), custom_call_target="tpu_custom_call" | custom-call | flops 1000 | bytes 1000 | tf_op jit(solution)/shard_map/pallas_call | solution.py:61
  471.8 13.9 %collective-permute-done.39.refs_5_ = f32[1,896]{1,0:T(1,128)S(1)} collective-permute-done((f32[1,896]{1,0:T(1,128)S(1)}, f32[1,896]{1,0:T(1,128)S(1)}, u32[]{:S(2)}, u32[]{:S(2)}) %collective-permute-start.39) | collective-permute-done | bytes 3616 | tf_op jit(solution)/shard_map/ppermute | solution.py:25
  497.3 8.0 %collective-permute-done.42.refs_3_.refs_4_ = bf16[2,256,512]{2,1,0:T(8,128)(2,1)S(1)} collective-permute-done((bf16[2,256,512]{2,1,0:T(8,128)(2,1)S(1)}, bf16[2,256,512]{2,1,0:T(8,128)(2,1)S(1)}, u32[]{:S(2)}, u32[]{:S(2)}) %collective-permute-start.42) | collective-permute-done | bytes 524320 | tf_op jit(solution)/shard_map/ppermute | solution.py:25
  525.4 5.6 %shard_map.234.refs_6_ = f32[512,2048]{1,0:T(8,128)} custom-call(s32[4]{0:T(128)} %pad_add_fusion.refs_0_, s32[1]{0:T(128)} %bitcast.8.refs_1_, bf16[4,256,512]{2,1,0:T(8,128)(2,1)} %get-tuple-element.206.refs_2_, bf16[4,256,512]{2,1,0:T(8,128)(2,1)} %get-tuple-element.212.refs_3_, bf16[4,256,512]{2,1,0:T(8,128)(2,1)} %copy-done.13, ...), custom_call_target="tpu_custom_call" | custom-call | flops 1000 | bytes 1000 | tf_op jit(solution)/shard_map/pallas_call | solution.py:61
  531.1 5.4 shard_map.235.refs_6_
  542.2 4.8 shard_map.236
  547.0 4.5 convert_add_fusion
  (310 shorter events, 148.5 us)
Async XLA Ops:
  7.2 78.1 %all-gather.5.cloned.1.call-start = ((), (), s32[]{:S(2)}) async-start(), calls=%async_computation | async-start | bytes 9437184 | tf_op jit(solution)/shard_map/all_gather | solution.py:807
  7.9 153.2 %all-gather.7.cloned.1.call-start = ((), (), s32[]{:S(2)}) async-start(), calls=%async_computation.1 | async-start | bytes 9437184 | tf_op jit(solution)/shard_map/all_gather | solution.py:808
  17.1 60.8 %collective-permute-start.4 = (f32[1,896]{1,0:T(1,128)S(1)}, f32[1,896]{1,0:T(1,128)S(1)}, u32[]{:S(2)}, u32[]{:S(2)}) collective-permute-start(f32[1,896]{1,0:T(1,128)S(1)} %pad_maximum_fusion.6), channel_id=1, source_target_pairs={{0,8},{8,0},{1,9},{9,1},{2,10},{10,2},{3,11},{11,3},{4,12},{12,4},... | collective-permute-start | bytes 10760 | tf_op jit(solution)/shard_map/ppermute | solution.py:25
  26.7 51.3 %collective-permute-start.6 = (bf16[2,512,512]{2,1,0:T(8,128)(2,1)}, bf16[2,512,512]{2,1,0:T(8,128)(2,1)S(1)}, u32[]{:S(2)}, u32[]{:S(2)}) collective-permute-start(bf16[2,512,512]{2,1,0:T(8,128)(2,1)} %get-tuple-element.125), channel_id=1, source_target_pairs={{0,8},{8,0},{1,9},{9,1},{2,10},{10,2},{3,11},{11,3},{4,12},{12,4},... | collective-permute-start | bytes 3145736 | tf_op jit(solution)/shard_map/ppermute | solution.py:25
  28.6 49.3 %collective-permute-start.5 = (bf16[2,512,512]{2,1,0:T(8,128)(2,1)}, bf16[2,512,512]{2,1,0:T(8,128)(2,1)S(1)}, u32[]{:S(2)}, u32[]{:S(2)}) collective-permute-start(bf16[2,512,512]{2,1,0:T(8,128)(2,1)} %get-tuple-element.124.refs_0_), channel_id=1, source_target_pairs={{0,2},{2,0},{1,3},{3,1},{4,6},{6,4},{5,7},{7,5},{8,10},{10,8},{9,1... | collective-permute-start | bytes 3145736 | tf_op jit(solution)/shard_map/ppermute | solution.py:25
  80.2 26.3 %collective-permute-start.8 = (bf16[2,512,512]{2,1,0:T(8,128)(2,1)}, bf16[2,512,512]{2,1,0:T(8,128)(2,1)S(1)}, u32[]{:S(2)}, u32[]{:S(2)}) collective-permute-start(bf16[2,512,512]{2,1,0:T(8,128)(2,1)} %get-tuple-element.131.refs_3_.refs_4_.refs_17_.refs_18_.refs_13_.refs_14_), channel_id=1, source_target_pairs={{0,16},{16,0},{1,17},{17,1},{2,18},{18,2},{3,19},{19,3},{4,20},{20... | collective-permute-start | bytes 3145736 | tf_op jit(solution)/shard_map/ppermute | solution.py:25
  81.7 45.1 %collective-permute-start.9 = (bf16[2,512,512]{2,1,0:T(8,128)(2,1)}, bf16[2,512,512]{2,1,0:T(8,128)(2,1)S(1)}, u32[]{:S(2)}, u32[]{:S(2)}) collective-permute-start(bf16[2,512,512]{2,1,0:T(8,128)(2,1)} %get-tuple-element.130.refs_5_.refs_6_.refs_11_.refs_12_.refs_7_.refs_8_), channel_id=1, source_target_pairs={{0,8},{8,0},{1,9},{9,1},{2,10},{10,2},{3,11},{11,3},{4,12},{12,4},... | collective-permute-start | bytes 3145736 | tf_op jit(solution)/shard_map/ppermute | solution.py:25
  82.6 44.5 %collective-permute-start.7 = (bf16[2,512,512]{2,1,0:T(8,128)(2,1)}, bf16[2,512,512]{2,1,0:T(8,128)(2,1)}, u32[]{:S(2)}, u32[]{:S(2)}) collective-permute-start(bf16[2,512,512]{2,1,0:T(8,128)(2,1)} %get-tuple-element.130.refs_5_.refs_6_.refs_11_.refs_12_.refs_7_.refs_8_), channel_id=1, source_target_pairs={{0,16},{16,0},{1,17},{17,1},{2,18},{18,2},{3,19},{19,3},{4,20},{20... | collective-permute-start | bytes 3145736 | tf_op jit(solution)/shard_map/ppermute | solution.py:25
  128.3 25.3 %collective-permute-start.11 = (bf16[2,512,512]{2,1,0:T(8,128)(2,1)}, bf16[2,512,512]{2,1,0:T(8,128)(2,1)S(1)}, u32[]{:S(2)}, u32[]{:S(2)}) collective-permute-start(bf16[2,512,512]{2,1,0:T(8,128)(2,1)} %get-tuple-element.135.refs_5_.refs_6_.refs_19_.refs_20_.refs_15_.refs_16_), channel_id=1, source_target_pairs={{0,16},{16,0},{1,17},{17,1},{2,18},{18,2},{3,19},{19,3},{4,20},{20... | collective-permute-start | bytes 3145736 | tf_op jit(solution)/shard_map/ppermute | solution.py:25
  155.2 33.6 %collective-permute-start.13 = (bf16[2,256,512]{2,1,0:T(8,128)(2,1)}, bf16[2,256,512]{2,1,0:T(8,128)(2,1)S(1)}, u32[]{:S(2)}, u32[]{:S(2)}) collective-permute-start(bf16[2,256,512]{2,1,0:T(8,128)(2,1)} %get-tuple-element.141.refs_11_.refs_12_.refs_33_.refs_34_.refs_49_.refs_50_.refs_65_.refs_66_.refs_29_.ref, ...), channel_id=1, source_target_pairs={{0,16},{16,0},{1,17},{17,1},{2,18},{18,2},{3,19},{19,3},{4,20},{20... | collective-permute-start | bytes 1572872 | tf_op jit(solution)/shard_map/ppermute | solution.py:25
  157.2 31.6 %collective-permute-start.15 = (bf16[2,256,512]{2,1,0:T(8,128)(2,1)}, bf16[2,256,512]{2,1,0:T(8,128)(2,1)S(1)}, u32[]{:S(2)}, u32[]{:S(2)}) collective-permute-start(bf16[2,256,512]{2,1,0:T(8,128)(2,1)} %get-tuple-element.142.refs_5_.refs_6_.refs_27_.refs_28_.refs_43_.refs_44_.refs_59_.refs_60_.refs_23_.refs_24_), channel_id=1, source_target_pairs={{0,8},{8,0},{1,9},{9,1},{2,10},{10,2},{3,11},{11,3},{4,12},{12,4},... | collective-permute-start | bytes 1572872 | tf_op jit(solution)/shard_map/ppermute | solution.py:25
  160.6 28.2 %collective-permute-start.14 = (bf16[2,256,512]{2,1,0:T(8,128)(2,1)}, bf16[2,256,512]{2,1,0:T(8,128)(2,1)S(1)}, u32[]{:S(2)}, u32[]{:S(2)}) collective-permute-start(bf16[2,256,512]{2,1,0:T(8,128)(2,1)} %get-tuple-element.142.refs_5_.refs_6_.refs_27_.refs_28_.refs_43_.refs_44_.refs_59_.refs_60_.refs_23_.refs_24_), channel_id=1, source_target_pairs={{0,16},{16,0},{1,17},{17,1},{2,18},{18,2},{3,19},{19,3},{4,20},{20... | collective-permute-start | bytes 1572872 | tf_op jit(solution)/shard_map/ppermute | solution.py:25
  190.6 35.4 %collective-permute-start.17 = (bf16[4,256,512]{2,1,0:T(8,128)(2,1)}, bf16[4,256,512]{2,1,0:T(8,128)(2,1)S(1)}, u32[]{:S(2)}, u32[]{:S(2)}) collective-permute-start(bf16[4,256,512]{2,1,0:T(8,128)(2,1)} %get-tuple-element.149), channel_id=1, source_target_pairs={{0,16},{16,0},{1,17},{17,1},{2,18},{18,2},{3,19},{19,3},{4,20},{20... | collective-permute-start | bytes 3145736 | tf_op jit(solution)/shard_map/ppermute | solution.py:25
  192.6 33.3 %collective-permute-start.16 = (bf16[2,256,512]{2,1,0:T(8,128)(2,1)}, bf16[2,256,512]{2,1,0:T(8,128)(2,1)S(1)}, u32[]{:S(2)}, u32[]{:S(2)}) collective-permute-start(bf16[2,256,512]{2,1,0:T(8,128)(2,1)} %get-tuple-element.147.refs_13_.refs_14_.refs_35_.refs_36_.refs_51_.refs_52_.refs_67_.refs_68_.refs_31_.ref, ...), channel_id=1, source_target_pairs={{0,16},{16,0},{1,17},{17,1},{2,18},{18,2},{3,19},{19,3},{4,20},{20... | collective-permute-start | bytes 1572872 | tf_op jit(solution)/shard_map/ppermute | solution.py:25
  230.5 71.6 %collective-permute-start.19 = (bf16[4,256,512]{2,1,0:T(8,128)(2,1)}, bf16[4,256,512]{2,1,0:T(8,128)(2,1)S(1)}, u32[]{:S(2)}, u32[]{:S(2)}) collective-permute-start(bf16[4,256,512]{2,1,0:T(8,128)(2,1)} %shard_map.213.refs_21_), channel_id=1, source_target_pairs={{0,8},{8,0},{1,9},{9,1},{2,10},{10,2},{3,11},{11,3},{4,12},{12,4},... | collective-permute-start | bytes 3145736 | tf_op jit(solution)/shard_map/ppermute | solution.py:25
  234.8 67.3 %collective-permute-start.18 = (bf16[4,256,512]{2,1,0:T(8,128)(2,1)}, bf16[4,256,512]{2,1,0:T(8,128)(2,1)S(1)}, u32[]{:S(2)}, u32[]{:S(2)}) collective-permute-start(bf16[4,256,512]{2,1,0:T(8,128)(2,1)} %get-tuple-element.173), channel_id=1, source_target_pairs={{0,16},{16,0},{1,17},{17,1},{2,18},{18,2},{3,19},{19,3},{4,20},{20... | collective-permute-start | bytes 3145736 | tf_op jit(solution)/shard_map/ppermute | solution.py:25
  236.3 65.8 %collective-permute-start.20 = (bf16[4,256,512]{2,1,0:T(8,128)(2,1)}, bf16[4,256,512]{2,1,0:T(8,128)(2,1)S(1)}, u32[]{:S(2)}, u32[]{:S(2)}) collective-permute-start(bf16[4,256,512]{2,1,0:T(8,128)(2,1)} %get-tuple-element.174), channel_id=1, source_target_pairs={{0,16},{16,0},{1,17},{17,1},{2,18},{18,2},{3,19},{19,3},{4,20},{20... | collective-permute-start | bytes 3145736 | tf_op jit(solution)/shard_map/ppermute | solution.py:25
  307.2 54.4 %collective-permute-start.24 = (bf16[4,256,512]{2,1,0:T(8,128)(2,1)}, bf16[4,256,512]{2,1,0:T(8,128)(2,1)S(1)}, u32[]{:S(2)}, u32[]{:S(2)}) collective-permute-start(bf16[4,256,512]{2,1,0:T(8,128)(2,1)} %shard_map.217.refs_7_), channel_id=1, source_target_pairs={{0,8},{8,0},{1,9},{9,1},{2,10},{10,2},{3,11},{11,3},{4,12},{12,4},... | collective-permute-start | bytes 3145736 | tf_op jit(solution)/shard_map/ppermute | solution.py:25
  315.2 46.4 %collective-permute-start.23 = (bf16[4,256,512]{2,1,0:T(8,128)(2,1)}, bf16[4,256,512]{2,1,0:T(8,128)(2,1)S(1)}, u32[]{:S(2)}, u32[]{:S(2)}) collective-permute-start(bf16[4,256,512]{2,1,0:T(8,128)(2,1)} %get-tuple-element.183), channel_id=1, source_target_pairs={{0,16},{16,0},{1,17},{17,1},{2,18},{18,2},{3,19},{19,3},{4,20},{20... | collective-permute-start | bytes 3145736 | tf_op jit(solution)/shard_map/ppermute | solution.py:25
  328.1 31.3 %collective-permute-start.21 = (bf16[2,256,512]{2,1,0:T(8,128)(2,1)}, bf16[2,256,512]{2,1,0:T(8,128)(2,1)S(1)}, u32[]{:S(2)}, u32[]{:S(2)}) collective-permute-start(bf16[2,256,512]{2,1,0:T(8,128)(2,1)} %get-tuple-element.179), channel_id=1, source_target_pairs={{0,16},{16,0},{1,17},{17,1},{2,18},{18,2},{3,19},{19,3},{4,20},{20... | collective-permute-start | bytes 1572872 | tf_op jit(solution)/shard_map/ppermute | solution.py:25
  328.6 33.0 %collective-permute-start.22 = (bf16[2,256,512]{2,1,0:T(8,128)(2,1)}, bf16[2,256,512]{2,1,0:T(8,128)(2,1)S(1)}, u32[]{:S(2)}, u32[]{:S(2)}) collective-permute-start(bf16[2,256,512]{2,1,0:T(8,128)(2,1)} %get-tuple-element.180), channel_id=1, source_target_pairs={{0,16},{16,0},{1,17},{17,1},{2,18},{18,2},{3,19},{19,3},{4,20},{20... | collective-permute-start | bytes 1572872 | tf_op jit(solution)/shard_map/ppermute | solution.py:25
  330.1 29.2 %collective-permute-start.25 = (f32[1,896]{1,0:T(1,128)S(1)}, f32[1,896]{1,0:T(1,128)S(1)}, u32[]{:S(2)}, u32[]{:S(2)}) collective-permute-start(f32[1,896]{1,0:T(1,128)S(1)} %copy-done.53), channel_id=1, source_target_pairs={{0,8},{8,0},{1,9},{9,1},{2,10},{10,2},{3,11},{11,3},{4,12},{12,4},... | collective-permute-start | bytes 10760 | tf_op jit(solution)/shard_map/ppermute | solution.py:25
  363.6 53.1 %collective-permute-start.30 = (bf16[2,2,1024,512]{3,2,1,0:T(8,128)(2,1)}, bf16[2,2,1024,512]{3,2,1,0:T(8,128)(2,1)}, u32[]{:S(2)}, u32[]{:S(2)}) collective-permute-start(bf16[2,2,1024,512]{3,2,1,0:T(8,128)(2,1)} %get-tuple-element.197), channel_id=1, source_target_pairs={{0,1},{1,0},{2,3},{3,2},{4,5},{5,4},{6,7},{7,6},{8,9},{9,8},{10,11... | collective-permute-start | bytes 12582920 | tf_op jit(solution)/shard_map/ppermute | solution.py:25
  368.1 41.9 %collective-permute-start.29 = (bf16[2,512,512]{2,1,0:T(8,128)(2,1)}, bf16[2,512,512]{2,1,0:T(8,128)(2,1)S(1)}, u32[]{:S(2)}, u32[]{:S(2)}) collective-permute-start(bf16[2,512,512]{2,1,0:T(8,128)(2,1)} %get-tuple-element.196), channel_id=1, source_target_pairs={{0,1},{1,0},{2,3},{3,2},{4,5},{5,4},{6,7},{7,6},{8,9},{9,8},{10,11... | collective-permute-start | bytes 3145736 | tf_op jit(solution)/shard_map/ppermute | solution.py:25
  371.4 45.4 %collective-permute-start.26 = (bf16[4,256,512]{2,1,0:T(8,128)(2,1)}, bf16[4,256,512]{2,1,0:T(8,128)(2,1)S(1)}, u32[]{:S(2)}, u32[]{:S(2)}) collective-permute-start(bf16[4,256,512]{2,1,0:T(8,128)(2,1)} %shard_map.222.refs_7_), channel_id=1, source_target_pairs={{0,8},{8,0},{1,9},{9,1},{2,10},{10,2},{3,11},{11,3},{4,12},{12,4},... | collective-permute-start | bytes 3145736 | tf_op jit(solution)/shard_map/ppermute | solution.py:25
  418.3 38.0 %collective-permute-start.31 = (bf16[2,2,1024,512]{3,2,1,0:T(8,128)(2,1)}, bf16[2,2,1024,512]{3,2,1,0:T(8,128)(2,1)}, u32[]{:S(2)}, u32[]{:S(2)}) collective-permute-start(bf16[2,2,1024,512]{3,2,1,0:T(8,128)(2,1)} %get-tuple-element.199), channel_id=1, source_target_pairs={{0,1},{1,0},{2,3},{3,2},{4,5},{5,4},{6,7},{7,6},{8,9},{9,8},{10,11... | collective-permute-start | bytes 12582920 | tf_op jit(solution)/shard_map/ppermute | solution.py:25
  425.3 27.8 %collective-permute-start.33 = (bf16[4,256,512]{2,1,0:T(8,128)(2,1)}, bf16[4,256,512]{2,1,0:T(8,128)(2,1)S(1)}, u32[]{:S(2)}, u32[]{:S(2)}) collective-permute-start(bf16[4,256,512]{2,1,0:T(8,128)(2,1)} %get-tuple-element.205), channel_id=1, source_target_pairs={{0,4},{4,0},{1,5},{5,1},{2,6},{6,2},{3,7},{7,3},{8,12},{12,8},{9,1... | collective-permute-start | bytes 3145736 | tf_op jit(solution)/shard_map/ppermute | solution.py:25
  428.8 26.0 %collective-permute-start.35 = (bf16[4,256,512]{2,1,0:T(8,128)(2,1)}, bf16[4,256,512]{2,1,0:T(8,128)(2,1)S(1)}, u32[]{:S(2)}, u32[]{:S(2)}) collective-permute-start(bf16[4,256,512]{2,1,0:T(8,128)(2,1)} %get-tuple-element.207), channel_id=1, source_target_pairs={{0,2},{2,0},{1,3},{3,1},{4,6},{6,4},{5,7},{7,5},{8,10},{10,8},{9,1... | collective-permute-start | bytes 3145736 | tf_op jit(solution)/shard_map/ppermute | solution.py:25
  431.1 25.2 %collective-permute-start.34 = (bf16[4,256,512]{2,1,0:T(8,128)(2,1)}, bf16[4,256,512]{2,1,0:T(8,128)(2,1)S(1)}, u32[]{:S(2)}, u32[]{:S(2)}) collective-permute-start(bf16[4,256,512]{2,1,0:T(8,128)(2,1)} %get-tuple-element.206.refs_2_), channel_id=1, source_target_pairs={{0,16},{16,0},{1,17},{17,1},{2,18},{18,2},{3,19},{19,3},{4,20},{20... | collective-permute-start | bytes 3145736 | tf_op jit(solution)/shard_map/ppermute | solution.py:25
  437.8 47.9 %collective-permute-start.37 = (bf16[1024,512]{1,0:T(8,128)(2,1)}, bf16[1024,512]{1,0:T(8,128)(2,1)}, u32[]{:S(2)}, u32[]{:S(2)}) collective-permute-start(bf16[1024,512]{1,0:T(8,128)(2,1)} %get-tuple-element.211), channel_id=1, source_target_pairs={{0,4},{4,0},{1,5},{5,1},{2,6},{6,2},{3,7},{7,3},{8,12},{12,8},{9,1... | collective-permute-start | bytes 3145736 | tf_op jit(solution)/shard_map/ppermute | solution.py:25
  518.7 28.3 %collective-permute-start.48 = (bf16[1024,512]{1,0:T(8,128)(2,1)}, bf16[1024,512]{1,0:T(8,128)(2,1)}, u32[]{:S(2)}, u32[]{:S(2)}) collective-permute-start(bf16[1024,512]{1,0:T(8,128)(2,1)} %get-tuple-element.225), channel_id=1, source_target_pairs={{0,4},{4,0},{1,5},{5,1},{2,6},{6,2},{3,7},{7,3},{8,12},{12,8},{9,1... | collective-permute-start | bytes 3145736 | tf_op jit(solution)/shard_map/ppermute | solution.py:25
  520.0 26.9 %collective-permute-start.47 = (bf16[1024,512]{1,0:T(8,128)(2,1)}, bf16[1024,512]{1,0:T(8,128)(2,1)}, u32[]{:S(2)}, u32[]{:S(2)}) collective-permute-start(bf16[1024,512]{1,0:T(8,128)(2,1)} %get-tuple-element.224.refs_6_), channel_id=1, source_target_pairs={{0,2},{2,0},{1,3},{3,1},{4,6},{6,4},{5,7},{7,5},{8,10},{10,8},{9,1... | collective-permute-start | bytes 3145736 | tf_op jit(solution)/shard_map/ppermute | solution.py:25
  (87 other events, 720.5 us)
Sparse Core Ops, SparseCore 0:
  9.6 70.2 all-gather.4
  81.5 75.9 all-gather.6
